TPU v7x, 32 devices: a whole 2x2x4 slice. The times are simulated.
32 devices in a mesh: seq: 8 (over y, x, core), tp: 2 (over z_hi), img: 2 (over z_lo).
Axes of the slice: x: 2, y: 2, z: 4 (z_hi: 2, z_lo: 2; z = z_hi * 2 + z_lo), core: 2. Of those that a mesh axis runs over, the one named last changes fastest.
Arguments:
- text: bfloat16 [2, 1024, 2048], P('img', 'seq'), may hold values from -6 to 6
- segment: int32 [2, 1024], P('img'), may hold values from 0 to 2, as said below
- features: bfloat16 [2, 16, 256, 1024], P('img', 'seq'), may hold values from -6 to 6
- image_count: int32 [2, 8], P('img'), may hold values from 1 to 2, as said below
- image_slot: int32 [2, 16], P('img'), may hold values from 0 to 15, as said below
- cotangent: bfloat16 [2, 1024, 2048], P('img', 'seq'), may hold values from -6 to 6
- input_gain: bfloat16 [2048], replicated, may hold values from 0.5 to 1.5
- input_shift: bfloat16 [2048], replicated, may hold values from -1.796875 to 1.796875
- query_weight: bfloat16 [2048, 2048], P(('seq', 'img'), 'tp'), may hold values from -0.125 to 0.125
- key_weight: bfloat16 [2048, 2048], P(('seq', 'img'), 'tp'), may hold values from -0.125 to 0.125
- value_weight: bfloat16 [2048, 2048], P(('seq', 'img'), 'tp'), may hold values from -0.125 to 0.125
- inner_gain: bfloat16 [2048], P('tp'), may hold values from 0.5 to 1.5
- inner_shift: bfloat16 [2048], P('tp'), may hold values from -1.796875 to 1.796875
- out_weight: bfloat16 [2048, 2048], P('tp', ('seq', 'img')), may hold values from -0.125 to 0.125
- middle_gain: bfloat16 [2048], replicated, may hold values from 0.5 to 1.5
- middle_shift: bfloat16 [2048], replicated, may hold values from -1.796875 to 1.796875
- up_weight: bfloat16 [2048, 8192], P(('seq', 'img'), 'tp'), may hold values from -0.125 to 0.125
- up_bias: bfloat16 [8192], P('tp'), may hold values from -1.796875 to 1.796875
- hidden_gain: bfloat16 [8192], P('tp'), may hold values from 0.5 to 1.5
- hidden_shift: bfloat16 [8192], P('tp'), may hold values from -1.796875 to 1.796875
- down_weight: bfloat16 [8192, 2048], P('tp', ('seq', 'img')), may hold values from -0.0625 to 0.0625
- latents: bfloat16 [64, 2048], P(None, ('seq', 'img')), may hold values from -6 to 6
- resample_query: bfloat16 [2048, 2048], P(('seq', 'img'), 'tp'), may hold values from -0.125 to 0.125
- resample_key: bfloat16 [1024, 2048], P(('seq', 'img'), 'tp'), may hold values from -0.1875 to 0.1875
- resample_value: bfloat16 [1024, 2048], P(('seq', 'img'), 'tp'), may hold values from -0.1875 to 0.1875
- resample_out: bfloat16 [2048, 2048], P('tp', ('seq', 'img')), may hold values from -1 to 1
Outputs:
- result: bfloat16 [2, 1024, 2048], P('img', 'seq')
- text_grad: float32 [2, 1024, 2048], P('img', 'seq')
- input_gain_grad: float32 [2048], replicated
- input_shift_grad: float32 [2048], replicated
- query_grad: float32 [2048, 2048], P(('seq', 'img'), 'tp')
- key_grad: float32 [2048, 2048], P(('seq', 'img'), 'tp')
- value_grad: float32 [2048, 2048], P(('seq', 'img'), 'tp')
- inner_gain_grad: float32 [2048], P('tp')
- inner_shift_grad: float32 [2048], P('tp')
- out_grad: float32 [2048, 2048], P('tp', ('seq', 'img'))
- middle_gain_grad: float32 [2048], replicated
- middle_shift_grad: float32 [2048], replicated
- up_grad: float32 [2048, 8192], P(('seq', 'img'), 'tp')
- up_bias_grad: float32 [8192], P('tp')
- hidden_gain_grad: float32 [8192], P('tp')
- hidden_shift_grad: float32 [8192], P('tp')
- down_grad: float32 [8192, 2048], P('tp', ('seq', 'img'))
- latents_grad: float32 [64, 2048], P(None, ('seq', 'img'))
- resample_query_grad: float32 [2048, 2048], P(('seq', 'img'), 'tp')
- resample_key_grad: float32 [1024, 2048], P(('seq', 'img'), 'tp')
- resample_value_grad: float32 [1024, 2048], P(('seq', 'img'), 'tp')
- resample_out_grad: float32 [2048, 2048], P('tp', ('seq', 'img'))
Inputs may be any that keep to these rules, and one draw needn't show every extreme that they name: `segment`: token block b (rows 64 b to 64 b + 63) of a group belongs to sequence b mod 1; sequence s holds the documents 3 s, 3 s + 1 and 3 s + 2 in the order of its rows, each one or more rows, and the middle one has rows on every index of seq. `image_count`: some index of seq in each group holds 2 live slots and some holds one. `image_slot`: values are distinct within a group; only the live slots fill their block.
All inputs are finite; a program needn't handle non-finite values.
Results may differ from a plain program's by a relative error of at most 0.025.
Values may be sent and summed in bfloat16 or wider, within the bound.
A program may use at most 256 MiB of HBM per device.

v0:
```python
import functools

import jax
import jax.numpy as jnp
from jax import lax
from jax.sharding import PartitionSpec as P

HEAD = 64
FF = 8192
PATCH = 256
LAT = 64
SEQ_MAX = 2048
IMG_DEV = 2


EPSILON = 1e-05
HIGHEST_PRECISION = lax.Precision.HIGHEST


def shortened(x):

    def short(part):
        return part.astype(jnp.bfloat16) if part.dtype == jnp.float32 else part

    return jax.tree.map(short, x)


def xpos_factors(position, half_size):
    ladder = jnp.arange(half_size, dtype=jnp.float32)
    frequency = jnp.exp(ladder * (-2.0 * jnp.log(10000.0) / (2.0 * half_size)))
    decay_base = (ladder / half_size + 0.4) / 1.4
    angles = position[:, None] * frequency[None, :]
    growth = jnp.exp(position[:, None] / 512.0 * jnp.log(decay_base)[None, :])
    return (jnp.cos(angles)[:, None, :], jnp.sin(angles)[:, None, :], growth[:, None, :])


def rotate(inputs, cosine, sine_table, factor):
    half_size = inputs.shape[-1] // 2
    first_half = inputs[..., :half_size]
    second_half = inputs[..., half_size:]
    turned = jnp.concatenate(
        [
            first_half * cosine - second_half * sine_table,
            first_half * sine_table + second_half * cosine,
        ],
        -1,
    )
    return turned * jnp.concatenate([factor, factor], -1)


def rotate_back(gradient, cosine, sine_table, factor):
    half_size = gradient.shape[-1] // 2
    scaled = gradient * jnp.concatenate([factor, factor], -1)
    first_half = scaled[..., :half_size]
    second_half = scaled[..., half_size:]
    return jnp.concatenate(
        [
            first_half * cosine + second_half * sine_table,
            second_half * cosine - first_half * sine_table,
        ],
        -1,
    )


def tp_total(inputs):
    return jax.tree.map(lambda part: part.astype(jnp.float32), lax.psum(shortened(inputs), "tp"))


def full_norm(inputs, norm_gain, norm_shift):
    center = inputs - jnp.mean(inputs, -1, keepdims=True)
    spread = jnp.mean(center * center, -1, keepdims=True)
    factor = lax.rsqrt(spread + EPSILON)
    normal = center * factor
    return (normal * norm_gain + norm_shift, normal, factor)


def full_back(gradient, normal, factor, norm_gain):
    scaled = gradient * norm_gain
    return factor * (
        scaled
        - jnp.mean(scaled, -1, keepdims=True)
        - normal * jnp.mean(scaled * normal, -1, keepdims=True)
    )


def split_norm(inputs, norm_gain, norm_shift, full_width):
    totals = tp_total(
        (jnp.sum(inputs, -1, keepdims=True), jnp.sum(inputs * inputs, -1, keepdims=True))
    )
    average = totals[0] / full_width
    spread = totals[1] / full_width - average * average
    factor = lax.rsqrt(spread + EPSILON)
    normal = (inputs - average) * factor
    return (normal * norm_gain + norm_shift, normal, factor)


def split_back(gradient, normal, factor, norm_gain, full_width):
    scaled = gradient * norm_gain
    totals = tp_total(
        (jnp.sum(scaled, -1, keepdims=True), jnp.sum(scaled * normal, -1, keepdims=True))
    )
    return factor * (scaled - totals[0] / full_width - normal * (totals[1] / full_width))


def attend_piece(
    running, query_rot, key_piece, value_piece, row_index, row_segment, segment_all, score_scale
):
    heads_local = query_rot.shape[1]
    amount = key_piece.shape[0]
    block_size = 1024

    def step(state_in, number):
        first_row = number * block_size
        key_block = lax.dynamic_slice_in_dim(key_piece, first_row, block_size, 0).reshape(
            block_size, heads_local, -1
        )
        value_block = lax.dynamic_slice_in_dim(value_piece, first_row, block_size, 0).reshape(
            block_size, heads_local, -1
        )
        key_index = first_row + jnp.arange(block_size, dtype=jnp.int32)
        key_segment = lax.dynamic_slice_in_dim(segment_all, first_row, block_size, 0)
        scores = (
            jnp.einsum("qhd,khd->hqk", query_rot, key_block, preferred_element_type=jnp.float32)
            * score_scale
        )
        allowed = (key_index[None, :] <= row_index[:, None]) & (
            key_segment[None, :] == row_segment[:, None]
        )
        scores = jnp.where(allowed[None], scores, -1e30)
        best_old, total_old, accum_old = state_in
        best_new = jnp.maximum(best_old, jnp.max(scores, -1))
        weights = jnp.where(allowed[None], jnp.exp(scores - best_new[..., None]), 0.0)
        shrink = jnp.exp(best_old - best_new)
        total_new = total_old * shrink + jnp.sum(weights, -1)
        added = jnp.einsum(
            "hqk,khd->qhd",
            weights.astype(jnp.bfloat16),
            value_block,
            preferred_element_type=jnp.float32,
        )
        accum_new = accum_old * shrink.T[:, :, None] + added
        return ((best_new, total_new, accum_new), None)

    return lax.scan(step, running, jnp.arange(amount // block_size, dtype=jnp.int32))[0]


def attend_back(
    query_rot,
    key_all,
    value_all,
    grad_attended,
    log_total,
    delta,
    row_index,
    row_segment,
    segment_all,
    score_scale,
):
    heads_local = query_rot.shape[1]
    amount = key_all.shape[0]
    block_size = 1024

    def step(dquery, number):
        first_row = number * block_size
        key_block = lax.dynamic_slice_in_dim(key_all, first_row, block_size, 0).reshape(
            block_size, heads_local, -1
        )
        value_block = lax.dynamic_slice_in_dim(value_all, first_row, block_size, 0).reshape(
            block_size, heads_local, -1
        )
        key_index = first_row + jnp.arange(block_size, dtype=jnp.int32)
        key_segment = lax.dynamic_slice_in_dim(segment_all, first_row, block_size, 0)
        scores = (
            jnp.einsum("qhd,khd->hqk", query_rot, key_block, preferred_element_type=jnp.float32)
            * score_scale
        )
        allowed = (key_index[None, :] <= row_index[:, None]) & (
            key_segment[None, :] == row_segment[:, None]
        )
        weights = jnp.where(
            allowed[None],
            jnp.exp(jnp.where(allowed[None], scores, -1e30) - log_total[..., None]),
            0.0,
        )
        dweights = jnp.einsum(
            "qhd,khd->hqk", grad_attended, value_block, preferred_element_type=jnp.float32
        )
        dscores = (weights * (dweights - delta[..., None])).astype(jnp.bfloat16)
        dquery = (
            dquery
            + jnp.einsum("hqk,khd->qhd", dscores, key_block, preferred_element_type=jnp.float32)
            * score_scale
        )
        dkeys = (
            jnp.einsum("hqk,qhd->khd", dscores, query_rot, preferred_element_type=jnp.float32)
            * score_scale
        )
        dvalues = jnp.einsum(
            "hqk,qhd->khd",
            weights.astype(jnp.bfloat16),
            grad_attended,
            preferred_element_type=jnp.float32,
        )
        return (dquery, (dkeys, dvalues))

    start_grad = jnp.zeros(query_rot.shape, jnp.float32)
    dquery, outputs = lax.scan(step, start_grad, jnp.arange(amount // block_size, dtype=jnp.int32))
    return (dquery, outputs[0].reshape(amount, -1), outputs[1].reshape(amount, -1))


def on_device(
    text,
    segment,
    features,
    image_count,
    image_slot,
    cotangent,
    input_gain,
    input_shift,
    query_weight,
    key_weight,
    value_weight,
    inner_gain,
    inner_shift,
    out_weight,
    middle_gain,
    middle_shift,
    up_weight,
    up_bias,
    hidden_gain,
    hidden_shift,
    down_weight,
    latents,
    resample_query,
    resample_key,
    resample_value,
    resample_out,
):
    row_count = text.shape[1]
    model_width = text.shape[2]
    group_rows = segment.shape[1]
    seq_rank = lax.axis_index("seq")
    gathered_in = (
        lax.all_gather(query_weight, ("seq", "img"), axis=0, tiled=True),
        lax.all_gather(key_weight, ("seq", "img"), axis=0, tiled=True),
        lax.all_gather(value_weight, ("seq", "img"), axis=0, tiled=True),
        lax.all_gather(up_weight, ("seq", "img"), axis=0, tiled=True),
        lax.all_gather(resample_query, ("seq", "img"), axis=0, tiled=True),
        lax.all_gather(resample_key, ("seq", "img"), axis=0, tiled=True),
        lax.all_gather(resample_value, ("seq", "img"), axis=0, tiled=True),
    )
    query_full, key_full, value_full, up_full, probe_full, image_key_full, image_value_full = (
        gathered_in
    )
    gathered_out = (
        lax.all_gather(out_weight, ("seq", "img"), axis=1, tiled=True),
        lax.all_gather(down_weight, ("seq", "img"), axis=1, tiled=True),
        lax.all_gather(resample_out, ("seq", "img"), axis=1, tiled=True),
        lax.all_gather(latents, ("seq", "img"), axis=1, tiled=True),
    )
    out_full, down_full, image_out_full, latent_full = gathered_out
    half_width = query_full.shape[1]
    heads_local = half_width // HEAD
    score_scale = HEAD ** (-0.5)
    gelu_exact = functools.partial(jax.nn.gelu, approximate=False)
    image_slots = features.shape[1]
    pictures = features[0].reshape(image_slots * PATCH, features.shape[3])
    probe = (
        jnp.dot(latent_full, probe_full, preferred_element_type=jnp.float32)
        .astype(jnp.bfloat16)
        .reshape(LAT, heads_local, HEAD)
    )
    image_keys = (
        jnp.dot(pictures, image_key_full, preferred_element_type=jnp.float32)
        .astype(jnp.bfloat16)
        .reshape(image_slots, PATCH, heads_local, HEAD)
    )
    image_values = (
        jnp.dot(pictures, image_value_full, preferred_element_type=jnp.float32)
        .astype(jnp.bfloat16)
        .reshape(image_slots, PATCH, heads_local, HEAD)
    )
    image_scores = (
        jnp.einsum("qhd,iphd->ihqp", probe, image_keys, preferred_element_type=jnp.float32)
        * score_scale
    )
    image_probs = jax.nn.softmax(image_scores, -1)
    image_mixed = jnp.einsum(
        "ihqp,iphd->iqhd",
        image_probs.astype(jnp.bfloat16),
        image_values,
        preferred_element_type=jnp.float32,
    )
    image_mixed = image_mixed.astype(jnp.bfloat16).reshape(image_slots * LAT, half_width)
    embed = tp_total(jnp.dot(image_mixed, image_out_full, preferred_element_type=jnp.float32))
    embed = embed.astype(jnp.bfloat16).reshape(image_slots, LAT, model_width)
    image_total = image_slot.shape[1]
    slot_range = jnp.arange(image_total, dtype=jnp.int32)
    live = slot_range % IMG_DEV < jnp.repeat(image_count[0], IMG_DEV)
    block_local = row_count // LAT
    block_count = group_rows // LAT
    block_ids = seq_rank * block_local + jnp.arange(block_local, dtype=jnp.int32)
    owner = ((image_slot[0][None, :] == block_ids[:, None]) & live[None, :]).astype(jnp.float32)
    owner_low = owner.astype(jnp.bfloat16)
    taken = jnp.sum(owner, 1) > 0.5
    chosen = owner_low
    placed = jnp.einsum(
        "bi,ild->bld",
        chosen,
        lax.all_gather(embed, "seq", axis=0, tiled=True),
        preferred_element_type=jnp.float32,
    )
    text_blocks = text[0].astype(jnp.float32).reshape(block_local, LAT, model_width)
    mixed_in = jnp.where(taken[:, None, None], placed, text_blocks).reshape(row_count, model_width)
    segment_all = segment[0]
    docs_count = 3 * (group_rows // min(SEQ_MAX, group_rows))
    marks = (segment_all[:, None] == jnp.arange(docs_count, dtype=jnp.int32)[None, :]).astype(
        jnp.int32
    )
    earlier_rows = jnp.cumsum(marks, 0) - marks
    position_all = jnp.sum(earlier_rows * marks, 1)
    first_local = seq_rank * row_count
    row_index = first_local + jnp.arange(row_count, dtype=jnp.int32)
    row_segment = lax.dynamic_slice_in_dim(segment_all, first_local, row_count, 0)
    position = lax.dynamic_slice_in_dim(position_all, first_local, row_count, 0).astype(jnp.float32)
    cosine, sine_table, growth = xpos_factors(position, HEAD // 2)
    input_out, input_hat, input_factor = full_norm(
        mixed_in, input_gain.astype(jnp.float32), input_shift.astype(jnp.float32)
    )
    normed = input_out.astype(jnp.bfloat16)
    query_lin = jnp.dot(normed, query_full, preferred_element_type=jnp.float32).reshape(
        row_count, heads_local, HEAD
    )
    key_lin = jnp.dot(normed, key_full, preferred_element_type=jnp.float32).reshape(
        row_count, heads_local, HEAD
    )
    value_lin = jnp.dot(normed, value_full, preferred_element_type=jnp.float32)
    query_rot = rotate(query_lin, cosine, sine_table, growth).astype(jnp.bfloat16)
    keys_rot = (
        rotate(key_lin, cosine, sine_table, 1.0 / growth)
        .astype(jnp.bfloat16)
        .reshape(row_count, half_width)
    )
    values_low = value_lin.astype(jnp.bfloat16)
    start_state = (
        jnp.full((heads_local, row_count), -1e30, jnp.float32),
        jnp.zeros((heads_local, row_count), jnp.float32),
        jnp.zeros((row_count, heads_local, HEAD), jnp.float32),
    )
    best, weight_total, accum = attend_piece(
        start_state,
        query_rot,
        lax.all_gather(keys_rot, "seq", axis=0, tiled=True),
        lax.all_gather(values_low, "seq", axis=0, tiled=True),
        row_index,
        row_segment,
        segment_all,
        score_scale,
    )
    attended = accum / weight_total.T[:, :, None]
    log_total = best + jnp.log(weight_total)
    inner_out, inner_hat, inner_factor = split_norm(
        attended.reshape(row_count, half_width),
        inner_gain.astype(jnp.float32),
        inner_shift.astype(jnp.float32),
        model_width,
    )
    inner_low = inner_out.astype(jnp.bfloat16)
    middle = mixed_in + tp_total(jnp.dot(inner_low, out_full, preferred_element_type=jnp.float32))
    lifted_out, lifted_hat, lifted_factor = full_norm(
        middle, middle_gain.astype(jnp.float32), middle_shift.astype(jnp.float32)
    )
    lifted = lifted_out.astype(jnp.bfloat16)
    hidden_pre = jnp.dot(lifted, up_full, preferred_element_type=jnp.float32) + up_bias.astype(
        jnp.float32
    )
    activated, gelu_pull = jax.vjp(gelu_exact, hidden_pre)
    settled_out, settled_hat, settled_factor = split_norm(
        activated, hidden_gain.astype(jnp.float32), hidden_shift.astype(jnp.float32), FF
    )
    settled = settled_out.astype(jnp.bfloat16)
    final_rows = middle + tp_total(jnp.dot(settled, down_full, preferred_element_type=jnp.float32))
    result = final_rows.astype(jnp.bfloat16).reshape(1, row_count, model_width)
    grad_low = cotangent[0]
    grad_rows = grad_low.astype(jnp.float32)
    down_grad = jnp.dot(settled.T, grad_low, preferred_element_type=jnp.float32)
    d_settled = jnp.dot(grad_low, down_full.T, preferred_element_type=jnp.float32)
    hidden_gain_grad = jnp.sum(d_settled * settled_hat, 0)
    hidden_shift_grad = jnp.sum(d_settled, 0)
    d_activated = split_back(
        d_settled, settled_hat, settled_factor, hidden_gain.astype(jnp.float32), FF
    )
    d_hidden = gelu_pull(d_activated)[0].astype(jnp.bfloat16)
    up_bias_grad = jnp.sum(d_hidden.astype(jnp.float32), 0)
    up_grad = jnp.dot(lifted.T, d_hidden, preferred_element_type=jnp.float32)
    d_lifted = tp_total(jnp.dot(d_hidden, up_full.T, preferred_element_type=jnp.float32))
    middle_gain_grad = jnp.sum(d_lifted * lifted_hat, 0)
    middle_shift_grad = jnp.sum(d_lifted, 0)
    d_middle = grad_rows + full_back(
        d_lifted, lifted_hat, lifted_factor, middle_gain.astype(jnp.float32)
    )
    d_branch = d_middle.astype(jnp.bfloat16)
    out_grad = jnp.dot(inner_low.T, d_branch, preferred_element_type=jnp.float32)
    d_inner = jnp.dot(d_branch, out_full.T, preferred_element_type=jnp.float32)
    inner_gain_grad = jnp.sum(d_inner * inner_hat, 0)
    inner_shift_grad = jnp.sum(d_inner, 0)
    d_attended = split_back(
        d_inner, inner_hat, inner_factor, inner_gain.astype(jnp.float32), model_width
    )
    d_attended = d_attended.astype(jnp.bfloat16).reshape(row_count, heads_local, HEAD)
    delta = jnp.sum(d_attended.astype(jnp.float32) * attended, -1).T
    key_back, value_back = (
        lax.all_gather(keys_rot, "seq", axis=0, tiled=True),
        lax.all_gather(values_low, "seq", axis=0, tiled=True),
    )
    d_query_rot, d_key_term, d_value_term = attend_back(
        query_rot,
        key_back,
        value_back,
        d_attended,
        log_total,
        delta,
        row_index,
        row_segment,
        segment_all,
        score_scale,
    )
    d_key_sum, d_value_sum = (
        lax.psum_scatter(
            d_key_term.astype(jnp.bfloat16), "seq", scatter_dimension=0, tiled=True
        ).astype(jnp.float32),
        lax.psum_scatter(
            d_value_term.astype(jnp.bfloat16), "seq", scatter_dimension=0, tiled=True
        ).astype(jnp.float32),
    )
    d_query_lin = (
        rotate_back(d_query_rot, cosine, sine_table, growth)
        .astype(jnp.bfloat16)
        .reshape(row_count, half_width)
    )
    d_key_lin = (
        rotate_back(
            d_key_sum.reshape(row_count, heads_local, HEAD), cosine, sine_table, 1.0 / growth
        )
        .astype(jnp.bfloat16)
        .reshape(row_count, half_width)
    )
    d_value_lin = d_value_sum.astype(jnp.bfloat16)
    query_grad = jnp.dot(normed.T, d_query_lin, preferred_element_type=jnp.float32)
    key_grad = jnp.dot(normed.T, d_key_lin, preferred_element_type=jnp.float32)
    value_grad = jnp.dot(normed.T, d_value_lin, preferred_element_type=jnp.float32)
    d_normed_part = (
        jnp.dot(d_query_lin, query_full.T, preferred_element_type=jnp.float32)
        + jnp.dot(d_key_lin, key_full.T, preferred_element_type=jnp.float32)
        + jnp.dot(d_value_lin, value_full.T, preferred_element_type=jnp.float32)
    )
    d_normed = tp_total(d_normed_part)
    input_gain_grad = jnp.sum(d_normed * input_hat, 0)
    input_shift_grad = jnp.sum(d_normed, 0)
    d_mixed = d_middle + full_back(
        d_normed, input_hat, input_factor, input_gain.astype(jnp.float32)
    )
    d_blocks = d_mixed.reshape(block_local, LAT, model_width)
    text_grad = jnp.where(taken[:, None, None], 0.0, d_blocks).reshape(1, row_count, model_width)
    my_target = lax.dynamic_slice_in_dim(image_slot[0], seq_rank * image_slots, image_slots, 0)
    my_live = lax.dynamic_slice_in_dim(live, seq_rank * image_slots, image_slots, 0)
    owner_mine = (
        (jnp.arange(block_count, dtype=jnp.int32)[:, None] == my_target[None, :]) & my_live[None, :]
    ).astype(jnp.bfloat16)
    chosen = owner_mine
    d_embed = jnp.einsum(
        "bi,bld->ild",
        chosen,
        lax.all_gather(d_blocks.astype(jnp.bfloat16), "seq", axis=0, tiled=True),
        preferred_element_type=jnp.float32,
    )
    d_embed_low = d_embed.astype(jnp.bfloat16).reshape(image_slots * LAT, model_width)
    resample_out_grad = jnp.dot(image_mixed.T, d_embed_low, preferred_element_type=jnp.float32)
    d_image_mixed = jnp.dot(d_embed_low, image_out_full.T, preferred_element_type=jnp.float32)
    d_image_mixed = d_image_mixed.astype(jnp.bfloat16).reshape(image_slots, LAT, heads_local, HEAD)
    d_image_probs = jnp.einsum(
        "iqhd,iphd->ihqp", d_image_mixed, image_values, preferred_element_type=jnp.float32
    )
    d_image_scores = image_probs * (
        d_image_probs - jnp.sum(image_probs * d_image_probs, -1, keepdims=True)
    )
    d_image_scores = d_image_scores.astype(jnp.bfloat16)
    d_probe = (
        jnp.einsum("ihqp,iphd->qhd", d_image_scores, image_keys, preferred_element_type=jnp.float32)
        * score_scale
    )
    d_image_keys = (
        jnp.einsum("ihqp,qhd->iphd", d_image_scores, probe, preferred_element_type=jnp.float32)
        * score_scale
    ).astype(jnp.bfloat16)
    d_image_values = jnp.einsum(
        "ihqp,iqhd->iphd",
        image_probs.astype(jnp.bfloat16),
        d_image_mixed,
        preferred_element_type=jnp.float32,
    ).astype(jnp.bfloat16)
    resample_key_grad = jnp.dot(
        pictures.T,
        d_image_keys.reshape(image_slots * PATCH, half_width),
        preferred_element_type=jnp.float32,
    )
    resample_value_grad = jnp.dot(
        pictures.T,
        d_image_values.reshape(image_slots * PATCH, half_width),
        preferred_element_type=jnp.float32,
    )
    d_probe_flat = d_probe.reshape(LAT, half_width)
    resample_query_grad = jnp.dot(
        latent_full.astype(jnp.float32).T, d_probe_flat, precision=HIGHEST_PRECISION
    )
    latent_grad = tp_total(
        jnp.dot(d_probe_flat, probe_full.astype(jnp.float32).T, precision=HIGHEST_PRECISION)
    )
    summed_in = (
        lax.psum_scatter(query_grad, ("seq", "img"), scatter_dimension=0, tiled=True),
        lax.psum_scatter(key_grad, ("seq", "img"), scatter_dimension=0, tiled=True),
        lax.psum_scatter(value_grad, ("seq", "img"), scatter_dimension=0, tiled=True),
        lax.psum_scatter(up_grad, ("seq", "img"), scatter_dimension=0, tiled=True),
        lax.psum_scatter(resample_query_grad, ("seq", "img"), scatter_dimension=0, tiled=True),
        lax.psum_scatter(resample_key_grad, ("seq", "img"), scatter_dimension=0, tiled=True),
        lax.psum_scatter(resample_value_grad, ("seq", "img"), scatter_dimension=0, tiled=True),
    )
    summed_out = (
        lax.psum_scatter(out_grad, ("seq", "img"), scatter_dimension=1, tiled=True),
        lax.psum_scatter(down_grad, ("seq", "img"), scatter_dimension=1, tiled=True),
        lax.psum_scatter(resample_out_grad, ("seq", "img"), scatter_dimension=1, tiled=True),
        lax.psum_scatter(latent_grad, ("seq", "img"), scatter_dimension=1, tiled=True),
    )
    summed_small = lax.psum(
        (
            input_gain_grad,
            input_shift_grad,
            inner_gain_grad,
            inner_shift_grad,
            middle_gain_grad,
            middle_shift_grad,
            up_bias_grad,
            hidden_gain_grad,
            hidden_shift_grad,
        ),
        ("seq", "img"),
    )
    return (
        result,
        text_grad,
        summed_small[0],
        summed_small[1],
        summed_in[0],
        summed_in[1],
        summed_in[2],
        summed_small[2],
        summed_small[3],
        summed_out[0],
        summed_small[4],
        summed_small[5],
        summed_in[3],
        summed_small[6],
        summed_small[7],
        summed_small[8],
        summed_out[1],
        summed_out[3],
        summed_in[4],
        summed_in[5],
        summed_in[6],
        summed_out[2],
    )


def solution(mesh):
    placed = (
        P("img", "seq", None),
        P("img", None),
        P("img", "seq", None, None),
        P("img", None),
        P("img", None),
        P("img", "seq", None),
        P(),
        P(),
        P(("seq", "img"), "tp"),
        P(("seq", "img"), "tp"),
        P(("seq", "img"), "tp"),
        P("tp"),
        P("tp"),
        P("tp", ("seq", "img")),
        P(),
        P(),
        P(("seq", "img"), "tp"),
        P("tp"),
        P("tp"),
        P("tp"),
        P("tp", ("seq", "img")),
        P(None, ("seq", "img")),
        P(("seq", "img"), "tp"),
        P(("seq", "img"), "tp"),
        P(("seq", "img"), "tp"),
        P("tp", ("seq", "img")),
    )
    return jax.shard_map(
        on_device,
        mesh=mesh,
        in_specs=placed,
        out_specs=(
            P("img", "seq", None),
            P("img", "seq", None),
            P(),
            P(),
            P(("seq", "img"), "tp"),
            P(("seq", "img"), "tp"),
            P(("seq", "img"), "tp"),
            P("tp"),
            P("tp"),
            P("tp", ("seq", "img")),
            P(),
            P(),
            P(("seq", "img"), "tp"),
            P("tp"),
            P("tp"),
            P("tp"),
            P("tp", ("seq", "img")),
            P(None, ("seq", "img")),
            P(("seq", "img"), "tp"),
            P(("seq", "img"), "tp"),
            P(("seq", "img"), "tp"),
            P("tp", ("seq", "img")),
        ),
        check_vma=False,
    )
```

profile of v0, /device:TPU:0, one launch (start us, length us, event | category | flops | bytes accessed | tf_op | source)
XLA Modules:
  0.0 3979.9 jit_solution(12504719159859527210)
XLA Ops:
  10.0 32.5 all_gather.49
  61.3 42.6 %all-gather.17.cloned.1.call-done = bf16[1024,1024]{1,0:T(8,128)(2,1)} async-done(((bf16[64,1024]{1,0:T(8,128)(2,1)}), bf16[1024,1024]{1,0:T(8,128)(2,1)}) %all-gather.17.cloned.1.call-update) | async-done | bytes 2097168 | tf_op jit(solution)/shard_map/all_gather | solution.py:249
  113.2 40.3 %all-gather.19.cloned.1.call-done = bf16[2048,1024]{1,0:T(8,128)(2,1)} async-done(((bf16[128,1024]{1,0:T(8,128)(2,1)}), bf16[2048,1024]{1,0:T(8,128)(2,1)}) %all-gather.19.cloned.1.call-update) | async-done | bytes 4194320 | tf_op jit(solution)/shard_map/all_gather | solution.py:248
  166.2 39.1 all-gather.21.cloned.1.call-done
  209.1 41.7 %all-reduce.13.cloned.1.call-done = bf16[2,64,2048]{2,1,0:T(8,128)(2,1)} async-done(((bf16[2,64,2048]{2,1,0:T(8,128)(2,1)}), bf16[2,64,2048]{2,1,0:T(8,128)(2,1)}) %all-reduce.13.cloned.1.call-update) | async-done | bytes 524304 | tf_op jit(solution)/shard_map/psum | solution.py:66
  254.1 34.4 all-gather.23.cloned.1.call-done
  296.9 40.2 %all-gather.31.cloned.1.call-done = bf16[2048,1024]{1,0:T(8,128)(2,1)} async-done(((bf16[128,1024]{1,0:T(8,128)(2,1)}), bf16[2048,1024]{1,0:T(8,128)(2,1)}) %all-gather.31.cloned.1.call-update) | async-done | bytes 4194320 | tf_op jit(solution)/shard_map/all_gather | solution.py:246
  342.7 44.8 %all-gather.25.cloned.1.call-done = bf16[2048,1024]{1,0:T(8,128)(2,1)} async-done(((bf16[128,1024]{1,0:T(8,128)(2,1)}), bf16[2048,1024]{1,0:T(8,128)(2,1)}) %all-gather.25.cloned.1.call-update) | async-done | bytes 4194320 | tf_op jit(solution)/shard_map/all_gather | solution.py:244
  394.0 43.8 %all-gather.27.cloned.1.call-done = bf16[2048,1024]{1,0:T(8,128)(2,1)} async-done(((bf16[128,1024]{1,0:T(8,128)(2,1)}), bf16[2048,1024]{1,0:T(8,128)(2,1)}) %all-gather.27.cloned.1.call-update) | async-done | bytes 4194320 | tf_op jit(solution)/shard_map/all_gather | solution.py:245
  473.7 26.9 all-gather.29.cloned.1.call-done
  517.3 33.5 all-gather.35.cloned.1.call-done
  557.8 38.7 all-reduce.15.cloned.1.call-done
  599.1 91.4 %all-gather.37.cloned.1.call-done = bf16[2048,4096]{1,0:T(8,128)(2,1)} async-done(((bf16[128,4096]{1,0:T(8,128)(2,1)}), bf16[2048,4096]{1,0:T(8,128)(2,1)}) %all-gather.37.cloned.1.call-update) | async-done | bytes 16777232 | tf_op jit(solution)/shard_map/all_gather | solution.py:247
  711.5 74.8 %all-gather.39.cloned.1.call-done = bf16[4096,2048]{1,0:T(8,128)(2,1)} async-done(((bf16[4096,128]{1,0:T(8,128)(2,1)}), bf16[4096,2048]{1,0:T(8,128)(2,1)}) %all-gather.39.cloned.1.call-update) | async-done | bytes 16777232 | tf_op jit(solution)/shard_map/all_gather | solution.py:257
  827.4 41.4 %all-reduce.17.cloned.1.call-done = bf16[128,2048]{1,0:T(8,128)(2,1)} async-done(((bf16[128,2048]{1,0:T(8,128)(2,1)}), bf16[128,2048]{1,0:T(8,128)(2,1)}) %all-reduce.17.cloned.1.call-update) | async-done | bytes 524304 | tf_op jit(solution)/shard_map/psum | solution.py:66
  920.3 23.1 reduce-scatter.40.cloned.1.call-done
  954.0 33.9 reduce-scatter.42.cloned.1.call-done
  992.9 41.2 %all-reduce.19.cloned.1.call-done = bf16[128,2048]{1,0:T(8,128)(2,1)} async-done(((bf16[128,2048]{1,0:T(8,128)(2,1)}), bf16[128,2048]{1,0:T(8,128)(2,1)}) %all-reduce.19.cloned.1.call-update) | async-done | bytes 524304 | tf_op jit(solution)/shard_map/psum | solution.py:66
  1049.7 25.5 all-gather.41.cloned.1.call-done
  1102.1 46.7 %all-reduce.23.cloned.1.call-done = (bf16[128,2048]{1,0:T(8,128)(2,1)}, bf16[64,2048]{1,0:T(8,128)(2,1)}) async-done(((bf16[128,2048]{1,0:T(8,128)(2,1)}, bf16[64,2048]{1,0:T(8,128)(2,1)}), (bf16[128,2048]{1,0:T(8,128)(2,1)}, bf16[64,2048]{1,0:T(8,128)(2,1)})) %all-reduce.23.cloned.1.call-update) | async-done | bytes 786448 | tf_op jit(solution)/shard_map/psum | solution.py:66
  1236.4 91.6 %reduce-scatter.36.cloned.1.call-done = f32[128,1024]{0,1:T(8,128)} async-done(((f32[2048,1024]{0,1:T(8,128)}), f32[128,1024]{0,1:T(8,128)}) %reduce-scatter.36.cloned.1.call-update) | async-done | bytes 524304 | tf_op jit(solution)/shard_map/reduce_scatter | solution.py:524
  1330.1 106.3 %all-reduce.21.cloned.1.call-done = (f32[2048]{0:T(1024)}, f32[2048]{0:T(1024)}, f32[1024]{0:T(1024)}, f32[1024]{0:T(1024)}, f32[2048]{0:T(1024)}, /*index=5*/f3...) async-done(((f32[2048]{0:T(1024)}, f32[2048]{0:T(1024)}, f32[1024]{0:T(1024)}, f32[1024]{0:T(1024)}, f32[2048]{0:T(1024)}, /*index=5*/f32[2048]{0:T(1024)}, ...) | async-done | bytes 90128 | tf_op jit(solution)/shard_map/psum | solution.py:534
  1436.3 59.0 %reduce-scatter.34.cloned.1.call-done = f32[64,128]{1,0:T(8,128)} async-done(((f32[64,2048]{1,0:T(8,128)}), f32[64,128]{1,0:T(8,128)}) %reduce-scatter.34.cloned.1.call-update) | async-done | bytes 32784 | tf_op jit(solution)/shard_map/reduce_scatter | solution.py:532
  1495.4 178.8 %reduce-scatter.28.cloned.1.call-done = f32[1024,128]{1,0:T(8,128)} async-done(((f32[1024,2048]{1,0:T(8,128)}), f32[1024,128]{1,0:T(8,128)}) %reduce-scatter.28.cloned.1.call-update) | async-done | bytes 524304 | tf_op jit(solution)/shard_map/reduce_scatter | solution.py:529
  1674.2 96.7 %reduce-scatter.44.cloned.1.call-done = f32[64,1024]{1,0:T(8,128)} async-done(((f32[1024,1024]{1,0:T(8,128)}), f32[64,1024]{1,0:T(8,128)}) %reduce-scatter.44.cloned.1.call-update) | async-done | bytes 262160
  1770.9 96.0 %reduce-scatter.46.cloned.1.call-done = f32[64,1024]{1,0:T(8,128)} async-done(((f32[1024,1024]{1,0:T(8,128)}), f32[64,1024]{1,0:T(8,128)}) %reduce-scatter.46.cloned.1.call-update) | async-done | bytes 262160
  1867.0 179.9 %reduce-scatter.22.cloned.1.call-done = f32[128,1024]{1,0:T(8,128)} async-done(((f32[2048,1024]{1,0:T(8,128)}), f32[128,1024]{1,0:T(8,128)}) %reduce-scatter.22.cloned.1.call-update) | async-done | bytes 524304 | tf_op jit(solution)/shard_map/reduce_scatter | solution.py:520
  2046.8 180.6 %reduce-scatter.24.cloned.1.call-done = f32[128,1024]{1,0:T(8,128)} async-done(((f32[2048,1024]{1,0:T(8,128)}), f32[128,1024]{1,0:T(8,128)}) %reduce-scatter.24.cloned.1.call-update) | async-done | bytes 524304 | tf_op jit(solution)/shard_map/reduce_scatter | solution.py:521
  2227.4 180.4 %reduce-scatter.26.cloned.1.call-done = f32[128,1024]{1,0:T(8,128)} async-done(((f32[2048,1024]{1,0:T(8,128)}), f32[128,1024]{1,0:T(8,128)}) %reduce-scatter.26.cloned.1.call-update) | async-done | bytes 524304 | tf_op jit(solution)/shard_map/reduce_scatter | solution.py:522
  2407.8 180.6 %reduce-scatter.38.cloned.1.call-done = f32[1024,128]{1,0:T(8,128)} async-done(((f32[1024,2048]{1,0:T(8,128)}), f32[1024,128]{1,0:T(8,128)}) %reduce-scatter.38.cloned.1.call-update) | async-done | bytes 524304 | tf_op jit(solution)/shard_map/reduce_scatter | solution.py:531
  2588.4 686.4 %reduce-scatter.30.cloned.1.call-done = f32[128,4096]{1,0:T(8,128)} async-done(((f32[2048,4096]{1,0:T(8,128)}), f32[128,4096]{1,0:T(8,128)}) %reduce-scatter.30.cloned.1.call-update) | async-done | bytes 2097168 | tf_op jit(solution)/shard_map/reduce_scatter | solution.py:523
  3274.8 686.4 %reduce-scatter.32.cloned.1.call-done = f32[4096,128]{1,0:T(8,128)} async-done(((f32[4096,2048]{1,0:T(8,128)}), f32[4096,128]{1,0:T(8,128)}) %reduce-scatter.32.cloned.1.call-update) | async-done | bytes 2097168 | tf_op jit(solution)/shard_map/reduce_scatter | solution.py:530
  (426 shorter events, 404.5 us)
Async XLA Ops:
  7.9 95.9 %all-gather.17.cloned.1.call-start = ((), (), s32[]{:S(2)}) async-start(), calls=%async_computation.14 | async-start | bytes 2228224 | tf_op jit(solution)/shard_map/all_gather | solution.py:249
  8.7 144.8 %all-gather.19.cloned.1.call-start = ((), (), s32[]{:S(2)}) async-start(), calls=%async_computation.15 | async-start | bytes 4456448 | tf_op jit(solution)/shard_map/all_gather | solution.py:248
  9.4 195.9 %all-gather.21.cloned.1.call-start = ((), (), s32[]{:S(2)}) async-start(), calls=%async_computation.16 | async-start | bytes 4456448 | tf_op jit(solution)/shard_map/all_gather | solution.py:258
  10.0 240.8 %all-reduce.13.cloned.1.call-start = ((), (), s32[]{:S(2)}) async-start(), calls=%async_computation.17 | async-start | bytes 1048576 | tf_op jit(solution)/shard_map/psum | solution.py:66
  209.0 79.5 %all-gather.23.cloned.1.call-start = ((), (), s32[]{:S(2)}) async-start(), calls=%async_computation.18 | async-start | bytes 4718592 | tf_op jit(solution)/shard_map/all_gather | solution.py:310
  250.8 86.3 %all-gather.31.cloned.1.call-start = ((), (), s32[]{:S(2)}) async-start(), calls=%async_computation.22 | async-start | bytes 4456448 | tf_op jit(solution)/shard_map/all_gather | solution.py:246
  251.6 135.9 %all-gather.25.cloned.1.call-start = ((), (), s32[]{:S(2)}) async-start(), calls=%async_computation.19 | async-start | bytes 4456448 | tf_op jit(solution)/shard_map/all_gather | solution.py:244
  252.3 185.4 %all-gather.27.cloned.1.call-start = ((), (), s32[]{:S(2)}) async-start(), calls=%async_computation.20 | async-start | bytes 4456448 | tf_op jit(solution)/shard_map/all_gather | solution.py:245
  253.1 216.7 %all-gather.33.cloned.1.call-start = ((), (), s32[]{:S(2)}) async-start(), calls=%async_computation.23 | async-start | bytes 2359296 | tf_op jit(solution)/shard_map/all_gather | solution.py:354
  340.8 159.8 %all-gather.29.cloned.1.call-start = ((), (), s32[]{:S(2)}) async-start(), calls=%async_computation.21 | async-start | bytes 2359296 | tf_op jit(solution)/shard_map/all_gather | solution.py:353
  450.6 100.2 %all-gather.35.cloned.1.call-start = ((), (), s32[]{:S(2)}) async-start(), calls=%async_computation.24 | async-start | bytes 4456448 | tf_op jit(solution)/shard_map/all_gather | solution.py:256
  451.2 145.3 %all-reduce.15.cloned.1.call-start = ((), (), s32[]{:S(2)}) async-start(), calls=%async_computation.25 | async-start | bytes 1048576 | tf_op jit(solution)/shard_map/psum | solution.py:66
  554.7 135.9 %all-gather.37.cloned.1.call-start = ((), (), s32[]{:S(2)}) async-start(), calls=%async_computation.26 | async-start | bytes 17825792 | tf_op jit(solution)/shard_map/all_gather | solution.py:247
  555.3 231.0 %all-gather.39.cloned.1.call-start = ((), (), s32[]{:S(2)}) async-start(), calls=%async_computation.27 | async-start | bytes 17825792 | tf_op jit(solution)/shard_map/all_gather | solution.py:257
  555.9 312.9 %all-reduce.17.cloned.1.call-start = ((), (), s32[]{:S(2)}) async-start(), calls=%async_computation.28 | async-start | bytes 1048576 | tf_op jit(solution)/shard_map/psum | solution.py:66
  827.0 116.4 %reduce-scatter.40.cloned.1.call-start = ((), (), s32[]{:S(2)}) async-start(), calls=%async_computation.40 | async-start | bytes 2359296
  903.0 84.8 %reduce-scatter.42.cloned.1.call-start = ((), (), s32[]{:S(2)}) async-start(), calls=%async_computation.41 | async-start | bytes 2359296
  914.4 119.8 %all-reduce.19.cloned.1.call-start = ((), (), s32[]{:S(2)}) async-start(), calls=%async_computation.29 | async-start | bytes 1048576 | tf_op jit(solution)/shard_map/psum | solution.py:66
  992.7 82.5 %all-gather.41.cloned.1.call-start = ((), (), s32[]{:S(2)}) async-start(), calls=%async_computation.36 | async-start | bytes 4718592 | tf_op jit(solution)/shard_map/all_gather | solution.py:474
  1039.3 109.5 %all-reduce.23.cloned.1.call-start = ((), (), s32[]{:S(2)}) async-start(), calls=%async_computation.45 | async-start | bytes 1572864 | tf_op jit(solution)/shard_map/psum | solution.py:66
  1095.7 232.4 %reduce-scatter.36.cloned.1.call-start = ((), (), s32[]{:S(2)}) async-start(), calls=%async_computation.38 | async-start | bytes 8912896 | tf_op jit(solution)/shard_map/reduce_scatter | solution.py:524
  1101.3 335.0 %all-reduce.21.cloned.1.call-start = ((), (), s32[]{:S(2)}) async-start(), calls=%async_computation.44 | async-start | bytes 180224 | tf_op jit(solution)/shard_map/psum | solution.py:534
  1102.1 393.3 %reduce-scatter.34.cloned.1.call-start = ((), (), s32[]{:S(2)}) async-start(), calls=%async_computation.37 | async-start | bytes 557056 | tf_op jit(solution)/shard_map/reduce_scatter | solution.py:532
  1150.6 523.5 %reduce-scatter.28.cloned.1.call-start = ((), (), s32[]{:S(2)}) async-start(), calls=%async_computation.33 | async-start | bytes 8912896 | tf_op jit(solution)/shard_map/reduce_scatter | solution.py:529
  1156.5 614.4 %reduce-scatter.44.cloned.1.call-start = ((), (), s32[]{:S(2)}) async-start(), calls=%async_computation.42 | async-start | bytes 4456448
  1168.1 698.8 %reduce-scatter.46.cloned.1.call-start = ((), (), s32[]{:S(2)}) async-start(), calls=%async_computation.43 | async-start | bytes 4456448
  1180.9 865.9 %reduce-scatter.22.cloned.1.call-start = ((), (), s32[]{:S(2)}) async-start(), calls=%async_computation.30 | async-start | bytes 8912896 | tf_op jit(solution)/shard_map/reduce_scatter | solution.py:520
  1186.6 1040.8 %reduce-scatter.24.cloned.1.call-start = ((), (), s32[]{:S(2)}) async-start(), calls=%async_computation.31 | async-start | bytes 8912896 | tf_op jit(solution)/shard_map/reduce_scatter | solution.py:521
  1192.2 1215.6 %reduce-scatter.26.cloned.1.call-start = ((), (), s32[]{:S(2)}) async-start(), calls=%async_computation.32 | async-start | bytes 8912896 | tf_op jit(solution)/shard_map/reduce_scatter | solution.py:522
  1197.9 1390.6 %reduce-scatter.38.cloned.1.call-start = ((), (), s32[]{:S(2)}) async-start(), calls=%async_computation.39 | async-start | bytes 8912896 | tf_op jit(solution)/shard_map/reduce_scatter | solution.py:531
  1203.5 2071.3 %reduce-scatter.30.cloned.1.call-start = ((), (), s32[]{:S(2)}) async-start(), calls=%async_computation.34 | async-start | bytes 35651584 | tf_op jit(solution)/shard_map/reduce_scatter | solution.py:523
  1218.1 2743.0 %reduce-scatter.32.cloned.1.call-start = ((), (), s32[]{:S(2)}) async-start(), calls=%async_computation.35 | async-start | bytes 35651584 | tf_op jit(solution)/shard_map/reduce_scatter | solution.py:530
  (101 other events, 3364.4 us)
Sparse Core Ops, SparseCore 0:
  9.6 47.1 all-gather.14
  58.3 45.5 all-gather.16
  105.4 48.0 all-gather.18
  154.8 50.4 all-gather.20
  209.1 41.6 all-reduce.12
  252.7 35.7 all-gather.22
  290.1 47.0 all-gather.30
  338.8 48.6 all-gather.24
  389.1 48.6 all-gather.26
  440.2 29.4 all-gather.32
  502.0 48.8 all-gather.34
  554.8 41.5 all-reduce.14
  597.9 92.6 all-gather.36
  691.9 94.3 all-gather.38
  827.1 41.6 all-reduce.16
  903.1 40.2 reduce-scatter.39
  946.6 41.2 reduce-scatter.41
  992.8 41.2 all-reduce.18
  1039.5 35.7 all-gather.40
  1095.8 52.9 all-reduce.22
  1151.2 176.7 reduce-scatter.35
  1332.6 103.6 all-reduce.20
  1439.0 56.3 reduce-scatter.33
  1498.3 175.7 reduce-scatter.27
  1677.0 93.8 reduce-scatter.43
  1773.7 93.1 reduce-scatter.45
  1869.9 176.8 reduce-scatter.21
  2049.8 177.5 reduce-scatter.23
  2230.2 177.5 reduce-scatter.25
  2410.8 177.5 reduce-scatter.37
  2591.5 683.2 reduce-scatter.29
  3277.7 683.4 reduce-scatter.31
  (1 shorter events, 28.1 us)
where the time goes:
time: 3990 us; the launch traced here: 3980 us
  waiting for transfers between devices  3570 us (89%)
  matrix products  211 us (5%)
  local copies, waits for them, and re-layouts  83.9 us (2%)
  blocking collectives  58.5 us (1%)
  other arithmetic  40.9 us (1%)
    reduce_scatter x1, waiting for transfers between devices, on_device(): lax.psum_scatter(down_grad, ('seq', 'img'), scatter_dimension=1, tiled=True)  686 us
    reduce_scatter x1, waiting for transfers between devices, on_device(): lax.psum_scatter(up_grad, ('seq', 'img'), scatter_dimension=0, tiled=True)  686 us
    unnamed x37, waiting for transfers between devices  257 us
    psum x5, waiting for transfers between devices, tp_total(): lax.psum(shortened(inputs), 'tp')  210 us
    reduce_scatter x1, waiting for transfers between devices, on_device(): lax.psum_scatter(resample_out_grad, ('seq', 'img'), scatter_dimension=1,...  181 us
    reduce_scatter x1, waiting for transfers between devices, on_device(): lax.psum_scatter(key_grad, ('seq', 'img'), scatter_dimension=0, tiled=True)  181 us
    reduce_scatter x1, waiting for transfers between devices, on_device(): lax.psum_scatter(value_grad, ('seq', 'img'), scatter_dimension=0, tiled=T...  180 us
    reduce_scatter x1, waiting for transfers between devices, on_device(): lax.psum_scatter(query_grad, ('seq', 'img'), scatter_dimension=0, tiled=T...  180 us
  transfers between devices with their start and end apart: 33, of which 33 were waited for; matrix products, arithmetic and copies ran while one was open for 5% of the time, Pallas kernels for 0%

commit v1 on v0

--- a/solution.py
+++ b/solution.py
@@ -3,8 +3,11 @@
 import jax
 import jax.numpy as jnp
 from jax import lax
+from jax.experimental import pallas as pl
+from jax.experimental.pallas import tpu as pltpu
 from jax.sharding import PartitionSpec as P
 
+SEQ, TP, IMG = "seq", "tp", "img"
 HEAD = 64
 FF = 8192
 PATCH = 256
@@ -63,7 +66,7 @@
 
 
 def tp_total(inputs):
-    return jax.tree.map(lambda part: part.astype(jnp.float32), lax.psum(shortened(inputs), "tp"))
+    return jax.tree.map(lambda part: part.astype(jnp.float32), lax.psum(shortened(inputs), TP))
 
 
 def full_norm(inputs, norm_gain, norm_shift):
@@ -239,24 +242,24 @@
     row_count = text.shape[1]
     model_width = text.shape[2]
     group_rows = segment.shape[1]
-    seq_rank = lax.axis_index("seq")
+    seq_rank = lax.axis_index(SEQ)
     gathered_in = (
-        lax.all_gather(query_weight, ("seq", "img"), axis=0, tiled=True),
-        lax.all_gather(key_weight, ("seq", "img"), axis=0, tiled=True),
-        lax.all_gather(value_weight, ("seq", "img"), axis=0, tiled=True),
-        lax.all_gather(up_weight, ("seq", "img"), axis=0, tiled=True),
-        lax.all_gather(resample_query, ("seq", "img"), axis=0, tiled=True),
-        lax.all_gather(resample_key, ("seq", "img"), axis=0, tiled=True),
-        lax.all_gather(resample_value, ("seq", "img"), axis=0, tiled=True),
+        lax.all_gather(query_weight, (SEQ, IMG), axis=0, tiled=True),
+        lax.all_gather(key_weight, (SEQ, IMG), axis=0, tiled=True),
+        lax.all_gather(value_weight, (SEQ, IMG), axis=0, tiled=True),
+        lax.all_gather(up_weight, (SEQ, IMG), axis=0, tiled=True),
+        lax.all_gather(resample_query, (SEQ, IMG), axis=0, tiled=True),
+        lax.all_gather(resample_key, (SEQ, IMG), axis=0, tiled=True),
+        lax.all_gather(resample_value, (SEQ, IMG), axis=0, tiled=True),
     )
     query_full, key_full, value_full, up_full, probe_full, image_key_full, image_value_full = (
         gathered_in
     )
     gathered_out = (
-        lax.all_gather(out_weight, ("seq", "img"), axis=1, tiled=True),
-        lax.all_gather(down_weight, ("seq", "img"), axis=1, tiled=True),
-        lax.all_gather(resample_out, ("seq", "img"), axis=1, tiled=True),
-        lax.all_gather(latents, ("seq", "img"), axis=1, tiled=True),
+        lax.all_gather(out_weight, (SEQ, IMG), axis=1, tiled=True),
+        lax.all_gather(down_weight, (SEQ, IMG), axis=1, tiled=True),
+        lax.all_gather(resample_out, (SEQ, IMG), axis=1, tiled=True),
+        lax.all_gather(latents, (SEQ, IMG), axis=1, tiled=True),
     )
     out_full, down_full, image_out_full, latent_full = gathered_out
     half_width = query_full.shape[1]
@@ -307,7 +310,7 @@
     placed = jnp.einsum(
         "bi,ild->bld",
         chosen,
-        lax.all_gather(embed, "seq", axis=0, tiled=True),
+        lax.all_gather(embed, SEQ, axis=0, tiled=True),
         preferred_element_type=jnp.float32,
     )
     text_blocks = text[0].astype(jnp.float32).reshape(block_local, LAT, model_width)
@@ -350,8 +353,8 @@
     best, weight_total, accum = attend_piece(
         start_state,
         query_rot,
-        lax.all_gather(keys_rot, "seq", axis=0, tiled=True),
-        lax.all_gather(values_low, "seq", axis=0, tiled=True),
+        lax.all_gather(keys_rot, SEQ, axis=0, tiled=True),
+        lax.all_gather(values_low, SEQ, axis=0, tiled=True),
         row_index,
         row_segment,
         segment_all,
@@ -410,8 +413,8 @@
     d_attended = d_attended.astype(jnp.bfloat16).reshape(row_count, heads_local, HEAD)
     delta = jnp.sum(d_attended.astype(jnp.float32) * attended, -1).T
     key_back, value_back = (
-        lax.all_gather(keys_rot, "seq", axis=0, tiled=True),
-        lax.all_gather(values_low, "seq", axis=0, tiled=True),
+        lax.all_gather(keys_rot, SEQ, axis=0, tiled=True),
+        lax.all_gather(values_low, SEQ, axis=0, tiled=True),
     )
     d_query_rot, d_key_term, d_value_term = attend_back(
         query_rot,
@@ -427,10 +430,10 @@
     )
     d_key_sum, d_value_sum = (
         lax.psum_scatter(
-            d_key_term.astype(jnp.bfloat16), "seq", scatter_dimension=0, tiled=True
+            d_key_term.astype(jnp.bfloat16), SEQ, scatter_dimension=0, tiled=True
         ).astype(jnp.float32),
         lax.psum_scatter(
-            d_value_term.astype(jnp.bfloat16), "seq", scatter_dimension=0, tiled=True
+            d_value_term.astype(jnp.bfloat16), SEQ, scatter_dimension=0, tiled=True
         ).astype(jnp.float32),
     )
     d_query_lin = (
@@ -471,7 +474,7 @@
     d_embed = jnp.einsum(
         "bi,bld->ild",
         chosen,
-        lax.all_gather(d_blocks.astype(jnp.bfloat16), "seq", axis=0, tiled=True),
+        lax.all_gather(d_blocks.astype(jnp.bfloat16), SEQ, axis=0, tiled=True),
         preferred_element_type=jnp.float32,
     )
     d_embed_low = d_embed.astype(jnp.bfloat16).reshape(image_slots * LAT, model_width)
@@ -517,19 +520,19 @@
         jnp.dot(d_probe_flat, probe_full.astype(jnp.float32).T, precision=HIGHEST_PRECISION)
     )
     summed_in = (
-        lax.psum_scatter(query_grad, ("seq", "img"), scatter_dimension=0, tiled=True),
-        lax.psum_scatter(key_grad, ("seq", "img"), scatter_dimension=0, tiled=True),
-        lax.psum_scatter(value_grad, ("seq", "img"), scatter_dimension=0, tiled=True),
-        lax.psum_scatter(up_grad, ("seq", "img"), scatter_dimension=0, tiled=True),
-        lax.psum_scatter(resample_query_grad, ("seq", "img"), scatter_dimension=0, tiled=True),
-        lax.psum_scatter(resample_key_grad, ("seq", "img"), scatter_dimension=0, tiled=True),
-        lax.psum_scatter(resample_value_grad, ("seq", "img"), scatter_dimension=0, tiled=True),
+        lax.psum_scatter(query_grad, (SEQ, IMG), scatter_dimension=0, tiled=True),
+        lax.psum_scatter(key_grad, (SEQ, IMG), scatter_dimension=0, tiled=True),
+        lax.psum_scatter(value_grad, (SEQ, IMG), scatter_dimension=0, tiled=True),
+        lax.psum_scatter(up_grad, (SEQ, IMG), scatter_dimension=0, tiled=True),
+        lax.psum_scatter(resample_query_grad, (SEQ, IMG), scatter_dimension=0, tiled=True),
+        lax.psum_scatter(resample_key_grad, (SEQ, IMG), scatter_dimension=0, tiled=True),
+        lax.psum_scatter(resample_value_grad, (SEQ, IMG), scatter_dimension=0, tiled=True),
     )
     summed_out = (
-        lax.psum_scatter(out_grad, ("seq", "img"), scatter_dimension=1, tiled=True),
-        lax.psum_scatter(down_grad, ("seq", "img"), scatter_dimension=1, tiled=True),
-        lax.psum_scatter(resample_out_grad, ("seq", "img"), scatter_dimension=1, tiled=True),
-        lax.psum_scatter(latent_grad, ("seq", "img"), scatter_dimension=1, tiled=True),
+        lax.psum_scatter(out_grad, (SEQ, IMG), scatter_dimension=1, tiled=True),
+        lax.psum_scatter(down_grad, (SEQ, IMG), scatter_dimension=1, tiled=True),
+        lax.psum_scatter(resample_out_grad, (SEQ, IMG), scatter_dimension=1, tiled=True),
+        lax.psum_scatter(latent_grad, (SEQ, IMG), scatter_dimension=1, tiled=True),
     )
     summed_small = lax.psum(
         (
@@ -543,7 +546,7 @@
             hidden_gain_grad,
             hidden_shift_grad,
         ),
-        ("seq", "img"),
+        (SEQ, IMG),
     )
     return (
         result,
@@ -571,62 +574,1341 @@
     )
 
 
+MESH_IDS = pl.DeviceIdType.MESH
+ANYWHERE = pl.BlockSpec(memory_space=pl.ANY)
+ON_CHIP = pl.BlockSpec(memory_space=pltpu.VMEM)
+LANES = 128
+PLANE = 8
+VMEM_BYTES = 60 * 1024 * 1024
+PIECES = 4
+FRONT, BACK, ALL, ROWS, INWARD, OUTWARD = range(6)
+
+
+def narrow_heads(mesh):
+    return mesh.shape[SEQ] != PLANE or mesh.shape[IMG] != 2 or mesh.shape[TP] != 2
+
+
+def flipped(number, bit):
+    step = 2**bit
+    return number + step - 2 * step * ((number // step) % 2)
+
+
+class Places:
+    def __init__(self):
+        self.seq, self.tp, self.img = (lax.axis_index(name) for name in (SEQ, TP, IMG))
+        self.s_core, self.s_x, self.s_y = (flipped(self.seq, bit) for bit in range(3))
+        self.s_xy = flipped(self.s_x, 2)
+        self.core, self.x, self.y = (self.at(seq) for seq in (self.s_core, self.s_x, self.s_y))
+        self.tp_peer = (self.seq, 1 - self.tp, self.img)
+        self.img_peer = (self.seq, self.tp, 1 - self.img)
+
+    def at(self, seq):
+        return (seq, self.tp, self.img)
+
+
+def greet(peers):
+    barrier = pltpu.get_barrier_semaphore()
+    for peer in peers:
+        pl.semaphore_signal(barrier, inc=1, device_id=peer, device_id_type=MESH_IDS)
+    pl.semaphore_wait(barrier, len(peers))
+
+
+def remote(src, dst, send, recv, peer):
+    return pltpu.make_async_remote_copy(
+        src_ref=src, dst_ref=dst, send_sem=send, recv_sem=recv, device_id=peer, device_id_type=MESH_IDS
+    )
+
+
+def rows_at(ref, first, count):
+    return ref.at[pl.ds(pl.multiple_of(first, 16), count)]
+
+
+class Spread:
+    def __init__(self, here, out, block, first, count, send, recv):
+        self.here, self.out, self.block = here, out, block
+        self.first, self.count, self.send, self.recv = first, count, send, recv
+        self.half = count // 2
+        self.sent = []
+
+    def part(self, seq, which):
+        first = seq * self.block + self.first
+        if which == ALL:
+            return rows_at(self.out, first, self.count)
+        return rows_at(self.out, first + (self.half if which == BACK else 0), self.half)
+
+    def copy(self, src, dst, slot, peer):
+        return remote(src, dst, self.send.at[slot], self.recv.at[slot], peer)
+
+    def go(self, src, dst, slot, peer):
+        made = self.copy(src, dst, slot, peer)
+        made.start()
+        self.sent.append(made)
+
+    def own(self, src, src_first):
+        here, seq = self.here, self.here.seq
+
+        def own_part(which):
+            if which == ALL:
+                return rows_at(src, src_first, self.count)
+            return rows_at(src, src_first + (self.half if which == BACK else 0), self.half)
+
+        self.go(own_part(FRONT), self.part(seq, FRONT), 0, here.x)
+        self.go(own_part(BACK), self.part(seq, BACK), 1, here.y)
+        self.go(own_part(BACK), self.part(seq, BACK), 2, here.x)
+        self.go(own_part(FRONT), self.part(seq, FRONT), 3, here.y)
+        self.go(own_part(ALL), self.part(seq, ALL), 4, here.core)
+
+    def arrived(self, slot, seq, which):
+        target = self.part(seq, which)
+        self.copy(target, target, slot, self.here.core).wait_recv()
+
+    def forward(self):
+        here = self.here
+        self.arrived(0, here.s_x, FRONT)
+        self.go(self.part(here.s_x, FRONT), self.part(here.s_x, FRONT), 5, here.y)
+        self.arrived(1, here.s_y, BACK)
+        self.go(self.part(here.s_y, BACK), self.part(here.s_y, BACK), 6, here.x)
+        self.arrived(2, here.s_x, BACK)
+        self.go(self.part(here.s_x, ALL), self.part(here.s_x, ALL), 7, here.core)
+        self.arrived(3, here.s_y, FRONT)
+        self.go(self.part(here.s_y, ALL), self.part(here.s_y, ALL), 8, here.core)
+
+    def corner(self):
+        here = self.here
+        self.arrived(5, here.s_xy, FRONT)
+        self.arrived(6, here.s_xy, BACK)
+        self.go(self.part(here.s_xy, ALL), self.part(here.s_xy, ALL), 9, here.core)
+
+    def finish(self):
+        core = self.here.s_core
+        self.arrived(4, core, ALL)
+        self.arrived(7, flipped(core, 1), ALL)
+        self.arrived(8, flipped(core, 2), ALL)
+        self.arrived(9, flipped(flipped(core, 1), 2), ALL)
+        for made in self.sent:
+            made.wait_send()
+
+
+def wavefront(stages, count, waiting=()):
+    waiting = list(waiting)
+    ticks = count + max(lag for lag, _ in stages)
+    share = -(-len(waiting) // max(ticks - 2, 1))
+    for tick in range(ticks):
+        for lag, stage in reversed(stages):
+            piece = tick - lag
+            if 0 <= piece < count:
+                stage(piece)
+        for launch in waiting[:share]:
+            launch()
+        del waiting[:share]
+
+
+def weight_blocks(weight, side):
+    if side == INWARD:
+        return (weight.shape[0], weight.shape[1] // PLANE)
+    return (weight.shape[0] // PLANE, weight.shape[1])
+
+
+def intake(gathered, weights, sides, cid):
+    n_rows, n_weights = len(gathered), len(weights)
+    pieces = PIECES
+
+    def kernel(*refs):
+        row_refs, weight_refs = refs[:n_rows], refs[n_rows : n_rows + n_weights]
+        refs = refs[n_rows + n_weights :]
+        row_outs, weight_outs = refs[:n_rows], refs[n_rows : n_rows + n_weights]
+        local, send, recv, w_local, w_send, w_recv, z_send, z_recv = refs[n_rows + n_weights :]
+        here = Places()
+        seq, tp, img = here.seq, here.tp, here.img
+        others = [lax.rem(seq + step, PLANE) for step in range(1, PLANE)]
+        greet([(other, tp, img) for other in others] + [here.img_peer])
+
+        def slot_of(out, side, shape, from_seq, from_img):
+            number = from_seq * 2 + from_img
+            if side == INWARD:
+                return out.at[pl.ds(pl.multiple_of(number * shape[0], shape[0]), shape[0])]
+            return out.at[:, pl.ds(pl.multiple_of(number * shape[1], shape[1]), shape[1])]
+
+        def block_of(weight, side, shape, to_seq):
+            if side == INWARD:
+                return weight.at[:, pl.ds(pl.multiple_of(to_seq * shape[1], shape[1]), shape[1])]
+            return weight.at[pl.ds(pl.multiple_of(to_seq * shape[0], shape[0]), shape[0])]
+
+        flights, own_copies = [], []
+
+        def begin(index):
+            weight, out, side = weight_refs[index], weight_outs[index], sides[index]
+            shape = weight_blocks(weight, side)
+            mine = pltpu.make_async_copy(
+                block_of(weight, side, shape, seq), slot_of(out, side, shape, seq, img), w_local.at[index]
+            )
+            mine.start()
+            crossing = remote(
+                block_of(weight, side, shape, seq),
+                slot_of(out, side, shape, seq, img),
+                z_send.at[index, 0],
+                z_recv.at[index, 0],
+                here.img_peer,
+            )
+            crossing.start()
+            own_copies.append(mine)
+            flights.append(crossing)
+            for step, other in enumerate(others, 1):
+                made = remote(
+                    block_of(weight, side, shape, other),
+                    slot_of(out, side, shape, seq, img),
+                    w_send.at[index, step],
+                    w_recv.at[index, step],
+                    here.at(other),
+                )
+                made.start()
+                flights.append(made)
+
+        spreads = []
+        for number, (rows, out) in enumerate(zip(row_refs, row_outs)):
+            block = rows.shape[0]
+            count = block // pieces
+            keep = pltpu.make_async_copy(rows, rows_at(out, seq * block, block), local.at[number])
+            keep.start()
+            own_copies.append(keep)
+            for piece in range(pieces):
+                at = number * pieces + piece
+                spreads.append(
+                    (Spread(here, out, block, piece * count, count, send.at[at], recv.at[at]), rows, piece * count)
+                )
+
+        def cross(piece):
+            for index in range(piece, n_weights, len(spreads)):
+                weight, out, side = weight_refs[index], weight_outs[index], sides[index]
+                shape = weight_blocks(weight, side)
+                for step in range(1, PLANE):
+                    source = lax.rem(seq + PLANE - step, PLANE)
+                    landed = slot_of(out, side, shape, source, img)
+                    remote(landed, landed, w_send.at[index, step], w_recv.at[index, step], here.core).wait_recv()
+                    crossing = remote(
+                        landed, landed, z_send.at[index, step], z_recv.at[index, step], here.img_peer
+                    )
+                    crossing.start()
+                    flights.append(crossing)
+
+        def own_rows(piece):
+            for index in range(piece, n_weights, len(spreads)):
+                begin(index)
+            spreads[piece][0].own(spreads[piece][1], spreads[piece][2])
+
+        wavefront(
+            [
+                (0, own_rows),
+                (2, lambda piece: spreads[piece][0].forward()),
+                (3, lambda piece: cross(piece)),
+                (4, lambda piece: spreads[piece][0].corner()),
+            ],
+            len(spreads),
+        )
+        for index, (weight, out, side) in enumerate(zip(weight_refs, weight_outs, sides)):
+            shape = weight_blocks(weight, side)
+            for step in range(PLANE):
+                source = lax.rem(seq + PLANE - step, PLANE)
+                landed = slot_of(out, side, shape, source, 1 - img)
+                remote(landed, landed, z_send.at[index, step], z_recv.at[index, step], here.core).wait_recv()
+        for spread, _, _ in spreads:
+            spread.finish()
+        for made in flights:
+            made.wait_send()
+        for made in own_copies:
+            made.wait()
+
+    def whole(weight, side):
+        shape = weight_blocks(weight, side)
+        if side == INWARD:
+            return jax.ShapeDtypeStruct((2 * PLANE * shape[0], shape[1]), weight.dtype)
+        return jax.ShapeDtypeStruct((shape[0], 2 * PLANE * shape[1]), weight.dtype)
+
+    dma = pltpu.SemaphoreType.DMA
+    outs = [jax.ShapeDtypeStruct((PLANE * rows.shape[0], rows.shape[1]), rows.dtype) for rows in gathered]
+    outs += [whole(weight, side) for weight, side in zip(weights, sides)]
+    made = pl.pallas_call(
+        kernel,
+        out_shape=tuple(outs),
+        in_specs=[ANYWHERE] * (n_rows + n_weights),
+        out_specs=tuple([ANYWHERE] * len(outs)),
+        scratch_shapes=[
+            dma((n_rows,)),
+            dma((n_rows * pieces, 10)),
+            dma((n_rows * pieces, 10)),
+            dma((n_weights,)),
+            dma((n_weights, PLANE)),
+            dma((n_weights, PLANE)),
+            dma((n_weights, PLANE)),
+            dma((n_weights, PLANE)),
+        ],
+        compiler_params=pltpu.CompilerParams(
+            collective_id=cid, has_side_effects=True, vmem_limit_bytes=VMEM_BYTES
+        ),
+    )(*gathered, *weights)
+    return made[:n_rows], made[n_rows:]
+
+
+class Rider:
+    inputs, out_shapes, scratch = (), (), ()
+
+    def bind(self, here, ins, outs, scratch):
+        self.here, self.ins, self.outs, self.held = here, ins, outs, scratch
+        self.sent, self.kept, self.due, self.launches = [], [], [], []
+
+    def keep(self, src, dst, sem):
+        made = pltpu.make_async_copy(src, dst, sem)
+        self.launches.append(made.start)
+        self.kept.append(made)
+
+    def send(self, src, dst, send, recv, peer):
+        made = remote(src, dst, send, recv, peer)
+        self.launches.append(made.start)
+        self.sent.append(made)
+
+    def finish(self):
+        for dst, send, recv in self.due:
+            remote(dst, dst, send, recv, self.here.core).wait_recv()
+        for made in self.sent:
+            made.wait_send()
+        for made in self.kept:
+            made.wait()
+
+
+class PlaneWeights(Rider):
+    def __init__(self, weights, sides):
+        self.inputs, self.sides = weights, sides
+        self.blocks = [weight_blocks(weight, side) for weight, side in zip(weights, sides)]
+        self.out_shapes = [
+            jax.ShapeDtypeStruct((PLANE,) + block, weight.dtype) for block, weight in zip(self.blocks, weights)
+        ]
+        dma = pltpu.SemaphoreType.DMA
+        self.scratch = [dma((len(weights), PLANE)), dma((len(weights), PLANE))]
+
+    def peers(self, here):
+        return [here.at(lax.rem(here.seq + step, PLANE)) for step in range(1, PLANE)]
+
+    def start(self):
+        here, (send, recv) = self.here, self.held
+        for index, (weight, out, side, block) in enumerate(zip(self.ins, self.outs, self.sides, self.blocks)):
+            for step in range(PLANE):
+                target = lax.rem(here.seq + step, PLANE)
+                source = lax.rem(here.seq + PLANE - step, PLANE)
+                if side == INWARD:
+                    part = weight.at[:, pl.ds(pl.multiple_of(target * block[1], block[1]), block[1])]
+                else:
+                    part = weight.at[pl.ds(pl.multiple_of(target * block[0], block[0]), block[0])]
+                if step == 0:
+                    self.keep(part, out.at[here.seq], recv.at[index, 0])
+                else:
+                    self.send(part, out.at[here.seq], send.at[index, step], recv.at[index, step], here.at(target))
+                    self.due.append((out.at[source], send.at[index, step], recv.at[index, step]))
+
+
+class CrossWeights(Rider):
+    def __init__(self, blocks, sides):
+        self.inputs, self.sides = blocks, sides
+        self.out_shapes = []
+        for block, side in zip(blocks, sides):
+            count, rows, columns = block.shape
+            shape = (count, 2, rows, columns) if side == INWARD else (rows, count * 2 * columns)
+            self.out_shapes.append(jax.ShapeDtypeStruct(shape, block.dtype))
+        dma = pltpu.SemaphoreType.DMA
+        self.scratch = [dma((len(blocks), PLANE)), dma((len(blocks), PLANE)), dma((len(blocks), PLANE))]
+
+    def peers(self, here):
+        return [here.img_peer]
+
+    def start(self):
+        here, (send, recv, local) = self.here, self.held
+        for index, (block, out, side) in enumerate(zip(self.ins, self.outs, self.sides)):
+            width = block.shape[2]
+            for seq in range(PLANE):
+
+                def place(img, seq=seq, width=width, out=out, side=side):
+                    if side == INWARD:
+                        return out.at[seq, img]
+                    return out.at[:, pl.ds(pl.multiple_of((seq * 2 + img) * width, width), width)]
+
+                self.send(
+                    block.at[seq], place(here.img), send.at[index, seq], recv.at[index, seq], here.img_peer
+                )
+                self.keep(block.at[seq], place(here.img), local.at[index, seq])
+                self.due.append((place(1 - here.img), send.at[index, seq], recv.at[index, seq]))
+
+
+class CrossGrads(Rider):
+    def __init__(self, grads, sides):
+        self.inputs, self.sides = grads, sides
+        self.out_shapes = []
+        for grad, side in zip(grads, sides):
+            if side == INWARD:
+                shape = (grad.shape[0], grad.shape[2], grad.shape[3])
+            else:
+                shape = (PLANE, grad.shape[0], grad.shape[1] // (2 * PLANE))
+            self.out_shapes.append(jax.ShapeDtypeStruct(shape, grad.dtype))
+        dma = pltpu.SemaphoreType.DMA
+        self.scratch = [dma((len(grads), PLANE)), dma((len(grads), PLANE))]
+
+    def peers(self, here):
+        return [here.img_peer]
+
+    def start(self):
+        here, (send, recv) = self.here, self.held
+        for index, (grad, out, side) in enumerate(zip(self.ins, self.outs, self.sides)):
+            width = out.shape[2]
+            for seq in range(PLANE):
+                if side == INWARD:
+                    part = grad.at[seq, 1 - here.img]
+                else:
+                    part = grad.at[:, pl.ds(pl.multiple_of((seq * 2 + 1 - here.img) * width, width), width)]
+                self.send(part, out.at[seq], send.at[index, seq], recv.at[index, seq], here.img_peer)
+                self.due.append((out.at[seq], send.at[index, seq], recv.at[index, seq]))
+
+
+class Stream:
+    def __init__(self, left, right, across, row_inputs, row_kinds, row_outs, row_function, gather):
+        self.inputs = [left, right] + list(row_inputs)
+        self.across, self.row_kinds, self.row_outs = across, row_kinds, row_outs
+        self.row_function, self.gather = row_function, gather
+        rows_all = left.shape[0]
+        width = right.shape[0] if across else right.shape[1]
+        self.width, self.block, self.pieces = width, rows_all // PLANE, PIECES
+        self.count = self.block // self.pieces
+        self.half = self.count // 2
+        low_type = jnp.bfloat16
+        self.out_shapes = [shape for shape, _ in row_outs]
+        if gather:
+            self.out_shapes.append(jax.ShapeDtypeStruct((rows_all, width), low_type))
+        dma = pltpu.SemaphoreType.DMA
+        block, pieces, count, half = self.block, self.pieces, self.count, self.half
+        self.scratch = [
+            pltpu.VMEM((4, block, width), low_type),
+            pltpu.VMEM((4, block, width), low_type),
+            pltpu.VMEM((4, block, width), jnp.float32),
+            pltpu.VMEM((pieces, half, width), low_type),
+            pltpu.VMEM((pieces, half, width), low_type),
+            pltpu.VMEM((pieces, count, width), low_type),
+            pltpu.VMEM((pieces, count, width), low_type),
+            pltpu.VMEM((pieces, count, width), low_type),
+            pltpu.VMEM((pieces, count, width), low_type),
+            pltpu.VMEM((block, width), low_type),
+            dma((4,)),
+            dma((4,)),
+            dma((pieces, 7)),
+            dma((pieces, 7)),
+            dma((pieces, 10)),
+            dma((pieces, 10)),
+            dma((pieces,)),
+        ]
+
+    def out_specs(self):
+        return [ON_CHIP] * len(self.row_outs) + [ANYWHERE] * (len(self.out_shapes) - len(self.row_outs))
+
+    def peers(self, here):
+        return [here.core, here.x, here.y, here.tp_peer]
+
+    def bind(self, here, ins, outs, scratch):
+        self.here = here
+        self.left, self.right, self.ins = ins[0], ins[1], ins[2:]
+        self.outs = outs
+        (self.away, self.core_in, self.near, self.from_xd, self.from_yd, self.from_x, self.from_y) = scratch[:7]
+        (self.mine, self.theirs, self.low, self.c_send, self.c_recv) = scratch[7:12]
+        (self.send, self.recv, self.g_send, self.g_recv, self.l_sem) = scratch[12:]
+        self.sent, self.spreads, self.core_copies = [], [], {}
+
+    def chunk(self, base, kind):
+        if kind in (1, 3):
+            base = flipped(base, 1)
+        if kind in (2, 3):
+            base = flipped(base, 2)
+        return base
+
+    def product(self, seq, target, low_type):
+        first = pl.multiple_of(seq * self.block, self.block)
+        rows = self.left[pl.ds(first, self.block), :]
+        step = min(512, self.width)
+        for column in range(0, self.width, step):
+            if self.across:
+                part = lax.dot_general(
+                    rows,
+                    self.right[column : column + step, :],
+                    (((1,), (1,)), ((), ())),
+                    preferred_element_type=jnp.float32,
+                )
+            else:
+                part = jnp.dot(
+                    rows, self.right[:, column : column + step], preferred_element_type=jnp.float32
+                )
+            target[:, column : column + step] = part.astype(low_type)
+
+    def begin(self):
+        here = self.here
+        for kind in (3, 1, 2, 0):
+            self.product(self.chunk(here.s_core, kind), self.away.at[kind], jnp.bfloat16)
+            made = remote(
+                self.away.at[kind], self.core_in.at[kind], self.c_send.at[kind], self.c_recv.at[kind], here.core
+            )
+            made.start()
+            self.core_copies[kind] = made
+            self.product(self.chunk(here.seq, kind), self.near.at[kind], jnp.float32)
+
+    def go(self, src, dst, piece, slot, peer):
+        made = remote(src, dst, self.send.at[piece, slot], self.recv.at[piece, slot], peer)
+        made.start()
+        self.sent.append(made)
+
+    def landed(self, dst, piece, slot):
+        remote(dst, dst, self.send.at[piece, slot], self.recv.at[piece, slot], self.here.core).wait_recv()
+
+    def held(self, kind, piece, which=ALL):
+        first, rows = piece * self.count, self.count
+        if which != ALL:
+            first, rows = first + (self.half if which == BACK else 0), self.half
+        return self.core_in.at[kind, pl.ds(first, rows)]
+
+    def folded(self, kind, piece):
+        if piece == 0:
+            self.core_copies[kind].wait_recv()
+        near = self.near[kind, pl.ds(piece * self.count, self.count), :]
+        return self.held(kind, piece)[...].astype(jnp.float32) + near
+
+    def first_sends(self, piece):
+        here, half = self.here, self.half
+        self.held(3, piece)[...] = self.folded(3, piece).astype(jnp.bfloat16)
+        self.go(self.held(3, piece, FRONT), self.from_xd.at[piece], piece, 0, here.x)
+        self.go(self.held(3, piece, BACK), self.from_yd.at[piece], piece, 1, here.y)
+        self.held(1, piece)[...] = self.folded(1, piece).astype(jnp.bfloat16)
+        self.go(self.held(1, piece, FRONT), self.from_x.at[piece, pl.ds(0, half)], piece, 2, here.x)
+        self.held(2, piece)[...] = self.folded(2, piece).astype(jnp.bfloat16)
+        self.go(self.held(2, piece, BACK), self.from_y.at[piece, pl.ds(half, half)], piece, 3, here.y)
+
+    def second_sends(self, piece):
+        here, half = self.here, self.half
+        self.landed(self.from_xd.at[piece], piece, 0)
+        at = self.held(2, piece, FRONT)
+        at[...] = (at[...].astype(jnp.float32) + self.from_xd[piece].astype(jnp.float32)).astype(jnp.bfloat16)
+        self.go(at, self.from_y.at[piece, pl.ds(0, half)], piece, 4, here.y)
+        self.landed(self.from_yd.at[piece], piece, 1)
+        at = self.held(1, piece, BACK)
+        at[...] = (at[...].astype(jnp.float32) + self.from_yd[piece].astype(jnp.float32)).astype(jnp.bfloat16)
+        self.go(at, self.from_x.at[piece, pl.ds(half, half)], piece, 5, here.x)
+
+    def plane_sum(self, piece):
+        half = self.half
+        self.landed(self.from_x.at[piece, pl.ds(0, half)], piece, 2)
+        self.landed(self.from_y.at[piece, pl.ds(half, half)], piece, 3)
+        self.landed(self.from_y.at[piece, pl.ds(0, half)], piece, 4)
+        self.landed(self.from_x.at[piece, pl.ds(half, half)], piece, 5)
+        total = self.folded(0, piece)
+        total = total + self.from_x[piece].astype(jnp.float32) + self.from_y[piece].astype(jnp.float32)
+        self.mine[piece] = total.astype(jnp.bfloat16)
+        self.go(self.mine.at[piece], self.theirs.at[piece], piece, 6, self.here.tp_peer)
+
+    def rows_done(self, piece):
+        here = self.here
+        self.landed(self.theirs.at[piece], piece, 6)
+        total = self.mine[piece].astype(jnp.float32) + self.theirs[piece].astype(jnp.float32)
+        rows = pl.ds(piece * self.count, self.count)
+        views = [ref.at[rows] if kind == ROWS else ref for ref, kind in zip(self.ins, self.row_kinds)]
+        out_views = [ref.at[rows] if kind == ROWS else ref for ref, (_, kind) in zip(self.outs, self.row_outs)]
+        given = self.row_function(total, piece, views, out_views)
+        if self.gather:
+            out = self.outs[-1]
+            self.low[rows, :] = given
+            first = pl.multiple_of(here.seq * self.block + piece * self.count, 16)
+            keep = pltpu.make_async_copy(self.low.at[rows], out.at[pl.ds(first, self.count)], self.l_sem.at[piece])
+            keep.start()
+            spread = Spread(
+                here, out, self.block, piece * self.count, self.count, self.g_send.at[piece], self.g_recv.at[piece]
+            )
+            spread.own(self.low, piece * self.count)
+            self.spreads.append((spread, keep))
+
+    def stages(self):
+        stages = [(0, self.first_sends), (1, self.second_sends), (2, self.plane_sum), (4, self.rows_done)]
+        if self.gather:
+            stages.append((5, lambda piece: self.spreads[piece][0].forward()))
+            stages.append((6, lambda piece: self.spreads[piece][0].corner()))
+        return stages
+
+    def finish(self):
+        for spread, keep in self.spreads:
+            spread.finish()
+            keep.wait()
+        for made in self.sent:
+            made.wait_send()
+        for made in self.core_copies.values():
+            made.wait_send()
+
+
+def exchange(streams, riders, cid):
+    parts = list(streams) + list(riders)
+
+    def kernel(*refs):
+        here = Places()
+        refs = list(refs)
+
+        def take(count):
+            taken = refs[:count]
+            del refs[:count]
+            return taken
+
+        ins = [take(len(part.inputs)) for part in parts]
+        outs = [take(len(part.out_shapes)) for part in parts]
+        for part, part_ins, part_outs in zip(parts, ins, outs):
+            part.bind(here, part_ins, part_outs, take(len(part.scratch)))
+        wide_riders = [rider for rider in riders if len(rider.peers(here)) > 1]
+        peers = [here.tp_peer]
+        if any(not isinstance(rider, PlaneWeights) for rider in riders):
+            peers.append(here.img_peer)
+        if wide_riders:
+            peers += wide_riders[0].peers(here)
+        else:
+            peers += [here.core, here.x, here.y]
+        greet(peers)
+        streams[0].begin()
+        for rider in riders:
+            rider.start()
+        for stream in streams[1:]:
+            stream.begin()
+        stages = []
+        for stream in reversed(streams):
+            stages += stream.stages()
+        wavefront(stages, PIECES, [launch for rider in riders for launch in rider.launches])
+        for part in parts:
+            part.finish()
+
+    out_shapes = [shape for part in parts for shape in part.out_shapes]
+    in_specs = [ON_CHIP] * sum(len(stream.inputs) for stream in streams)
+    in_specs += [ANYWHERE] * sum(len(rider.inputs) for rider in riders)
+    out_specs = [spec for stream in streams for spec in stream.out_specs()]
+    out_specs += [ANYWHERE] * sum(len(rider.out_shapes) for rider in riders)
+    made = pl.pallas_call(
+        kernel,
+        out_shape=tuple(out_shapes),
+        in_specs=in_specs,
+        out_specs=tuple(out_specs),
+        scratch_shapes=[item for part in parts for item in part.scratch],
+        compiler_params=pltpu.CompilerParams(
+            collective_id=cid, has_side_effects=True, vmem_limit_bytes=VMEM_BYTES
+        ),
+    )(*[value for part in parts for value in part.inputs])
+    made = list(made)
+    split = []
+    for part in parts:
+        split.append(made[: len(part.out_shapes)])
+        del made[: len(part.out_shapes)]
+    return split
+
+
+def finale(pairs, late, sides, late_sides, small, latents_t, query_rows, cid):
+    n, n_late = len(sides), len(late_sides)
+    all_sides = list(sides) + list(late_sides)
+    grads = [grad for grad, _ in pairs] + list(late)
+
+    def block_shape(grad, side):
+        if side == INWARD:
+            return (grad.shape[2], grad.shape[3])
+        return (grad.shape[0], grad.shape[1] // (2 * PLANE))
+
+    blocks = [block_shape(grad, side) for grad, side in zip(grads, all_sides)]
+    total = n + n_late
+
+    def kernel(*refs):
+        refs = list(refs)
+
+        def take(count):
+            taken = refs[:count]
+            del refs[:count]
+            return taken
+
+        grad_refs = take(total)
+        theirs = take(n)
+        small_ref, latents_ref, query_ref = take(3)
+        out_refs = take(total)
+        sums_out, query_out, latent_out = take(3)
+        late_theirs = take(n_late)
+        summed = take(total)
+        small_theirs, small_mine, small_all, lat_mine, lat_theirs = take(5)
+        z_send, z_recv, send, recv, local, s_send, s_recv = take(7)
+        here = Places()
+        seq, img = here.seq, here.img
+        ring = [here.at(lax.rem(seq + step, PLANE)) for step in range(1, PLANE)]
+        greet(ring + [here.img_peer, here.tp_peer])
+        theirs = theirs + late_theirs
+
+        def part_of(index, to_seq, to_img):
+            ref, block = grad_refs[index], blocks[index]
+            if all_sides[index] == INWARD:
+                return ref.at[to_seq, to_img]
+            return ref.at[:, pl.ds(pl.multiple_of((to_seq * 2 + to_img) * block[1], block[1]), block[1])]
+
+        def slot_of(index, from_seq):
+            ref, block = out_refs[index], blocks[index]
+            if all_sides[index] == INWARD:
+                return ref.at[:, pl.ds(pl.multiple_of(from_seq * block[1], block[1]), block[1])]
+            return ref.at[pl.ds(pl.multiple_of(from_seq * block[0], block[0]), block[0])]
+
+        waits, crossings = [], {}
+        small_cross = remote(small_ref, small_theirs, s_send.at[0], s_recv.at[0], here.img_peer)
+        small_cross.start()
+        for index in range(n, total):
+            for step in range(PLANE):
+                target = lax.rem(seq + step, PLANE)
+                made = remote(
+                    part_of(index, target, 1 - img),
+                    theirs[index].at[target],
+                    z_send.at[index - n, step],
+                    z_recv.at[index - n, step],
+                    here.img_peer,
+                )
+                made.start()
+                crossings[index, step] = made
+
+        def deliver(index):
+            for step in range(PLANE):
+                target = lax.rem(seq + step, PLANE)
+                if index >= n:
+                    crossings[index, step].wait_recv()
+                mine = part_of(index, target, img)[...].astype(jnp.float32)
+                summed[index][target] = (mine + theirs[index][target].astype(jnp.float32)).astype(jnp.bfloat16)
+                if step == 0:
+                    made = pltpu.make_async_copy(summed[index].at[target], slot_of(index, seq), local.at[index])
+                    made.start()
+                    waits.append(made.wait)
+                    continue
+                made = remote(
+                    summed[index].at[target],
+                    slot_of(index, seq),
+                    send.at[index, step],
+                    recv.at[index, step],
+                    here.at(target),
+                )
+                made.start()
+                waits.append(made.wait_send)
+
+        deliver(0)
+        small_cross.wait()
+        small_mine[...] = small_ref[...] + small_theirs[...]
+        small_all[seq] = small_mine[...]
+        small_copies = []
+        for step, peer in enumerate(ring, 1):
+            made = remote(small_mine, small_all.at[seq], s_send.at[step], s_recv.at[step], peer)
+            made.start()
+            small_copies.append(made)
+        for index in range(1, total):
+            deliver(index)
+        for made in small_copies:
+            made.wait()
+        sums_out[...] = small_all[...]
+        rows = latents_ref.shape[1]
+        latent_part = jnp.zeros(lat_mine.shape, jnp.float32)
+        columns = small_all.shape[2]
+        for source in range(PLANE):
+            probe = small_all[source, :rows, :]
+            at = slice(source * columns, (source + 1) * columns)
+            query_out[:, at] = jnp.dot(
+                latents_ref[...], probe, precision=HIGHEST_PRECISION, preferred_element_type=jnp.float32
+            )
+            latent_part += lax.dot_general(
+                probe,
+                query_ref[:, at],
+                (((1,), (1,)), ((), ())),
+                precision=HIGHEST_PRECISION,
+                preferred_element_type=jnp.float32,
+            )
+        lat_mine[...] = latent_part
+        last = remote(lat_mine, lat_theirs, s_send.at[PLANE], s_recv.at[PLANE], here.tp_peer)
+        last.start()
+        last.wait()
+        latent_out[...] = lat_mine[...] + lat_theirs[...]
+        for index in range(total):
+            for step in range(1, PLANE):
+                source = lax.rem(seq + PLANE - step, PLANE)
+                at = slot_of(index, source)
+                remote(at, at, send.at[index, step], recv.at[index, step], here.core).wait_recv()
+        for wait in waits:
+            wait()
+        for made in crossings.values():
+            made.wait_send()
+
+    dma, low_type, f32 = pltpu.SemaphoreType.DMA, jnp.bfloat16, jnp.float32
+    outs = []
+    for block, side in zip(blocks, all_sides):
+        shape = (block[0], PLANE * block[1]) if side == INWARD else (PLANE * block[0], block[1])
+        outs.append(jax.ShapeDtypeStruct(shape, low_type))
+    small_shapes = [
+        jax.ShapeDtypeStruct((PLANE,) + small.shape, f32),
+        jax.ShapeDtypeStruct(query_rows.shape, f32),
+        jax.ShapeDtypeStruct((latents_t.shape[1], latents_t.shape[0]), f32),
+    ]
+    made = pl.pallas_call(
+        kernel,
+        out_shape=tuple(outs + small_shapes),
+        in_specs=[ON_CHIP] * (total + n + 3),
+        out_specs=tuple([ANYWHERE] * total + [ON_CHIP] * 3),
+        scratch_shapes=[pltpu.VMEM((PLANE,) + block, low_type) for block in blocks[n:]]
+        + [pltpu.VMEM((PLANE,) + block, low_type) for block in blocks]
+        + [
+            pltpu.VMEM(small.shape, f32),
+            pltpu.VMEM(small.shape, f32),
+            pltpu.VMEM((PLANE,) + small.shape, f32),
+            pltpu.VMEM((latents_t.shape[1], latents_t.shape[0]), f32),
+            pltpu.VMEM((latents_t.shape[1], latents_t.shape[0]), f32),
+            dma((n_late, PLANE)),
+            dma((n_late, PLANE)),
+            dma((total, PLANE)),
+            dma((total, PLANE)),
+            dma((total,)),
+            dma((PLANE + 1,)),
+            dma((PLANE + 1,)),
+        ],
+        compiler_params=pltpu.CompilerParams(
+            collective_id=cid, has_side_effects=True, vmem_limit_bytes=VMEM_BYTES
+        ),
+    )(*grads, *[given for _, given in pairs], small, latents_t, query_rows)
+    return made[:total], made[total:]
+
+
+def widened(arrays):
+    def kernel(*refs):
+        for src, dst in zip(refs[: len(arrays)], refs[len(arrays) :]):
+            dst[...] = src[...].astype(jnp.float32)
+
+    return pl.pallas_call(
+        kernel,
+        out_shape=tuple(jax.ShapeDtypeStruct(array.shape, jnp.float32) for array in arrays),
+        in_specs=[ON_CHIP] * len(arrays),
+        out_specs=tuple([ON_CHIP] * len(arrays)),
+        compiler_params=pltpu.CompilerParams(vmem_limit_bytes=VMEM_BYTES),
+    )(*arrays)
+
+
+def small_total(values, cid):
+    def kernel(in_ref, out_ref, plane, mine, theirs, send, recv):
+        here = Places()
+        seq, tp, img = here.seq, here.tp, here.img
+        peers = [(lax.rem(seq + step, PLANE), tp, img) for step in range(1, PLANE)]
+        greet(peers + [here.tp_peer])
+        made = []
+        for step, peer in enumerate(peers):
+            copy = remote(in_ref, plane.at[step], send.at[step], recv.at[step], peer)
+            copy.start()
+            made.append(copy)
+        total = in_ref[...]
+        for step, copy in enumerate(made):
+            copy.wait_recv()
+            total = total + plane[step]
+        mine[...] = total
+        last = remote(mine, theirs, send.at[PLANE - 1], recv.at[PLANE - 1], here.tp_peer)
+        last.start()
+        last.wait()
+        out_ref[...] = mine[...] + theirs[...]
+        for copy in made:
+            copy.wait_send()
+
+    dma = pltpu.SemaphoreType.DMA
+    return pl.pallas_call(
+        kernel,
+        out_shape=jax.ShapeDtypeStruct(values.shape, values.dtype),
+        in_specs=[ON_CHIP],
+        out_specs=ON_CHIP,
+        scratch_shapes=[
+            pltpu.VMEM((PLANE - 1,) + values.shape, values.dtype),
+            pltpu.VMEM(values.shape, values.dtype),
+            pltpu.VMEM(values.shape, values.dtype),
+            dma((PLANE,)),
+            dma((PLANE,)),
+        ],
+        compiler_params=pltpu.CompilerParams(collective_id=cid, has_side_effects=True),
+    )(values)
+
+
+def small_gather(values, cid):
+    def kernel(in_ref, out_ref, send, recv):
+        here = Places()
+        seq, tp, img = here.seq, here.tp, here.img
+        peers = []
+        for step in range(2 * PLANE):
+            if step == 0:
+                continue
+            peers.append((lax.rem(seq + step // 2, PLANE), tp, lax.rem(img + step % 2, 2)))
+        greet(peers)
+        out_ref[seq, img] = in_ref[...]
+        made = []
+        for step, peer in enumerate(peers):
+            copy = remote(in_ref, out_ref.at[seq, img], send.at[step], recv.at[step], peer)
+            copy.start()
+            made.append(copy)
+        for copy in made:
+            copy.wait()
+
+    dma = pltpu.SemaphoreType.DMA
+    return pl.pallas_call(
+        kernel,
+        out_shape=jax.ShapeDtypeStruct((PLANE, 2) + values.shape, values.dtype),
+        in_specs=[ON_CHIP],
+        out_specs=ON_CHIP,
+        scratch_shapes=[dma((2 * PLANE - 1,)), dma((2 * PLANE - 1,))],
+        compiler_params=pltpu.CompilerParams(
+            collective_id=cid, has_side_effects=True, vmem_limit_bytes=VMEM_BYTES
+        ),
+    )(values)
+
+
+def norm_rows(rows, gain, shift):
+    center = rows - jnp.mean(rows, -1, keepdims=True)
+    factor = lax.rsqrt(jnp.mean(center * center, -1, keepdims=True) + EPSILON)
+    normal = center * factor
+    return (normal * gain + shift, normal, factor)
+
+
+def dot32(left, right):
+    return jnp.dot(left, right, preferred_element_type=jnp.float32)
+
+
+def on_plane(
+    text,
+    segment,
+    features,
+    image_count,
+    image_slot,
+    cotangent,
+    input_gain,
+    input_shift,
+    query_weight,
+    key_weight,
+    value_weight,
+    inner_gain,
+    inner_shift,
+    out_weight,
+    middle_gain,
+    middle_shift,
+    up_weight,
+    up_bias,
+    hidden_gain,
+    hidden_shift,
+    down_weight,
+    latents,
+    resample_query,
+    resample_key,
+    resample_value,
+    resample_out,
+):
+    f32, low = jnp.float32, jnp.bfloat16
+    row_count, model_width = text.shape[1], text.shape[2]
+    group_rows = segment.shape[1]
+    seq_rank = lax.axis_index(SEQ)
+    image_slots = features.shape[1]
+    image_total = image_slot.shape[1]
+    half_width = query_weight.shape[1]
+    own_width = half_width // PLANE
+    own_heads = own_width // HEAD
+    score_scale = HEAD ** (-0.5)
+
+    rows, own = intake(
+        (features[0].reshape(image_slots * PATCH, features.shape[3]),),
+        (
+            resample_key,
+            resample_value,
+            resample_query,
+            resample_out,
+            query_weight,
+            key_weight,
+            value_weight,
+            out_weight,
+        ),
+        (INWARD, INWARD, INWARD, OUTWARD, INWARD, INWARD, INWARD, OUTWARD),
+        1,
+    )
+    (pictures,) = rows
+    image_key_own, image_value_own, probe_own, image_out_own, query_own, key_own, value_own, out_own = own
+    qkv_own = jnp.concatenate([query_own, key_own, value_own], 1)
+    latent_all = small_gather(latents, 2).transpose(2, 0, 1, 3).reshape(LAT, model_width)
+
+    probe = dot32(latent_all, probe_own).astype(low).reshape(LAT, own_heads, HEAD)
+    image_keys = dot32(pictures, image_key_own).astype(low).reshape(image_total, PATCH, own_heads, HEAD)
+    image_values = dot32(pictures, image_value_own).astype(low).reshape(image_total, PATCH, own_heads, HEAD)
+    image_scores = (
+        jnp.einsum("qhd,iphd->ihqp", probe, image_keys, preferred_element_type=f32) * score_scale
+    )
+    image_probs = jax.nn.softmax(image_scores, -1)
+    image_mixed = jnp.einsum(
+        "ihqp,iphd->iqhd", image_probs.astype(low), image_values, preferred_element_type=f32
+    )
+    image_mixed = image_mixed.astype(low).reshape(image_total, LAT * own_width)
+
+    slot_range = jnp.arange(image_total, dtype=jnp.int32)
+    live = slot_range % IMG_DEV < jnp.repeat(image_count[0], IMG_DEV)
+    block_count = group_rows // LAT
+    owner = (
+        (image_slot[0][None, :] == jnp.arange(block_count, dtype=jnp.int32)[:, None]) & live[None, :]
+    ).astype(low)
+    mixed_placed = dot32(owner, image_mixed).astype(low).reshape(group_rows, own_width)
+    taken = jnp.repeat((jnp.sum(owner.astype(f32), 1) > 0.5).astype(f32), LAT)[:, None]
+    taken_own = lax.dynamic_slice_in_dim(taken, seq_rank * row_count, row_count, 0)
+
+    def wide(vector):
+        return vector.astype(f32)[None, :]
+
+    def own_part(vector):
+        width = vector.shape[0] // PLANE
+        return lax.dynamic_slice_in_dim(vector, seq_rank * width, width, 0)
+
+    def begin(total, piece, views, outs):
+        text_view, taken_view, gain, shift = views
+        embed = total.astype(jnp.bfloat16).astype(jnp.float32)
+        mixed = jnp.where(taken_view[...] > 0.5, embed, text_view[...].astype(jnp.float32))
+        outs[0][...] = mixed
+        return norm_rows(mixed, gain[...], shift[...])[0].astype(jnp.bfloat16)
+
+    rows_wide = jax.ShapeDtypeStruct((row_count, model_width), f32)
+    (mixed_in, normed), hidden_blocks = exchange(
+        [
+            Stream(
+                mixed_placed,
+                image_out_own,
+                False,
+                (text[0], taken_own, wide(input_gain), wide(input_shift)),
+                (ROWS, ROWS, ALL, ALL),
+                ((rows_wide, ROWS),),
+                begin,
+                True,
+            )
+        ],
+        [PlaneWeights((up_weight, down_weight), (INWARD, OUTWARD))],
+        3,
+    )
+
+    segment_all = segment[0]
+    docs_count = 3 * (group_rows // min(SEQ_MAX, group_rows))
+    marks = (segment_all[:, None] == jnp.arange(docs_count, dtype=jnp.int32)[None, :]).astype(jnp.int32)
+    earlier_rows = jnp.cumsum(marks, 0) - marks
+    position = jnp.sum(earlier_rows * marks, 1).astype(f32)
+    cosine, sine_table, growth = xpos_factors(position, HEAD // 2)
+    row_index = jnp.arange(group_rows, dtype=jnp.int32)
+    allowed = (row_index[None, :] <= row_index[:, None]) & (segment_all[None, :] == segment_all[:, None])
+
+    cot_late, _ = lax.optimization_barrier((cotangent[0], normed))
+    cot_all = lax.all_gather(cot_late, SEQ, axis=0, tiled=True)
+    lin = dot32(normed, qkv_own)
+    query_rot = rotate(
+        lin[:, :own_width].reshape(group_rows, own_heads, HEAD), cosine, sine_table, growth
+    ).astype(low)
+    keys_rot = rotate(
+        lin[:, own_width : 2 * own_width].reshape(group_rows, own_heads, HEAD), cosine, sine_table, 1.0 / growth
+    ).astype(low)
+    values = lin[:, 2 * own_width :].astype(low).reshape(group_rows, own_heads, HEAD)
+    scores = jnp.einsum("qhd,khd->hqk", query_rot, keys_rot, preferred_element_type=f32) * score_scale
+    probs = jax.nn.softmax(jnp.where(allowed[None], scores, -1e30), -1)
+    attended = jnp.einsum("hqk,khd->qhd", probs.astype(low), values, preferred_element_type=f32)
+    attended = attended.reshape(group_rows, own_width)
+
+    def split_stats(parts, cid):
+        total = small_total(jnp.stack(parts), cid)
+        return [total[number][:, None] for number in range(len(parts))]
+
+    inner_sum, inner_square = split_stats((jnp.sum(attended, 1), jnp.sum(attended * attended, 1)), 4)
+    average = inner_sum / model_width
+    inner_factor = lax.rsqrt(inner_square / model_width - average * average + EPSILON)
+    inner_hat = (attended - average) * inner_factor
+    inner_gain_own = wide(own_part(inner_gain))
+    inner_low = (inner_hat * inner_gain_own + wide(own_part(inner_shift))).astype(low)
+
+    def middle_step(total, piece, views, outs):
+        mixed_view, gain, shift = views
+        middle = mixed_view[...] + total
+        outs[0][...] = middle
+        return norm_rows(middle, gain[...], shift[...])[0].astype(jnp.bfloat16)
+
+    (middle, lifted), hidden_own = exchange(
+        [
+            Stream(
+                inner_low,
+                out_own,
+                False,
+                (mixed_in, wide(middle_gain), wide(middle_shift)),
+                (ROWS, ALL, ALL),
+                ((rows_wide, ROWS),),
+                middle_step,
+                True,
+            )
+        ],
+        [CrossWeights(hidden_blocks, (INWARD, OUTWARD))],
+        5,
+    )
+    up_own, down_own = hidden_own[0].reshape(model_width, -1), hidden_own[1]
+    own_hidden = up_own.shape[1]
+
+    hidden_pre = dot32(lifted, up_own) + wide(own_part(up_bias))
+    activated, gelu_pull = jax.vjp(functools.partial(jax.nn.gelu, approximate=False), hidden_pre)
+    d_settled = dot32(cot_all, down_own.T)
+    hidden_gain_own = wide(own_part(hidden_gain))
+    scaled = d_settled * hidden_gain_own
+    sum_act, sum_square, sum_scaled, sum_cross = split_stats(
+        (
+            jnp.sum(activated, 1),
+            jnp.sum(activated * activated, 1),
+            jnp.sum(scaled, 1),
+            jnp.sum(scaled * activated, 1),
+        ),
+        6,
+    )
+    average = sum_act / FF
+    hidden_factor = lax.rsqrt(sum_square / FF - average * average + EPSILON)
+    settled_hat = (activated - average) * hidden_factor
+    settled = (settled_hat * hidden_gain_own + wide(own_part(hidden_shift))).astype(low)
+    mean_scaled = sum_scaled / FF
+    mean_cross = hidden_factor * (sum_cross / FF - average * mean_scaled)
+    d_activated = hidden_factor * (scaled - mean_scaled - settled_hat * mean_cross)
+    d_hidden = gelu_pull(d_activated)[0].astype(low)
+    hidden_gain_grad = jnp.sum(d_settled * settled_hat, 0)
+    hidden_shift_grad = jnp.sum(d_settled, 0)
+    up_bias_grad = jnp.sum(d_hidden.astype(f32), 0)
+    down_grad = dot32(settled.T, cot_all).astype(low)
+    up_grad = dot32(lifted.T, d_hidden).astype(low)
+
+    def blocks_in(grad):
+        return grad.reshape(PLANE, 2, -1, grad.shape[1])
+
+    def last_step(total, piece, views, outs):
+        outs[0][...] = (views[0][...] + total).astype(jnp.bfloat16)
+
+    vector_out = jax.ShapeDtypeStruct((1, model_width), f32)
+
+    def norm_back_step(total, piece, views, outs):
+        rows_view, carried_view, gain = views
+        rows_in = rows_view[...]
+        center = rows_in - jnp.mean(rows_in, -1, keepdims=True)
+        factor = lax.rsqrt(jnp.mean(center * center, -1, keepdims=True) + EPSILON)
+        normal = center * factor
+        grad = carried_view[...].astype(jnp.float32) + full_back(total, normal, factor, gain[...])
+        outs[0][...] = grad
+        if piece == 0:
+            outs[1][...] = jnp.zeros_like(outs[1])
+            outs[2][...] = jnp.zeros_like(outs[2])
+        outs[1][...] += jnp.sum(total * normal, 0, keepdims=True)
+        outs[2][...] += jnp.sum(total, 0, keepdims=True)
+        return grad.astype(jnp.bfloat16)
+
+    hidden_grads = (blocks_in(up_grad), down_grad)
+    (d_middle, middle_gain_grad, middle_shift_grad, d_branch), hidden_theirs = exchange(
+        [
+            Stream(
+                d_hidden,
+                up_own,
+                True,
+                (middle, cotangent[0], wide(middle_gain)),
+                (ROWS, ROWS, ALL),
+                ((rows_wide, ROWS), (vector_out, ALL), (vector_out, ALL)),
+                norm_back_step,
+                True,
+            )
+        ],
+        [CrossGrads(hidden_grads, (INWARD, OUTWARD))],
+        8,
+    )
+
+    out_grad = dot32(inner_low.T, d_branch).astype(low)
+    d_inner = dot32(d_branch, out_own.T)
+    inner_gain_grad = jnp.sum(d_inner * inner_hat, 0)
+    inner_shift_grad = jnp.sum(d_inner, 0)
+    scaled = d_inner * inner_gain_own
+    sum_scaled, sum_cross = split_stats((jnp.sum(scaled, 1), jnp.sum(scaled * inner_hat, 1)), 9)
+    d_attended = inner_factor * (scaled - sum_scaled / model_width - inner_hat * (sum_cross / model_width))
+    d_attended = d_attended.astype(low).reshape(group_rows, own_heads, HEAD)
+    delta = jnp.sum(d_attended.astype(f32) * attended.reshape(group_rows, own_heads, HEAD), -1).T
+    d_probs = jnp.einsum("qhd,khd->hqk", d_attended, values, preferred_element_type=f32)
+    d_scores = (probs * (d_probs - delta[..., None])).astype(low)
+    d_query = jnp.einsum("hqk,khd->qhd", d_scores, keys_rot, preferred_element_type=f32) * score_scale
+    d_key = jnp.einsum("hqk,qhd->khd", d_scores, query_rot, preferred_element_type=f32) * score_scale
+    d_value = jnp.einsum("hqk,qhd->khd", probs.astype(low), d_attended, preferred_element_type=f32)
+    d_lin = jnp.concatenate(
+        [
+            rotate_back(d_query, cosine, sine_table, growth).astype(low).reshape(group_rows, own_width),
+            rotate_back(d_key, cosine, sine_table, 1.0 / growth).astype(low).reshape(group_rows, own_width),
+            d_value.astype(low).reshape(group_rows, own_width),
+        ],
+        1,
+    )
+    lin_grad = dot32(normed.T, d_lin).astype(low)
+    layer_grads = (
+        blocks_in(lin_grad[:, :own_width]),
+        blocks_in(lin_grad[:, own_width : 2 * own_width]),
+        blocks_in(lin_grad[:, 2 * own_width :]),
+        out_grad,
+    )
+    layer_sides = (INWARD, INWARD, INWARD, OUTWARD)
+    (d_mixed, input_gain_grad, input_shift_grad, d_rows), (result,), layer_theirs = exchange(
+        [
+            Stream(
+                d_lin,
+                qkv_own,
+                True,
+                (mixed_in, d_middle, wide(input_gain)),
+                (ROWS, ROWS, ALL),
+                ((rows_wide, ROWS), (vector_out, ALL), (vector_out, ALL)),
+                norm_back_step,
+                True,
+            ),
+            Stream(
+                settled,
+                down_own,
+                False,
+                (middle,),
+                (ROWS,),
+                ((jax.ShapeDtypeStruct((row_count, model_width), low), ROWS),),
+                last_step,
+                False,
+            ),
+        ],
+        [CrossGrads(layer_grads, layer_sides)],
+        10,
+    )
+    text_grad = jnp.where(taken_own > 0.5, 0.0, d_mixed)
+
+    image_out_grad = dot32(mixed_placed.T, d_rows).astype(low)
+    d_mixed_rows = dot32(d_rows, image_out_own.T).astype(low)
+    d_image_mixed = dot32(owner.T, d_mixed_rows.reshape(block_count, LAT * own_width)).astype(low)
+    d_image_mixed = d_image_mixed.reshape(image_total, LAT, own_heads, HEAD)
+    d_image_probs = jnp.einsum("iqhd,iphd->ihqp", d_image_mixed, image_values, preferred_element_type=f32)
+    d_image_scores = image_probs * (
+        d_image_probs - jnp.sum(image_probs * d_image_probs, -1, keepdims=True)
+    )
+    d_image_scores = d_image_scores.astype(low)
+    d_probe = jnp.einsum("ihqp,iphd->qhd", d_image_scores, image_keys, preferred_element_type=f32) * score_scale
+    d_image_keys = (
+        jnp.einsum("ihqp,qhd->iphd", d_image_scores, probe, preferred_element_type=f32) * score_scale
+    ).astype(low)
+    d_image_values = jnp.einsum(
+        "ihqp,iqhd->iphd", image_probs.astype(low), d_image_mixed, preferred_element_type=f32
+    ).astype(low)
+    picture_rows = image_total * PATCH
+    image_grad = dot32(
+        pictures.T,
+        jnp.concatenate(
+            [d_image_keys.reshape(picture_rows, own_width), d_image_values.reshape(picture_rows, own_width)], 1
+        ),
+    ).astype(low)
+
+    own_vectors = jnp.concatenate(
+        [inner_gain_grad, inner_shift_grad, up_bias_grad, hidden_gain_grad, hidden_shift_grad]
+    )
+    row_vectors = jnp.concatenate(
+        [input_gain_grad[0], input_shift_grad[0], middle_gain_grad[0], middle_shift_grad[0]]
+    )
+    packed = jnp.concatenate([row_vectors, own_vectors]).reshape(-1, LANES)
+    spare = -packed.shape[0] % 8
+    packed = jnp.concatenate([d_probe.reshape(LAT, own_width), jnp.pad(packed, ((0, spare), (0, 0)))], 0)
+    image_grads = (blocks_in(image_grad[:, :own_width]), blocks_in(image_grad[:, own_width:]), image_out_grad)
+    owned, (spread, resample_query_grad, latent_grad) = finale(
+        list(zip(hidden_grads + layer_grads, hidden_theirs + layer_theirs)),
+        image_grads,
+        (INWARD, OUTWARD) + layer_sides,
+        (INWARD, INWARD, OUTWARD),
+        packed,
+        latents.astype(f32).T,
+        resample_query.astype(f32),
+        12,
+    )
+    up_sum, down_sum, query_sum, key_sum, value_sum, out_sum, image_key_sum, image_value_sum, image_out_sum = widened(owned)
+    spread = spread.reshape(PLANE, -1)
+    first = LAT * own_width
+    row_sums = spread[:, first : first + row_vectors.shape[0]].sum(0).reshape(4, model_width)
+    own_sums = spread[:, first + row_vectors.shape[0] :]
+
+    def joined(start, width):
+        return own_sums[:, start : start + width].reshape(-1)
+
+    inner_gain_sum = joined(0, own_width)
+    inner_shift_sum = joined(own_width, own_width)
+    up_bias_sum = joined(2 * own_width, own_hidden)
+    hidden_gain_sum = joined(2 * own_width + own_hidden, own_hidden)
+    hidden_shift_sum = joined(2 * own_width + 2 * own_hidden, own_hidden)
+
+    return (
+        result[None],
+        text_grad[None],
+        row_sums[0],
+        row_sums[1],
+        query_sum,
+        key_sum,
+        value_sum,
+        inner_gain_sum,
+        inner_shift_sum,
+        out_sum,
+        row_sums[2],
+        row_sums[3],
+        up_sum,
+        up_bias_sum,
+        hidden_gain_sum,
+        hidden_shift_sum,
+        down_sum,
+        latent_grad,
+        resample_query_grad,
+        image_key_sum,
+        image_value_sum,
+        image_out_sum,
+    )
+
+
 def solution(mesh):
     placed = (
-        P("img", "seq", None),
-        P("img", None),
-        P("img", "seq", None, None),
-        P("img", None),
-        P("img", None),
-        P("img", "seq", None),
+        P(IMG, SEQ, None),
+        P(IMG, None),
+        P(IMG, SEQ, None, None),
+        P(IMG, None),
+        P(IMG, None),
+        P(IMG, SEQ, None),
         P(),
         P(),
-        P(("seq", "img"), "tp"),
-        P(("seq", "img"), "tp"),
-        P(("seq", "img"), "tp"),
-        P("tp"),
-        P("tp"),
-        P("tp", ("seq", "img")),
+        P((SEQ, IMG), TP),
+        P((SEQ, IMG), TP),
+        P((SEQ, IMG), TP),
+        P(TP),
+        P(TP),
+        P(TP, (SEQ, IMG)),
         P(),
         P(),
-        P(("seq", "img"), "tp"),
-        P("tp"),
-        P("tp"),
-        P("tp"),
-        P("tp", ("seq", "img")),
-        P(None, ("seq", "img")),
-        P(("seq", "img"), "tp"),
-        P(("seq", "img"), "tp"),
-        P(("seq", "img"), "tp"),
-        P("tp", ("seq", "img")),
+        P((SEQ, IMG), TP),
+        P(TP),
+        P(TP),
+        P(TP),
+        P(TP, (SEQ, IMG)),
+        P(None, (SEQ, IMG)),
+        P((SEQ, IMG), TP),
+        P((SEQ, IMG), TP),
+        P((SEQ, IMG), TP),
+        P(TP, (SEQ, IMG)),
     )
     return jax.shard_map(
-        on_device,
+        on_device if narrow_heads(mesh) else on_plane,
         mesh=mesh,
         in_specs=placed,
         out_specs=(
-            P("img", "seq", None),
-            P("img", "seq", None),
+            P(IMG, SEQ, None),
+            P(IMG, SEQ, None),
             P(),
             P(),
-            P(("seq", "img"), "tp"),
-            P(("seq", "img"), "tp"),
-            P(("seq", "img"), "tp"),
-            P("tp"),
-            P("tp"),
-            P("tp", ("seq", "img")),
+            P((SEQ, IMG), TP),
+            P((SEQ, IMG), TP),
+            P((SEQ, IMG), TP),
+            P(TP),
+            P(TP),
+            P(TP, (SEQ, IMG)),
             P(),
             P(),
-            P(("seq", "img"), "tp"),
-            P("tp"),
-            P("tp"),
-            P("tp"),
-            P("tp", ("seq", "img")),
-            P(None, ("seq", "img")),
-            P(("seq", "img"), "tp"),
-            P(("seq", "img"), "tp"),
-            P(("seq", "img"), "tp"),
-            P("tp", ("seq", "img")),
+            P((SEQ, IMG), TP),
+            P(TP),
+            P(TP),
+            P(TP),
+            P(TP, (SEQ, IMG)),
+            P(None, (SEQ, IMG)),
+            P((SEQ, IMG), TP),
+            P((SEQ, IMG), TP),
+            P((SEQ, IMG), TP),
+            P(TP, (SEQ, IMG)),
         ),
         check_vma=False,
     )

time: 3990 us -> 653 us (0.16)
  waiting for transfers between devices: 3570 us -> 0.02 us
  Pallas kernels: 0 us -> 470 us
  matrix products: 211 us -> 89.4 us
  blocking collectives: 58.5 us -> 0 us
  local copies, waits for them, and re-layouts: 83.9 us -> 30.3 us
    reduce_scatter x9 -> x0, waiting for transfers between devices: 2420 us -> none  [the longest x1 686 us: on_device(): lax.psum_scatter(down_grad, ('seq', 'img'), scatter_dimension=1, tiled=True)]
    all_gather x14 -> x1, waiting for transfers between devices: 570 us -> 0.01 us  [on_plane(): cot_all = lax.all_gather(cot_late, SEQ, axis=0, tiled=True)]
    pallas_call x0 -> x11, Pallas kernels: none -> 470 us  [the longest x4 293 us: exchange(): pl.pallas_call(kernel, out_shape=tuple(out_shapes), in_specs=in_specs, ou...]
    psum x6 -> x0, waiting for transfers between devices: 316 us -> none  [the longest x5 210 us: tp_total(): lax.psum(shortened(inputs), 'tp')]
    unnamed x37 -> x1, waiting for transfers between devices: 257 us -> 0.02 us
    dot_general x41 -> x26, matrix products: 209 us -> 81.9 us  [the longest x16 65.6 us: dot32(): return jnp.dot(left, right, preferred_element_type=jnp.float32)]
  transfers between devices with their start and end apart: 33 -> 1, of which waited for: 33 -> 0; matrix products, arithmetic and copies ran while one was open for 5% -> 6% of each run, Pallas kernels for 0% -> 13%
where the time goes in v1:
time: 653 us; the launch traced here: 642 us
  Pallas kernels  470 us (72%)
  matrix products  89.4 us (14%)
  other arithmetic  37.2 us (6%)
  local copies, waits for them, and re-layouts  30.3 us (5%)
  between operations  15.5 us (2%)
    pallas_call x4, Pallas kernels, exchange(): pl.pallas_call(kernel, out_shape=tuple(out_shapes), in_specs=in_specs, ou...  293 us
    pallas_call x1, Pallas kernels, intake(): pl.pallas_call(kernel, out_shape=tuple(outs), in_specs=[ANYWHERE] * (n_ro...  72.3 us
    dot_general x16, matrix products, dot32(): return jnp.dot(left, right, preferred_element_type=jnp.float32)  65.6 us
    pallas_call x1, Pallas kernels, finale(): pl.pallas_call(kernel, out_shape=tuple(outs + small_shapes), in_specs=[ON...  56 us
    pallas_call x3, Pallas kernels, small_total(): pl.pallas_call(kernel, out_shape=jax.ShapeDtypeStruct(values.shape, value...  33.8 us
    unnamed x157, local copies, waits for them, and re-layouts  13.2 us
  transfers between devices with their start and end apart: 1, of which 0 were waited for; matrix products, arithmetic and copies ran while one was open for 6% of the time, Pallas kernels for 13%

profile of v1, /device:TPU:0, one launch (start us, length us, event | category | flops | bytes accessed | tf_op | source)
XLA Modules:
  0.0 642.1 jit_solution(11376371085260266205)
XLA Ops:
  7.2 72.3 %shard_map.417 = (bf16[4096,1024]{1,0:T(8,128)(2,1)}, bf16[1024,128]{1,0:T(8,128)(2,1)}, bf16[1024,128]{1,0:T(8,128)(2,1)}, bf16[2048,128]{1,0:T(8,128)(2,1)}, b...) custom-call(bf16[512,1024]{1,0:T(8,128)(2,1)} %bitcast.242, ...), custom_call_target="tpu_custom_call" | custom-call | tf_op jit(solution)/shard_map/pallas_call | solution.py:830
  79.5 5.7 convolution_convert_fusion.2
  87.8 9.2 %shard_map.418 = bf16[8,2,64,128]{3,2,1,0:T(8,128)(2,1)} custom-call(bf16[64,128]{1,0:T(8,128)(2,1)} %in_ref.1), custom_call_target="tpu_custom_call" | custom-call | tf_op jit(solution)/shard_map/pallas_call | solution.py:1448
  99.8 5.7 convolution_convert_fusion.3
  115.4 69.7 %shard_map.419 = (f32[128,2048]{1,0:T(8,128)}, bf16[1024,2048]{1,0:T(8,128)(2,1)}, bf16[8,128,512]{2,1,0:T(8,128)(2,1)}, bf16[8,512,128]{2,1,0:T(8,128)(2,1)}) custom-call(bf16[1024,128]{1,0:T(8,128)(2,1)} %reshape.502.refs_0_, bf16[128,2048]{1,0:T(8,128)(2,1)} %get-tuple-element.80.refs_1_, bf16[128,2048]{1,0:T(8,128)(2,1)} %bitcast.245, ...), custom_call_target="tpu_custom_call" | custom-call | tf_op jit(solution)/shard_map/pallas_call | solution.py:1187
  190.0 4.6 fusion.88
  198.5 6.6 %fusion.86 = (f32[2,1024]{1,0:T(2,128)S(1)}, f32[2,1024,1024]{1,2,0:T(8,128)}) fusion(pred[1024,1024]{0,1:T(8,128)(4,1)} %fusion.5, bf16[1024,2,64]{0,2,1:T(8,128)(2,1)S(1)} %get-tuple-element.206, bf16[1024,2,64]{0,2,1:T(8,128)(2,1)S(1)} %get-tuple-element.205), kind=kOutput, calls=%fused_computation.200 | convolution fusion | flops 276825088 | bytes 9969664 | tf_op jit(solution)/shard_map/sub | solution.py:1604
  205.1 4.6 fusion.7
  212.4 14.0 %shard_map.420 = f32[2,1024]{1,0:T(2,128)} custom-call(f32[2,1024]{1,0:T(2,128)} %pad_maximum_fusion.4.in_ref), custom_call_target="tpu_custom_call" | custom-call | tf_op jit(solution)/shard_map/pallas_call | solution.py:1412
  230.5 72.6 %shard_map.421 = (f32[128,2048]{1,0:T(8,128)}, bf16[1024,2048]{1,0:T(8,128)(2,1)}, bf16[8,2,128,512]{3,2,1,0:T(8,128)(2,1)}, bf16[512,2048]{1,0:T(8,128)(2,1)}) custom-call(bf16[1024,128]{1,0:T(8,128)(2,1)} %add_convert_fusion.2.refs_0_, bf16[128,2048]{1,0:T(8,128)(2,1)} %get-tuple-element.85.refs_1_, f32[128,2048]{1,0:T(8,128)} %get-tuple-element.86.refs_2_, ...), custom_call_target="tpu_custom_call" | custom-call | tf_op jit(solution)/shard_map/pallas_call | solution.py:1187
  306.6 6.5 %fusion.89 = f32[1024,512]{1,0:T(8,128)} fusion(bf16[1024,2048]{1,0:T(8,128)(2,1)} %get-tuple-element.89, bf16[2048,512]{1,0:T(8,128)(2,1)} %bitcast.223), kind=kOutput, calls=%fused_computation.203 | convolution fusion | flops 2147483648 | bytes 8388608 | tf_op jit(solution)/shard_map/dot_general | solution.py:1468
  313.1 11.3 %multiply_reduce_fusion.4 = (f32[1024]{0:T(1024)S(1)}, f32[1024]{0:T(1024)S(1)}, f32[1024]{0:T(1024)S(1)}, f32[1024]{0:T(1024)S(1)}, f32[1024,512]{1,0:T(8,128)}, /*index=5*/f32[1024,512]{1,0:T(8,128)}, f32[1024,512]{1,0:T(8,128)}) fusion(f32[512]{0:T(512)} %get-tuple-element.202, f32[1024,512]{1,0:T(8,128)} %fusion.89, ...), kind=kOutput, calls=%fused_computation.57 | convolution fusion | flops 2185228288 | bytes 14700544 | tf_op jit(solution)/shard_map/dot_general | solution.py:1468
  325.1 10.5 %shard_map.422 = f32[4,1024]{1,0:T(4,128)} custom-call(f32[4,1024]{1,0:T(4,128)} %pad_maximum_fusion.3.in_ref), custom_call_target="tpu_custom_call" | custom-call | tf_op jit(solution)/shard_map/pallas_call | solution.py:1412
  336.5 5.4 fusion.75
  341.9 3.8 convolution_convert_fusion.5
  345.7 3.8 convolution_convert_fusion.4.refs_6_.refs_1_
  349.4 70.7 %shard_map.423 = (f32[128,2048]{1,0:T(8,128)}, f32[1,2048]{1,0:T(1,128)}, f32[1,2048]{1,0:T(1,128)}, bf16[1024,2048]{1,0:T(8,128)(2,1)}, bf16[8,128,512]{2,1,0:T(8,128)(2,1)}, /*index=5*/bf16[8,512,128]{2,1,0:T(8,128)(2,1)}) custom-call(bf16[1024,512]{1,0:T(8,128)(2,1)} %copy-done.8, bf16[2048,512]{1,0:T(8,128)(2,1)} %bitcast.224, ...), custom_call_target="tpu_custom_call" | custom-call | tf_op jit(solution)/shard_map/pallas_call | solution.py:1187
  420.2 3.9 convolution_convert_fusion.8.refs_11_.refs_5_
  424.0 3.0 fusion.87
  427.1 2.0 copy.157
  429.1 2.2 multiply_reduce_fusion.5
  431.9 9.3 %shard_map.424 = f32[2,1024]{1,0:T(2,128)} custom-call(f32[2,1024]{1,0:T(2,128)} %pad_maximum_fusion.5.in_ref), custom_call_target="tpu_custom_call" | custom-call | tf_op jit(solution)/shard_map/pallas_call | solution.py:1412
  442.0 2.4 multiply_convert_fusion.3
  445.5 4.3 convolution_convert_fusion.11
  449.9 4.7 multiply_convert_fusion
  458.1 4.6 convolution_convert_fusion.6
  464.9 80.1 %shard_map.425 = (f32[128,2048]{1,0:T(8,128)}, f32[1,2048]{1,0:T(1,128)}, f32[1,2048]{1,0:T(1,128)}, bf16[1024,2048]{1,0:T(8,128)(2,1)}, bf16[128,2048]{1,0:T(8,...) custom-call(bf16[1024,384]{1,0:T(8,128)(2,1)} %pad_maximum_fusion.re, ...), custom_call_target="tpu_custom_call" | custom-call | tf_op jit(solution)/shard_map/pallas_call | solution.py:1187
  545.0 3.6 convolution_convert_fusion.12
  551.2 2.2 multiply_reduce_fusion.1
  558.6 5.8 fusion.25
  566.1 56.0 %shard_map.426 = (bf16[128,4096]{1,0:T(8,128)(2,1)}, bf16[4096,128]{1,0:T(8,128)(2,1)}, bf16[128,1024]{1,0:T(8,128)(2,1)}, bf16[128,1024]{1,0:T(8,128)(2,1)}, bf...) custom-call(bf16[8,2,128,512]{3,2,1,0:T(8,128)(2,1)} %bitcast.209, ...), custom_call_target="tpu_custom_call" | custom-call | tf_op jit(solution)/shard_map/pallas_call | solution.py:1346
  627.7 5.2 shard_map.427
  (254 shorter events, 60.2 us)
Async XLA Ops:
  7.2 306.0 %all-gather.2.cloned.1.call-start = ((), (), s32[]{:S(2)}) async-start(), calls=%async_computation | async-start | bytes 4718592 | tf_op jit(solution)/shard_map/all_gather | solution.py:1594
  86.3 13.5 %copy-start.66 = (bf16[1024,128]{1,0:T(8,128)(2,1)S(1)}, bf16[1024,128]{1,0:T(8,128)(2,1)}, u32[]{:S(2)}) copy-start(bf16[1024,128]{1,0:T(8,128)(2,1)} %get-tuple-element.77) | copy-start | bytes 786436
  87.8 19.5 %copy-start.1 = (bf16[16,256,2,64]{1,3,0,2:T(8,128)(2,1)}, bf16[16,256,2,64]{1,3,0,2:T(8,128)(2,1)S(1)}, u32[]{:S(2)}) copy-start(bf16[16,256,2,64]{1,3,0,2:T(8,128)(2,1)S(1)} %copy.148) | copy-start | bytes 3145732
  99.8 7.5 %copy-start.35 = (bf16[64,2,64]{2,1,0:T(2,128)(2,1)}, bf16[64,2,64]{2,1,0:T(2,128)(2,1)S(1)}, u32[]{:S(2)}) copy-start(bf16[64,2,64]{2,1,0:T(2,128)(2,1)S(1)} %reshape.500) | copy-start | bytes 49156
  113.0 72.2 %copy-start.26 = (bf16[128,1024]{1,0:T(8,128)(2,1)S(1)}, bf16[128,1024]{1,0:T(8,128)(2,1)}, u32[]{:S(2)}) copy-start(bf16[128,1024]{1,0:T(8,128)(2,1)} %refs_3_.1) | copy-start | bytes 786436
  115.4 70.6 %copy-start.41 = (bf16[64,128]{1,0:T(8,128)(2,1)S(1)}, bf16[64,128]{1,0:T(8,128)(2,1)}, u32[]{:S(2)}) copy-start(bf16[64,128]{1,0:T(8,128)(2,1)} %in_ref.1) | copy-start | bytes 49156
  115.4 71.4 %copy-start.39 = (s32[1,1024]{1,0:T(1,128)S(1)}, s32[1,1024]{1,0:T(1,128)}, u32[]{:S(2)}) copy-start(s32[1,1024]{1,0:T(1,128)} %param.27) | copy-start | bytes 12292
  194.7 15.1 %copy-start.10 = (bf16[1024,128]{0,1:T(8,128)(2,1)}, bf16[1024,128]{0,1:T(8,128)(2,1)S(1)}, u32[]{:S(2)}) copy-start(bf16[1024,128]{0,1:T(8,128)(2,1)S(1)} %slice.214) | copy-start | bytes 786436
  196.9 8.2 %copy-start.12 = (bf16[1024,2,64]{0,2,1:T(8,128)(2,1)}, bf16[1024,2,64]{0,2,1:T(8,128)(2,1)S(1)}, u32[]{:S(2)}) copy-start(bf16[1024,2,64]{0,2,1:T(8,128)(2,1)S(1)} %get-tuple-element.205) | copy-start | bytes 786436
  196.9 8.2 %copy-start.27 = (bf16[1024,2,64]{0,2,1:T(8,128)(2,1)}, bf16[1024,2,64]{0,2,1:T(8,128)(2,1)S(1)}, u32[]{:S(2)}) copy-start(bf16[1024,2,64]{0,2,1:T(8,128)(2,1)S(1)} %get-tuple-element.206) | copy-start | bytes 786436
  209.8 16.9 %copy-start.55 = (bf16[2048]{0:T(1024)(128)(2,1)S(1)}, bf16[2048]{0:T(1024)(128)(2,1)}, u32[]{:S(2)}) copy-start(bf16[2048]{0:T(1024)(128)(2,1)} %param.40) | copy-start | bytes 12292
  209.8 17.5 %copy-start.56 = (bf16[2048]{0:T(1024)(128)(2,1)S(1)}, bf16[2048]{0:T(1024)(128)(2,1)}, u32[]{:S(2)}) copy-start(bf16[2048]{0:T(1024)(128)(2,1)} %param.41) | copy-start | bytes 12292
  228.6 74.5 %copy-start.43 = (f32[128]{0:T(128)}, f32[128]{0:T(128)S(1)}, u32[]{:S(2)}) copy-start(f32[128]{0:T(128)S(1)} %get-tuple-element.204) | copy-start | bytes 1540
  229.4 73.7 %copy-start.37 = (f32[1,1024]{1,0:T(1,128)}, f32[1,1024]{1,0:T(1,128)S(1)}, u32[]{:S(2)}) copy-start(f32[1,1024]{1,0:T(1,128)S(1)} %get-tuple-element.185) | copy-start | bytes 12292
  229.4 73.7 %copy-start.38 = (f32[1024]{0:T(1024)}, f32[1024]{0:T(1024)S(1)}, u32[]{:S(2)}) copy-start(f32[1024]{0:T(1024)S(1)} %add_rsqrt_fusion.1) | copy-start | bytes 12292
  230.5 75.4 %copy-start.20 = (f32[1024,1,32]{0,2,1:T(8,128)S(1)}, f32[1024,1,32]{0,2,1:T(8,128)}, u32[]{:S(2)}) copy-start(f32[1024,1,32]{0,2,1:T(8,128)} %copy-done.19) | copy-start | bytes 393220
  230.5 75.4 %copy-start.22 = (f32[1024,1,32]{0,2,1:T(8,128)S(1)}, f32[1024,1,32]{0,2,1:T(8,128)}, u32[]{:S(2)}) copy-start(f32[1024,1,32]{0,2,1:T(8,128)} %copy-done.21) | copy-start | bytes 393220
  336.5 5.4 copy-start.65
  349.4 70.7 %copy-start.16 = (bf16[1024,128]{1,0:T(8,128)(2,1)S(1)}, bf16[1024,128]{1,0:T(8,128)(2,1)}, u32[]{:S(2)}) copy-start(bf16[1024,128]{1,0:T(8,128)(2,1)} %add_convert_fusion.2.refs_0_) | copy-start | bytes 786436
  464.9 80.1 %copy-start.34 = (bf16[128,2048]{1,0:T(8,128)(2,1)S(1)}, bf16[128,2048]{1,0:T(8,128)(2,1)}, u32[]{:S(2)}) copy-start(bf16[128,2048]{1,0:T(8,128)(2,1)} %get-tuple-element.80.refs_1_) | copy-start | bytes 1572868
  558.5 6.8 %copy-start.46 = (f32[1,2048]{1,0:T(1,128)S(1)}, f32[1,2048]{1,0:T(1,128)}, u32[]{:S(2)}) copy-start(f32[1,2048]{1,0:T(1,128)} %get-tuple-element.106) | copy-start | bytes 24580
  558.5 6.8 %copy-start.45 = (f32[1,2048]{1,0:T(1,128)S(1)}, f32[1,2048]{1,0:T(1,128)}, u32[]{:S(2)}) copy-start(f32[1,2048]{1,0:T(1,128)} %get-tuple-element.107) | copy-start | bytes 24580
  558.5 6.8 %copy-start.44 = (f32[1,2048]{1,0:T(1,128)S(1)}, f32[1,2048]{1,0:T(1,128)}, u32[]{:S(2)}) copy-start(f32[1,2048]{1,0:T(1,128)} %get-tuple-element.108) | copy-start | bytes 24580
  558.5 6.8 %copy-start.62 = (f32[128]{0:T(128)S(1)}, f32[128]{0:T(128)}, u32[]{:S(2)}) copy-start(f32[128]{0:T(128)} %get-tuple-element.136) | copy-start | bytes 1540
  558.5 6.8 %copy-start.67 = (f32[128]{0:T(128)S(1)}, f32[128]{0:T(128)}, u32[]{:S(2)}) copy-start(f32[128]{0:T(128)} %get-tuple-element.199) | copy-start | bytes 1540
  558.6 6.8 %copy-start.52 = (f32[512]{0:T(512)S(1)}, f32[512]{0:T(512)}, u32[]{:S(2)}) copy-start(f32[512]{0:T(512)} %get-tuple-element.145) | copy-start | bytes 6148
  558.6 6.8 %copy-start.51 = (f32[512]{0:T(512)S(1)}, f32[512]{0:T(512)}, u32[]{:S(2)}) copy-start(f32[512]{0:T(512)} %get-tuple-element.135) | copy-start | bytes 6148
  558.6 6.8 %copy-start.50 = (f32[512]{0:T(512)S(1)}, f32[512]{0:T(512)}, u32[]{:S(2)}) copy-start(f32[512]{0:T(512)} %get-tuple-element.134) | copy-start | bytes 6148
  566.1 60.5 %copy-start.57 = (pred[128]{0:T(512)(128)(4,1)S(1)}, pred[128]{0:T(512)(128)(4,1)}, u32[]{:S(2)}) copy-start(pred[128]{0:T(512)(128)(4,1)} %get-tuple-element.141) | copy-start | bytes 388
  627.7 5.2 copy-start.30
  627.7 6.0 copy-start.42
  627.7 6.6 %copy-start.33 = (f32[128,1024]{1,0:T(8,128)S(1)}, f32[128,1024]{1,0:T(8,128)}, u32[]{:S(2)}) copy-start(f32[128,1024]{1,0:T(8,128)} %get-tuple-element.249) | copy-start | bytes 1572868
  (37 other events, 96.2 us)
Sparse Core Ops, SparseCore 0:
  185.3 38.8 all-gather.1

commit v2 on v1

--- a/solution.py
+++ b/solution.py
@@ -581,7 +581,7 @@
 PLANE = 8
 VMEM_BYTES = 60 * 1024 * 1024
 PIECES = 4
-FRONT, BACK, ALL, ROWS, INWARD, OUTWARD = range(6)
+FRONT, BACK, ALL, ROWS, INWARD, OUTWARD, SHARED = range(7)
 
 
 def narrow_heads(mesh):
@@ -704,6 +704,8 @@
 
 
 def weight_blocks(weight, side):
+    if side == SHARED:
+        return weight.shape
     if side == INWARD:
         return (weight.shape[0], weight.shape[1] // PLANE)
     return (weight.shape[0] // PLANE, weight.shape[1])
@@ -730,6 +732,8 @@
             return out.at[:, pl.ds(pl.multiple_of(number * shape[1], shape[1]), shape[1])]
 
         def block_of(weight, side, shape, to_seq):
+            if side == SHARED:
+                return weight
             if side == INWARD:
                 return weight.at[:, pl.ds(pl.multiple_of(to_seq * shape[1], shape[1]), shape[1])]
             return weight.at[pl.ds(pl.multiple_of(to_seq * shape[0], shape[0]), shape[0])]
@@ -967,11 +971,11 @@
 
 
 class Stream:
-    def __init__(self, left, right, across, row_inputs, row_kinds, row_outs, row_function, gather):
-        self.inputs = [left, right] + list(row_inputs)
+    def __init__(self, rows_all, left, right, across, row_inputs, row_kinds, row_outs, row_function, gather):
+        self.own_left = left is not None
+        self.inputs = ([left] if self.own_left else []) + [right] + list(row_inputs)
         self.across, self.row_kinds, self.row_outs = across, row_kinds, row_outs
         self.row_function, self.gather = row_function, gather
-        rows_all = left.shape[0]
         width = right.shape[0] if across else right.shape[1]
         self.width, self.block, self.pieces = width, rows_all // PLANE, PIECES
         self.count = self.block // self.pieces
@@ -1010,7 +1014,9 @@
 
     def bind(self, here, ins, outs, scratch):
         self.here = here
-        self.left, self.right, self.ins = ins[0], ins[1], ins[2:]
+        if self.own_left:
+            self.left, ins = ins[0], ins[1:]
+        self.right, self.ins = ins[0], ins[1:]
         self.outs = outs
         (self.away, self.core_in, self.near, self.from_xd, self.from_yd, self.from_x, self.from_y) = scratch[:7]
         (self.mine, self.theirs, self.low, self.c_send, self.c_recv) = scratch[7:12]
@@ -1142,8 +1148,266 @@
             made.wait_send()
 
 
-def exchange(streams, riders, cid):
-    parts = list(streams) + list(riders)
+class Front(Rider):
+    def total_scratch(self, count, rows):
+        dma = pltpu.SemaphoreType.DMA
+        return [
+            pltpu.VMEM((PLANE - 1, count, rows), jnp.float32),
+            pltpu.VMEM((count, rows), jnp.float32),
+            pltpu.VMEM((count, rows), jnp.float32),
+            pltpu.VMEM((count, rows), jnp.float32),
+            dma((PLANE,)),
+            dma((PLANE,)),
+        ]
+
+    def peers(self, here):
+        return [here.at(lax.rem(here.seq + step, PLANE)) for step in range(1, PLANE)]
+
+    def small_sum(self, scratch):
+        here, (plane, own, mine, theirs, send, recv) = self.here, scratch
+        made = []
+        for step, peer in enumerate(self.peers(here)):
+            copy = remote(own, plane.at[step], send.at[step], recv.at[step], peer)
+            copy.start()
+            made.append(copy)
+        total = own[...]
+        for step, copy in enumerate(made):
+            copy.wait_recv()
+            total = total + plane[step]
+        mine[...] = total
+        last = remote(mine, theirs, send.at[PLANE - 1], recv.at[PLANE - 1], here.tp_peer)
+        last.start()
+        last.wait()
+        for copy in made:
+            copy.wait_send()
+        total = mine[...] + theirs[...]
+        count, rows = total.shape
+        return jnp.concatenate([total, jnp.zeros((8 - count, rows), jnp.float32)], 0).T
+
+
+class InnerFront(Front):
+    def __init__(self, attended, sums, gain, shift, full_width):
+        self.inputs = [attended, sums, gain, shift]
+        self.full_width = full_width
+        rows, width = attended.shape
+        self.out_shapes = [
+            jax.ShapeDtypeStruct((rows, width), jnp.bfloat16),
+            jax.ShapeDtypeStruct((rows, width), jnp.float32),
+            jax.ShapeDtypeStruct((rows, width), jnp.float32),
+        ]
+        self.scratch = self.total_scratch(sums.shape[0], rows)
+
+    def run(self):
+        attended, sums, gain, shift = self.ins
+        low, hat, factor_out = self.outs
+        self.held[1][...] = sums[...]
+        total = self.small_sum(self.held)
+        average = total[:, 0:1] / self.full_width
+        factor = lax.rsqrt(total[:, 1:2] / self.full_width - average * average + EPSILON)
+        normal = (attended[...] - average) * factor
+        hat[...] = normal
+        factor_out[...] = jnp.broadcast_to(factor, normal.shape)
+        low[...] = (normal * gain[...] + shift[...]).astype(jnp.bfloat16)
+        return low
+
+
+class GradFront(Front):
+    def grads(self, products):
+        here = self.here
+        for seq in range(PLANE):
+            for product in products:
+                self.launches.append(functools.partial(self.part, product, seq))
+
+    def part(self, product, seq):
+        left, right, outs, side, theirs, send, recv = product
+        here = self.here
+        span = (left.shape[1] if side == INWARD else right.shape[1]) // PLANE
+        at = slice(seq * span, (seq + 1) * span)
+        contract = (((0,), (0,)), ((), ()))
+        if side == INWARD:
+            made = lax.dot_general(left[:, at], right[...], contract, preferred_element_type=jnp.float32)
+        else:
+            made = lax.dot_general(left[...], right[:, at], contract, preferred_element_type=jnp.float32)
+        made = made.astype(jnp.bfloat16)
+        half = span // 2
+        for number, out in enumerate(outs):
+            if side == INWARD:
+                width = out.shape[3]
+                piece = made[:, number * width : (number + 1) * width]
+                out[seq, 0], out[seq, 1] = piece[:half], piece[half:]
+                src = out.at[seq, 1 - here.img]
+            else:
+                out[:, at] = made
+                src = out.at[:, pl.ds(pl.multiple_of((seq * 2 + 1 - here.img) * half, half), half)]
+            copy = remote(
+                src, theirs[number].at[seq], send.at[number, seq], recv.at[number, seq], here.img_peer
+            )
+            copy.start()
+            self.sent.append(copy)
+            self.due.append((theirs[number].at[seq], send.at[number, seq], recv.at[number, seq]))
+
+
+def grad_shapes(model_width, rows, side):
+    span = model_width // PLANE
+    if side == INWARD:
+        shapes = [(PLANE, 2, span // 2, rows), (PLANE, span // 2, rows)]
+    else:
+        shapes = [(rows, model_width), (PLANE, rows, span // 2)]
+    return [jax.ShapeDtypeStruct(shape, jnp.bfloat16) for shape in shapes]
+
+
+class HiddenFront(GradFront):
+    def __init__(self, activated, slope, d_settled, sums, gain, shift, lifted, cotangent_all, full_width):
+        self.inputs = [activated, slope, d_settled, sums, gain, shift, lifted, cotangent_all]
+        self.full_width = full_width
+        rows, width = activated.shape
+        model_width = lifted.shape[1]
+        low_shape = jax.ShapeDtypeStruct((rows, width), jnp.bfloat16)
+        up, up_theirs = grad_shapes(model_width, width, INWARD)
+        down, down_theirs = grad_shapes(model_width, width, OUTWARD)
+        self.out_shapes = [
+            low_shape,
+            low_shape,
+            jax.ShapeDtypeStruct((8, width), jnp.float32),
+            up,
+            down,
+            up_theirs,
+            down_theirs,
+        ]
+        dma = pltpu.SemaphoreType.DMA
+        self.scratch = self.total_scratch(sums.shape[0], rows) + [dma((1, PLANE))] * 4
+
+    def run(self):
+        activated, slope, d_settled, sums, gain, shift, lifted, cotangent_all = self.ins
+        settled, d_hidden, vectors, up, down, up_theirs, down_theirs = self.outs
+        self.held[1][...] = sums[...]
+        total = self.small_sum(self.held[:6]) / self.full_width
+        average = total[:, 0:1]
+        factor = lax.rsqrt(total[:, 1:2] - average * average + EPSILON)
+        mean_scaled = total[:, 2:3]
+        mean_cross = factor * (total[:, 3:4] - average * mean_scaled)
+        rows = activated.shape[0]
+        step = rows // PLANE
+        gain_sum = shift_sum = bias_sum = 0.0
+        for first in range(0, rows, step):
+            at = slice(first, first + step)
+            normal = (activated[at, :] - average[at]) * factor[at]
+            settled[at, :] = (normal * gain[...] + shift[...]).astype(jnp.bfloat16)
+            grad = d_settled[at, :]
+            inner = factor[at] * (grad * gain[...] - mean_scaled[at] - normal * mean_cross[at])
+            low = (slope[at, :] * inner).astype(jnp.bfloat16)
+            d_hidden[at, :] = low
+            gain_sum += jnp.sum(grad * normal, 0, keepdims=True)
+            shift_sum += jnp.sum(grad, 0, keepdims=True)
+            bias_sum += jnp.sum(low.astype(jnp.float32), 0, keepdims=True)
+        vectors[...] = jnp.zeros_like(vectors)
+        vectors[0:1, :], vectors[1:2, :], vectors[2:3, :] = gain_sum, shift_sum, bias_sum
+        up_send, up_recv, down_send, down_recv = self.held[6:]
+        self.grads(
+            [
+                (lifted, d_hidden, [up], INWARD, [up_theirs], up_send, up_recv),
+                (settled, cotangent_all, [down], OUTWARD, [down_theirs], down_send, down_recv),
+            ]
+        )
+        return d_hidden
+
+
+class AttendFront(GradFront):
+    def __init__(self, d_branch, out_part, hat, factor, gain, kept, tables, segment, normed, inner_low, full_width):
+        self.inputs = [d_branch, out_part, hat, factor, gain, *kept, *tables]
+        self.inputs += [segment[:, None], segment[None, :], normed, inner_low]
+        self.full_width = full_width
+        rows, width = hat.shape
+        model_width = normed.shape[1]
+        low_type, f32, dma = jnp.bfloat16, jnp.float32, pltpu.SemaphoreType.DMA
+        inward, inward_theirs = grad_shapes(model_width, width, INWARD)
+        out, out_theirs = grad_shapes(model_width, width, OUTWARD)
+        self.out_shapes = [jax.ShapeDtypeStruct((8, width), f32)]
+        self.out_shapes += [inward, inward, inward, out, inward_theirs, inward_theirs, inward_theirs, out_theirs]
+        self.scratch = self.total_scratch(2, rows) + [dma((3, PLANE)), dma((3, PLANE)), dma((1, PLANE)), dma((1, PLANE))]
+        self.scratch += [pltpu.VMEM((rows, width), low_type), pltpu.VMEM((rows, 3 * width), low_type)]
+        self.scratch += [pltpu.VMEM((rows, width), f32)] * 4
+
+    def run(self):
+        d_branch, out_part, hat, factor, gain, attended, q_ref, k_ref, v_ref, lse = self.ins[:10]
+        cos_ref, sin_ref, grow_ref, column_ref, row_ref, normed, inner_low = self.ins[10:]
+        vectors, *grads = self.outs
+        grad_send, grad_recv, out_send, out_recv, d_att, lin_out, d_inner, d_query, d_key, d_value = self.held[6:]
+        rows_all, width = hat.shape
+        f32, low_type = jnp.float32, jnp.bfloat16
+        gain_sum = shift_sum = 0.0
+        for first in range(0, rows_all, ATTEND_ROWS):
+            at = slice(first, first + ATTEND_ROWS)
+            grad = lax.dot_general(
+                d_branch[at, :], out_part[...], (((1,), (1,)), ((), ())), preferred_element_type=f32
+            )
+            d_inner[at, :] = grad
+            gain_sum += jnp.sum(grad * hat[at, :], 0, keepdims=True)
+            shift_sum += jnp.sum(grad, 0, keepdims=True)
+            scaled = grad * gain[...]
+            sums = [jnp.sum(scaled, 1, keepdims=True), jnp.sum(scaled * hat[at, :], 1, keepdims=True)]
+            self.held[1][:, at] = as_lanes(sums)[:2]
+        vectors[...] = jnp.zeros_like(vectors)
+        vectors[0:1, :], vectors[1:2, :] = gain_sum, shift_sum
+        total = self.small_sum(self.held[:6]) / self.full_width
+        d_att[...] = (
+            factor[...] * (d_inner[...] * gain[...] - total[:, 0:1] - hat[...] * total[:, 1:2])
+        ).astype(low_type)
+        heads, scale = width // HEAD, HEAD ** (-0.5)
+        for first in range(0, rows_all, ATTEND_ROWS):
+            at, keys = slice(first, first + ATTEND_ROWS), first + ATTEND_ROWS
+            allowed = allowed_part(column_ref, row_ref, first, ATTEND_ROWS, keys)
+            for head in range(heads):
+                lanes = slice(head * HEAD, (head + 1) * HEAD)
+                scores = lax.dot_general(
+                    q_ref[at, lanes] * scale,
+                    k_ref[:keys, lanes],
+                    (((1,), (1,)), ((), ())),
+                    preferred_element_type=f32,
+                )
+                scores = jnp.where(allowed, scores, -1e30)
+                probs = jnp.exp(scores - lse[at, head : head + 1])
+                d_rows = d_att[at, lanes]
+                d_probs = lax.dot_general(
+                    d_rows, v_ref[:keys, lanes], (((1,), (1,)), ((), ())), preferred_element_type=f32
+                )
+                delta = jnp.sum(d_rows.astype(f32) * attended[at, lanes], -1, keepdims=True)
+                d_scores = (probs * (d_probs - delta)).astype(low_type)
+                d_query[at, lanes] = jnp.dot(d_scores, k_ref[:keys, lanes], preferred_element_type=f32) * scale
+                key_part = (
+                    lax.dot_general(
+                        d_scores, q_ref[at, lanes], (((0,), (0,)), ((), ())), preferred_element_type=f32
+                    )
+                    * scale
+                )
+                value_part = lax.dot_general(
+                    probs.astype(low_type), d_rows, (((0,), (0,)), ((), ())), preferred_element_type=f32
+                )
+                if first:
+                    d_key[:first, lanes] += key_part[:first]
+                    d_value[:first, lanes] += value_part[:first]
+                d_key[first:keys, lanes] = key_part[first:]
+                d_value[first:keys, lanes] = value_part[first:]
+        for first in range(0, rows_all, ATTEND_ROWS):
+            at = slice(first, first + ATTEND_ROWS)
+            cosine, sine, growth = cos_ref[at, :], sin_ref[at, :], grow_ref[at, :]
+            scaled = d_query[at, :] * growth
+            lin_out[at, :width] = (scaled * cosine - halves_swapped(scaled) * sine).astype(low_type)
+            scaled = d_key[at, :] * (1.0 / growth)
+            lin_out[at, width : 2 * width] = (scaled * cosine - halves_swapped(scaled) * sine).astype(low_type)
+            lin_out[at, 2 * width :] = d_value[at, :].astype(low_type)
+        self.grads(
+            [
+                (normed, lin_out, grads[:3], INWARD, grads[4:7], grad_send, grad_recv),
+                (inner_low, d_branch, grads[3:4], OUTWARD, grads[7:], out_send, out_recv),
+            ]
+        )
+        return lin_out
+
+
+def exchange(front, streams, riders, cid):
+    fronts = [front] if front is not None else []
+    parts = fronts + list(streams) + list(riders)
 
     def kernel(*refs):
         here = Places()
@@ -1158,15 +1422,17 @@
         outs = [take(len(part.out_shapes)) for part in parts]
         for part, part_ins, part_outs in zip(parts, ins, outs):
             part.bind(here, part_ins, part_outs, take(len(part.scratch)))
-        wide_riders = [rider for rider in riders if len(rider.peers(here)) > 1]
+        wide_parts = fronts + [rider for rider in riders if isinstance(rider, PlaneWeights)]
         peers = [here.tp_peer]
-        if any(not isinstance(rider, PlaneWeights) for rider in riders):
+        if isinstance(front, GradFront) or any(not isinstance(rider, PlaneWeights) for rider in riders):
             peers.append(here.img_peer)
-        if wide_riders:
-            peers += wide_riders[0].peers(here)
+        if wide_parts:
+            peers += wide_parts[0].peers(here)
         else:
             peers += [here.core, here.x, here.y]
         greet(peers)
+        if front is not None:
+            streams[0].left = front.run()
         streams[0].begin()
         for rider in riders:
             rider.start()
@@ -1175,14 +1441,15 @@
         stages = []
         for stream in reversed(streams):
             stages += stream.stages()
-        wavefront(stages, PIECES, [launch for rider in riders for launch in rider.launches])
+        wavefront(stages, PIECES, [launch for part in fronts + list(riders) for launch in part.launches])
         for part in parts:
             part.finish()
 
     out_shapes = [shape for part in parts for shape in part.out_shapes]
-    in_specs = [ON_CHIP] * sum(len(stream.inputs) for stream in streams)
+    in_specs = [ON_CHIP] * sum(len(part.inputs) for part in fronts + list(streams))
     in_specs += [ANYWHERE] * sum(len(rider.inputs) for rider in riders)
-    out_specs = [spec for stream in streams for spec in stream.out_specs()]
+    out_specs = [ON_CHIP for part in fronts for _ in part.out_shapes]
+    out_specs += [spec for stream in streams for spec in stream.out_specs()]
     out_specs += [ANYWHERE] * sum(len(rider.out_shapes) for rider in riders)
     made = pl.pallas_call(
         kernel,
@@ -1385,76 +1652,320 @@
     )(*arrays)
 
 
-def small_total(values, cid):
-    def kernel(in_ref, out_ref, plane, mine, theirs, send, recv):
-        here = Places()
-        seq, tp, img = here.seq, here.tp, here.img
-        peers = [(lax.rem(seq + step, PLANE), tp, img) for step in range(1, PLANE)]
-        greet(peers + [here.tp_peer])
-        made = []
-        for step, peer in enumerate(peers):
-            copy = remote(in_ref, plane.at[step], send.at[step], recv.at[step], peer)
-            copy.start()
-            made.append(copy)
-        total = in_ref[...]
-        for step, copy in enumerate(made):
-            copy.wait_recv()
-            total = total + plane[step]
-        mine[...] = total
-        last = remote(mine, theirs, send.at[PLANE - 1], recv.at[PLANE - 1], here.tp_peer)
-        last.start()
-        last.wait()
-        out_ref[...] = mine[...] + theirs[...]
-        for copy in made:
-            copy.wait_send()
-
-    dma = pltpu.SemaphoreType.DMA
+IMAGES_A_STEP = 4
+
+
+def image_probs_of(probe, keys, scale):
+    scores = lax.dot_general(
+        probe * scale, keys, (((1,), (1,)), ((), ())), preferred_element_type=jnp.float32
+    )
+    weights = jnp.exp(scores - jnp.max(scores, -1, keepdims=True))
+    return weights * (1.0 / jnp.sum(weights, -1, keepdims=True))
+
+
+def image_forward(pictures, key_part, value_part, latent_all, probe_part, slots, live):
+    images, width = slots.shape[0], key_part.shape[1]
+    scale = HEAD ** (-0.5)
+    step = IMAGES_A_STEP * PATCH
+
+    def kernel(slots_ref, live_ref, pictures_ref, key_w, value_w, latent_ref, probe_w, keys, placed, probe, both_w):
+        number = pl.program_id(0)
+
+        @pl.when(number == 0)
+        def _():
+            probe[...] = jnp.dot(latent_ref[...], probe_w[...], preferred_element_type=jnp.float32).astype(
+                jnp.bfloat16
+            )
+            both_w[:, :width] = key_w[...]
+            both_w[:, width:] = value_w[...]
+
+        keys[...] = jnp.dot(pictures_ref[...], both_w[...], preferred_element_type=jnp.float32).astype(jnp.bfloat16)
+        for image in range(IMAGES_A_STEP):
+            slot = number * IMAGES_A_STEP + image
+            alive = (live_ref[slot] > 0).astype(jnp.float32)
+            rows = slice(image * PATCH, (image + 1) * PATCH)
+            mixed = []
+            for first in range(0, width, HEAD):
+                probs = image_probs_of(probe[:, first : first + HEAD], keys[rows, first : first + HEAD], scale)
+                values = keys[rows, width + first : width + first + HEAD]
+                mixed.append(jnp.dot(probs.astype(jnp.bfloat16), values, preferred_element_type=jnp.float32))
+            at = pl.ds(pl.multiple_of(slots_ref[slot] * LAT, LAT), LAT)
+            placed[at, :] = (jnp.concatenate(mixed, 1) * alive).astype(jnp.bfloat16)
+
+    def whole(shape):
+        return pl.BlockSpec(shape, lambda i, slots, live: (0, 0))
+
     return pl.pallas_call(
         kernel,
-        out_shape=jax.ShapeDtypeStruct(values.shape, values.dtype),
-        in_specs=[ON_CHIP],
-        out_specs=ON_CHIP,
-        scratch_shapes=[
-            pltpu.VMEM((PLANE - 1,) + values.shape, values.dtype),
-            pltpu.VMEM(values.shape, values.dtype),
-            pltpu.VMEM(values.shape, values.dtype),
-            dma((PLANE,)),
-            dma((PLANE,)),
-        ],
-        compiler_params=pltpu.CompilerParams(collective_id=cid, has_side_effects=True),
-    )(values)
-
-
-def small_gather(values, cid):
-    def kernel(in_ref, out_ref, send, recv):
-        here = Places()
-        seq, tp, img = here.seq, here.tp, here.img
-        peers = []
-        for step in range(2 * PLANE):
-            if step == 0:
-                continue
-            peers.append((lax.rem(seq + step // 2, PLANE), tp, lax.rem(img + step % 2, 2)))
-        greet(peers)
-        out_ref[seq, img] = in_ref[...]
-        made = []
-        for step, peer in enumerate(peers):
-            copy = remote(in_ref, out_ref.at[seq, img], send.at[step], recv.at[step], peer)
-            copy.start()
-            made.append(copy)
-        for copy in made:
-            copy.wait()
-
-    dma = pltpu.SemaphoreType.DMA
+        out_shape=(
+            jax.ShapeDtypeStruct((images * PATCH, 2 * width), jnp.bfloat16),
+            jax.ShapeDtypeStruct((images * LAT, width), jnp.bfloat16),
+            jax.ShapeDtypeStruct((LAT, width), jnp.bfloat16),
+        ),
+        grid_spec=pltpu.PrefetchScalarGridSpec(
+            num_scalar_prefetch=2,
+            grid=(images // IMAGES_A_STEP,),
+            in_specs=[
+                pl.BlockSpec((step, pictures.shape[1]), lambda i, slots, live: (i, 0)),
+                whole(key_part.shape),
+                whole(value_part.shape),
+                whole(latent_all.shape),
+                whole(probe_part.shape),
+            ],
+            out_specs=(
+                pl.BlockSpec((step, 2 * width), lambda i, slots, live: (i, 0)),
+                whole((images * LAT, width)),
+                whole((LAT, width)),
+            ),
+            scratch_shapes=[pltpu.VMEM((key_part.shape[0], 2 * width), jnp.bfloat16)],
+        ),
+        compiler_params=pltpu.CompilerParams(vmem_limit_bytes=VMEM_BYTES),
+    )(slots, live, pictures, key_part, value_part, latent_all, probe_part)
+
+
+def image_backward(d_rows, pictures, keys, probe, placed, out_part, slots, live):
+    images, width = slots.shape[0], probe.shape[1]
+    model_width, picture_width = d_rows.shape[1], pictures.shape[1]
+    scale = HEAD ** (-0.5)
+    f32, low_type = jnp.float32, jnp.bfloat16
+    step = IMAGES_A_STEP * PATCH
+    steps = images // IMAGES_A_STEP
+
+    def kernel(slots_ref, live_ref, d_ref, pictures_ref, keys_ref, probe_ref, placed_ref, out_w, *rest):
+        key_out, value_out, out_out, probe_out, both_sum, d_mixed, d_both = rest
+        number = pl.program_id(0)
+
+        @pl.when(number == 0)
+        def _():
+            probe_out[...] = jnp.zeros_like(probe_out)
+            d_mixed[...] = lax.dot_general(
+                d_ref[...], out_w[...], (((1,), (1,)), ((), ())), preferred_element_type=f32
+            ).astype(low_type)
+            out_out[...] = lax.dot_general(
+                placed_ref[...], d_ref[...], (((0,), (0,)), ((), ())), preferred_element_type=f32
+            ).astype(low_type)
+
+        for image in range(IMAGES_A_STEP):
+            slot = number * IMAGES_A_STEP + image
+            alive = (live_ref[slot] > 0).astype(low_type)
+            rows = slice(image * PATCH, (image + 1) * PATCH)
+            d_here = d_mixed[pl.ds(pl.multiple_of(slots_ref[slot] * LAT, LAT), LAT), :] * alive
+            d_probe = []
+            for first in range(0, width, HEAD):
+                at = slice(first, first + HEAD)
+                keys_here = keys_ref[rows, at]
+                values = keys_ref[rows, width + first : width + first + HEAD]
+                probs = image_probs_of(probe_ref[:, at], keys_here, scale)
+                d_probs = lax.dot_general(
+                    d_here[:, at], values, (((1,), (1,)), ((), ())), preferred_element_type=f32
+                )
+                d_scores = probs * (d_probs - jnp.sum(probs * d_probs, -1, keepdims=True))
+                d_scores = d_scores.astype(low_type)
+                d_probe.append(jnp.dot(d_scores, keys_here, preferred_element_type=f32) * scale)
+                d_both[rows, at] = (
+                    lax.dot_general(
+                        d_scores, probe_ref[:, at], (((0,), (0,)), ((), ())), preferred_element_type=f32
+                    )
+                    * scale
+                ).astype(low_type)
+                d_both[rows, width + first : width + first + HEAD] = lax.dot_general(
+                    probs.astype(low_type), d_here[:, at], (((0,), (0,)), ((), ())), preferred_element_type=f32
+                ).astype(low_type)
+            probe_out[...] += jnp.concatenate(d_probe, 1)
+        part = lax.dot_general(
+            pictures_ref[...], d_both[...], (((0,), (0,)), ((), ())), preferred_element_type=f32
+        )
+
+        @pl.when(number == 0)
+        def _():
+            both_sum[...] = part
+
+        @pl.when(number > 0)
+        def _():
+            both_sum[...] += part
+
+        @pl.when(number == steps - 1)
+        def _():
+            key_out[...] = both_sum[:, :width].astype(low_type)
+            value_out[...] = both_sum[:, width:].astype(low_type)
+
+    def whole(shape):
+        return pl.BlockSpec(shape, lambda i, slots, live: (0, 0))
+
+    def stepped(columns):
+        return pl.BlockSpec((step, columns), lambda i, slots, live: (i, 0))
+
     return pl.pallas_call(
         kernel,
-        out_shape=jax.ShapeDtypeStruct((PLANE, 2) + values.shape, values.dtype),
-        in_specs=[ON_CHIP],
-        out_specs=ON_CHIP,
-        scratch_shapes=[dma((2 * PLANE - 1,)), dma((2 * PLANE - 1,))],
-        compiler_params=pltpu.CompilerParams(
-            collective_id=cid, has_side_effects=True, vmem_limit_bytes=VMEM_BYTES
+        out_shape=(
+            jax.ShapeDtypeStruct((picture_width, width), low_type),
+            jax.ShapeDtypeStruct((picture_width, width), low_type),
+            jax.ShapeDtypeStruct((width, model_width), low_type),
+            jax.ShapeDtypeStruct((LAT, width), f32),
         ),
-    )(values)
+        grid_spec=pltpu.PrefetchScalarGridSpec(
+            num_scalar_prefetch=2,
+            grid=(steps,),
+            in_specs=[
+                whole(d_rows.shape),
+                stepped(picture_width),
+                stepped(2 * width),
+                whole(probe.shape),
+                whole(placed.shape),
+                whole(out_part.shape),
+            ],
+            out_specs=(
+                whole((picture_width, width)),
+                whole((picture_width, width)),
+                whole((width, model_width)),
+                whole((LAT, width)),
+            ),
+            scratch_shapes=[
+                pltpu.VMEM((picture_width, 2 * width), f32),
+                pltpu.VMEM((d_rows.shape[0], width), low_type),
+                pltpu.VMEM((step, 2 * width), low_type),
+            ],
+        ),
+        compiler_params=pltpu.CompilerParams(vmem_limit_bytes=VMEM_BYTES),
+    )(slots, live, d_rows, pictures, keys, probe, placed, out_part)
+
+
+def xpos_tables(position, width):
+    cosine, sine, growth = (table[:, 0, :] for table in xpos_factors(position, HEAD // 2))
+    repeats = width // HEAD
+    return (
+        jnp.tile(cosine, (1, 2 * repeats)),
+        jnp.tile(jnp.concatenate([-sine, sine], 1), (1, repeats)),
+        jnp.tile(growth, (1, 2 * repeats)),
+    )
+
+
+def halves_swapped(rows):
+    width, half = rows.shape[1], HEAD // 2
+    lane = lax.broadcasted_iota(jnp.int32, rows.shape, 1)
+    ahead = pltpu.roll(rows, width - half, 1)
+    behind = pltpu.roll(rows, half, 1)
+    return jnp.where(lane % HEAD < half, ahead, behind)
+
+
+def allowed_part(segment_column, segment_row, first, count, keys):
+    row = first + lax.broadcasted_iota(jnp.int32, (count, keys), 0)
+    column = lax.broadcasted_iota(jnp.int32, (count, keys), 1)
+    same = segment_column[pl.ds(first, count), :] == segment_row[:, :keys]
+    return same & (column <= row)
+
+
+ATTEND_ROWS = 256
+
+
+def attend_forward(normed, query_w, key_w, value_w, tables, segment):
+    rows_all, width = normed.shape[0], query_w.shape[1]
+    heads = width // HEAD
+    scale = HEAD ** (-0.5)
+    f32, low_type = jnp.float32, jnp.bfloat16
+
+    def kernel(normed_ref, query_ref, key_ref, value_ref, cos_ref, sin_ref, grow_ref, column_ref, row_ref, *outs):
+        q_out, k_out, v_out, att_out, lse_out, stat_out = outs
+        for first in range(0, rows_all, ATTEND_ROWS):
+            at = slice(first, first + ATTEND_ROWS)
+            rows = normed_ref[at, :]
+            cosine, sine, growth = cos_ref[at, :], sin_ref[at, :], grow_ref[at, :]
+            lin = jnp.dot(rows, query_ref[...], preferred_element_type=f32)
+            q_out[at, :] = ((lin * cosine + halves_swapped(lin) * sine) * growth).astype(low_type)
+            lin = jnp.dot(rows, key_ref[...], preferred_element_type=f32)
+            k_out[at, :] = ((lin * cosine + halves_swapped(lin) * sine) * (1.0 / growth)).astype(low_type)
+            v_out[at, :] = jnp.dot(rows, value_ref[...], preferred_element_type=f32).astype(low_type)
+        for first in range(0, rows_all, ATTEND_ROWS):
+            at, keys = slice(first, first + ATTEND_ROWS), first + ATTEND_ROWS
+            allowed = allowed_part(column_ref, row_ref, first, ATTEND_ROWS, keys)
+            for head in range(heads):
+                lanes = slice(head * HEAD, (head + 1) * HEAD)
+                scores = lax.dot_general(
+                    q_out[at, lanes] * scale,
+                    k_out[:keys, lanes],
+                    (((1,), (1,)), ((), ())),
+                    preferred_element_type=f32,
+                )
+                scores = jnp.where(allowed, scores, -1e30)
+                best = jnp.max(scores, -1, keepdims=True)
+                weights = jnp.exp(scores - best)
+                total = jnp.sum(weights, -1, keepdims=True)
+                probs = (weights * (1.0 / total)).astype(low_type)
+                att_out[at, lanes] = jnp.dot(probs, v_out[:keys, lanes], preferred_element_type=f32)
+                lse_out[at, head : head + 1] = best + jnp.log(total)
+        for first in range(0, rows_all, ATTEND_ROWS):
+            at = slice(first, first + ATTEND_ROWS)
+            rows = att_out[at, :]
+            sums = [jnp.sum(rows, 1, keepdims=True), jnp.sum(rows * rows, 1, keepdims=True)]
+            stat_out[:, at] = as_lanes(sums)[:2]
+
+    return pl.pallas_call(
+        kernel,
+        out_shape=(
+            jax.ShapeDtypeStruct((rows_all, width), low_type),
+            jax.ShapeDtypeStruct((rows_all, width), low_type),
+            jax.ShapeDtypeStruct((rows_all, width), low_type),
+            jax.ShapeDtypeStruct((rows_all, width), f32),
+            jax.ShapeDtypeStruct((rows_all, 8), f32),
+            jax.ShapeDtypeStruct((2, rows_all), f32),
+        ),
+        in_specs=[ON_CHIP] * 9,
+        out_specs=(ON_CHIP,) * 6,
+        compiler_params=pltpu.CompilerParams(vmem_limit_bytes=VMEM_BYTES),
+    )(normed, query_w, key_w, value_w, *tables, segment[:, None], segment[None, :])
+
+
+def as_lanes(columns):
+    rows = columns[0].shape[0]
+    lane = lax.broadcasted_iota(jnp.int32, (rows, LANES), 1)
+    joined = jnp.zeros((rows, LANES), jnp.float32)
+    for number, column in enumerate(columns):
+        joined = jnp.where(lane == number, column, joined)
+    return joined.T[:8, :]
+
+
+def hidden_forward(lifted, up_part, bias, cotangent_all, down_part, gain):
+    rows_all, width = lifted.shape[0], up_part.shape[1]
+    model_width = lifted.shape[1]
+    step = min(256, rows_all)
+    f32 = jnp.float32
+
+    def kernel(lifted_ref, up_ref, bias_ref, cot_ref, down_ref, gain_ref, act_out, slope_out, grad_out, stat_out):
+        pre = jnp.dot(lifted_ref[...], up_ref[...], preferred_element_type=f32) + bias_ref[...]
+        below = 0.5 + 0.5 * lax.erf(pre * (0.5**0.5))
+        activated = pre * below
+        act_out[...] = activated
+        slope_out[...] = below + pre * jnp.exp(-0.5 * pre * pre) * (1.0 / (2.0 * jnp.pi) ** 0.5)
+        grad = lax.dot_general(
+            cot_ref[...], down_ref[...], (((1,), (1,)), ((), ())), preferred_element_type=f32
+        )
+        grad_out[...] = grad
+        scaled = grad * gain_ref[...]
+        sums = [activated, activated * activated, scaled, scaled * activated]
+        stat_out[...] = as_lanes([jnp.sum(part, 1, keepdims=True) for part in sums])[:4]
+
+    def whole(shape):
+        return pl.BlockSpec(shape, lambda i: (0, 0))
+
+    def rows(columns):
+        return pl.BlockSpec((step, columns), lambda i: (i, 0))
+
+    wide_shape = jax.ShapeDtypeStruct((rows_all, width), f32)
+    return pl.pallas_call(
+        kernel,
+        out_shape=(wide_shape, wide_shape, wide_shape, jax.ShapeDtypeStruct((4, rows_all), f32)),
+        grid=(rows_all // step,),
+        in_specs=[
+            rows(model_width),
+            whole(up_part.shape),
+            whole(bias.shape),
+            rows(model_width),
+            whole(down_part.shape),
+            whole(gain.shape),
+        ],
+        out_specs=(rows(width), rows(width), rows(width), pl.BlockSpec((4, step), lambda i: (0, i))),
+        compiler_params=pltpu.CompilerParams(vmem_limit_bytes=VMEM_BYTES),
+    )(lifted, up_part, bias, cotangent_all, down_part, gain)
 
 
 def norm_rows(rows, gain, shift):
@@ -1513,41 +2024,31 @@
             resample_key,
             resample_value,
             resample_query,
+            latents,
             resample_out,
             query_weight,
             key_weight,
             value_weight,
             out_weight,
         ),
-        (INWARD, INWARD, INWARD, OUTWARD, INWARD, INWARD, INWARD, OUTWARD),
+        (INWARD, INWARD, INWARD, SHARED, OUTWARD, INWARD, INWARD, INWARD, OUTWARD),
         1,
     )
     (pictures,) = rows
-    image_key_own, image_value_own, probe_own, image_out_own, query_own, key_own, value_own, out_own = own
+    image_key_own, image_value_own, probe_own, latent_all, image_out_own, *layer_own = own
+    query_own, key_own, value_own, out_own = layer_own
     qkv_own = jnp.concatenate([query_own, key_own, value_own], 1)
-    latent_all = small_gather(latents, 2).transpose(2, 0, 1, 3).reshape(LAT, model_width)
-
-    probe = dot32(latent_all, probe_own).astype(low).reshape(LAT, own_heads, HEAD)
-    image_keys = dot32(pictures, image_key_own).astype(low).reshape(image_total, PATCH, own_heads, HEAD)
-    image_values = dot32(pictures, image_value_own).astype(low).reshape(image_total, PATCH, own_heads, HEAD)
-    image_scores = (
-        jnp.einsum("qhd,iphd->ihqp", probe, image_keys, preferred_element_type=f32) * score_scale
-    )
-    image_probs = jax.nn.softmax(image_scores, -1)
-    image_mixed = jnp.einsum(
-        "ihqp,iphd->iqhd", image_probs.astype(low), image_values, preferred_element_type=f32
-    )
-    image_mixed = image_mixed.astype(low).reshape(image_total, LAT * own_width)
 
     slot_range = jnp.arange(image_total, dtype=jnp.int32)
     live = slot_range % IMG_DEV < jnp.repeat(image_count[0], IMG_DEV)
+    live_mark = live.astype(jnp.int32)
     block_count = group_rows // LAT
-    owner = (
-        (image_slot[0][None, :] == jnp.arange(block_count, dtype=jnp.int32)[:, None]) & live[None, :]
-    ).astype(low)
-    mixed_placed = dot32(owner, image_mixed).astype(low).reshape(group_rows, own_width)
-    taken = jnp.repeat((jnp.sum(owner.astype(f32), 1) > 0.5).astype(f32), LAT)[:, None]
+    owner = (image_slot[0][None, :] == jnp.arange(block_count, dtype=jnp.int32)[:, None]) & live[None, :]
+    taken = jnp.repeat(jnp.any(owner, 1).astype(f32), LAT)[:, None]
     taken_own = lax.dynamic_slice_in_dim(taken, seq_rank * row_count, row_count, 0)
+    image_keys, mixed_placed, probe = image_forward(
+        pictures, image_key_own, image_value_own, latent_all, probe_own, image_slot[0], live_mark
+    )
 
     def wide(vector):
         return vector.astype(f32)[None, :]
@@ -1565,8 +2066,10 @@
 
     rows_wide = jax.ShapeDtypeStruct((row_count, model_width), f32)
     (mixed_in, normed), hidden_blocks = exchange(
+        None,
         [
             Stream(
+                group_rows,
                 mixed_placed,
                 image_out_own,
                 False,
@@ -1582,50 +2085,28 @@
     )
 
     segment_all = segment[0]
-    docs_count = 3 * (group_rows // min(SEQ_MAX, group_rows))
-    marks = (segment_all[:, None] == jnp.arange(docs_count, dtype=jnp.int32)[None, :]).astype(jnp.int32)
-    earlier_rows = jnp.cumsum(marks, 0) - marks
-    position = jnp.sum(earlier_rows * marks, 1).astype(f32)
-    cosine, sine_table, growth = xpos_factors(position, HEAD // 2)
     row_index = jnp.arange(group_rows, dtype=jnp.int32)
-    allowed = (row_index[None, :] <= row_index[:, None]) & (segment_all[None, :] == segment_all[:, None])
-
+    earlier = (row_index[None, :] < row_index[:, None]) & (segment_all[None, :] == segment_all[:, None])
+    tables = xpos_tables(jnp.sum(earlier.astype(f32), 1), own_width)
     cot_late, _ = lax.optimization_barrier((cotangent[0], normed))
     cot_all = lax.all_gather(cot_late, SEQ, axis=0, tiled=True)
-    lin = dot32(normed, qkv_own)
-    query_rot = rotate(
-        lin[:, :own_width].reshape(group_rows, own_heads, HEAD), cosine, sine_table, growth
-    ).astype(low)
-    keys_rot = rotate(
-        lin[:, own_width : 2 * own_width].reshape(group_rows, own_heads, HEAD), cosine, sine_table, 1.0 / growth
-    ).astype(low)
-    values = lin[:, 2 * own_width :].astype(low).reshape(group_rows, own_heads, HEAD)
-    scores = jnp.einsum("qhd,khd->hqk", query_rot, keys_rot, preferred_element_type=f32) * score_scale
-    probs = jax.nn.softmax(jnp.where(allowed[None], scores, -1e30), -1)
-    attended = jnp.einsum("hqk,khd->qhd", probs.astype(low), values, preferred_element_type=f32)
-    attended = attended.reshape(group_rows, own_width)
-
-    def split_stats(parts, cid):
-        total = small_total(jnp.stack(parts), cid)
-        return [total[number][:, None] for number in range(len(parts))]
-
-    inner_sum, inner_square = split_stats((jnp.sum(attended, 1), jnp.sum(attended * attended, 1)), 4)
-    average = inner_sum / model_width
-    inner_factor = lax.rsqrt(inner_square / model_width - average * average + EPSILON)
-    inner_hat = (attended - average) * inner_factor
+    query_rot, keys_rot, values, attended, log_total, inner_sums = attend_forward(
+        normed, query_own, key_own, value_own, tables, segment_all
+    )
+
     inner_gain_own = wide(own_part(inner_gain))
-    inner_low = (inner_hat * inner_gain_own + wide(own_part(inner_shift))).astype(low)
-
     def middle_step(total, piece, views, outs):
         mixed_view, gain, shift = views
         middle = mixed_view[...] + total
         outs[0][...] = middle
         return norm_rows(middle, gain[...], shift[...])[0].astype(jnp.bfloat16)
 
-    (middle, lifted), hidden_own = exchange(
+    (inner_low, inner_hat, inner_factor), (middle, lifted), hidden_own = exchange(
+        InnerFront(attended, inner_sums, inner_gain_own, wide(own_part(inner_shift)), model_width),
         [
             Stream(
-                inner_low,
+                group_rows,
+                None,
                 out_own,
                 False,
                 (mixed_in, wide(middle_gain), wide(middle_shift)),
@@ -1641,34 +2122,10 @@
     up_own, down_own = hidden_own[0].reshape(model_width, -1), hidden_own[1]
     own_hidden = up_own.shape[1]
 
-    hidden_pre = dot32(lifted, up_own) + wide(own_part(up_bias))
-    activated, gelu_pull = jax.vjp(functools.partial(jax.nn.gelu, approximate=False), hidden_pre)
-    d_settled = dot32(cot_all, down_own.T)
     hidden_gain_own = wide(own_part(hidden_gain))
-    scaled = d_settled * hidden_gain_own
-    sum_act, sum_square, sum_scaled, sum_cross = split_stats(
-        (
-            jnp.sum(activated, 1),
-            jnp.sum(activated * activated, 1),
-            jnp.sum(scaled, 1),
-            jnp.sum(scaled * activated, 1),
-        ),
-        6,
-    )
-    average = sum_act / FF
-    hidden_factor = lax.rsqrt(sum_square / FF - average * average + EPSILON)
-    settled_hat = (activated - average) * hidden_factor
-    settled = (settled_hat * hidden_gain_own + wide(own_part(hidden_shift))).astype(low)
-    mean_scaled = sum_scaled / FF
-    mean_cross = hidden_factor * (sum_cross / FF - average * mean_scaled)
-    d_activated = hidden_factor * (scaled - mean_scaled - settled_hat * mean_cross)
-    d_hidden = gelu_pull(d_activated)[0].astype(low)
-    hidden_gain_grad = jnp.sum(d_settled * settled_hat, 0)
-    hidden_shift_grad = jnp.sum(d_settled, 0)
-    up_bias_grad = jnp.sum(d_hidden.astype(f32), 0)
-    down_grad = dot32(settled.T, cot_all).astype(low)
-    up_grad = dot32(lifted.T, d_hidden).astype(low)
-
+    activated, slope, d_settled, hidden_sums = hidden_forward(
+        lifted, up_own, wide(own_part(up_bias)), cot_all, down_own, hidden_gain_own
+    )
     def blocks_in(grad):
         return grad.reshape(PLANE, 2, -1, grad.shape[1])
 
@@ -1692,11 +2149,22 @@
         outs[2][...] += jnp.sum(total, 0, keepdims=True)
         return grad.astype(jnp.bfloat16)
 
-    hidden_grads = (blocks_in(up_grad), down_grad)
-    (d_middle, middle_gain_grad, middle_shift_grad, d_branch), hidden_theirs = exchange(
+    hidden_made, (d_middle, middle_gain_grad, middle_shift_grad, d_branch) = exchange(
+        HiddenFront(
+            activated,
+            slope,
+            d_settled,
+            hidden_sums,
+            hidden_gain_own,
+            wide(own_part(hidden_shift)),
+            lifted,
+            cot_all,
+            FF,
+        ),
         [
             Stream(
-                d_hidden,
+                group_rows,
+                None,
                 up_own,
                 True,
                 (middle, cotangent[0], wide(middle_gain)),
@@ -1706,44 +2174,29 @@
                 True,
             )
         ],
-        [CrossGrads(hidden_grads, (INWARD, OUTWARD))],
+        [],
         8,
     )
 
-    out_grad = dot32(inner_low.T, d_branch).astype(low)
-    d_inner = dot32(d_branch, out_own.T)
-    inner_gain_grad = jnp.sum(d_inner * inner_hat, 0)
-    inner_shift_grad = jnp.sum(d_inner, 0)
-    scaled = d_inner * inner_gain_own
-    sum_scaled, sum_cross = split_stats((jnp.sum(scaled, 1), jnp.sum(scaled * inner_hat, 1)), 9)
-    d_attended = inner_factor * (scaled - sum_scaled / model_width - inner_hat * (sum_cross / model_width))
-    d_attended = d_attended.astype(low).reshape(group_rows, own_heads, HEAD)
-    delta = jnp.sum(d_attended.astype(f32) * attended.reshape(group_rows, own_heads, HEAD), -1).T
-    d_probs = jnp.einsum("qhd,khd->hqk", d_attended, values, preferred_element_type=f32)
-    d_scores = (probs * (d_probs - delta[..., None])).astype(low)
-    d_query = jnp.einsum("hqk,khd->qhd", d_scores, keys_rot, preferred_element_type=f32) * score_scale
-    d_key = jnp.einsum("hqk,qhd->khd", d_scores, query_rot, preferred_element_type=f32) * score_scale
-    d_value = jnp.einsum("hqk,qhd->khd", probs.astype(low), d_attended, preferred_element_type=f32)
-    d_lin = jnp.concatenate(
-        [
-            rotate_back(d_query, cosine, sine_table, growth).astype(low).reshape(group_rows, own_width),
-            rotate_back(d_key, cosine, sine_table, 1.0 / growth).astype(low).reshape(group_rows, own_width),
-            d_value.astype(low).reshape(group_rows, own_width),
-        ],
-        1,
-    )
-    lin_grad = dot32(normed.T, d_lin).astype(low)
-    layer_grads = (
-        blocks_in(lin_grad[:, :own_width]),
-        blocks_in(lin_grad[:, own_width : 2 * own_width]),
-        blocks_in(lin_grad[:, 2 * own_width :]),
-        out_grad,
-    )
-    layer_sides = (INWARD, INWARD, INWARD, OUTWARD)
-    (d_mixed, input_gain_grad, input_shift_grad, d_rows), (result,), layer_theirs = exchange(
+    settled, _, hidden_vectors, *hidden_pairs = hidden_made
+    attend_made, (d_mixed, input_gain_grad, input_shift_grad, d_rows), (result,) = exchange(
+        AttendFront(
+            d_branch,
+            out_own,
+            inner_hat,
+            inner_factor,
+            inner_gain_own,
+            (attended, query_rot, keys_rot, values, log_total),
+            tables,
+            segment_all,
+            normed,
+            inner_low,
+            model_width,
+        ),
         [
             Stream(
-                d_lin,
+                group_rows,
+                None,
                 qkv_own,
                 True,
                 (mixed_in, d_middle, wide(input_gain)),
@@ -1753,6 +2206,7 @@
                 True,
             ),
             Stream(
+                group_rows,
                 settled,
                 down_own,
                 False,
@@ -1763,49 +2217,30 @@
                 False,
             ),
         ],
-        [CrossGrads(layer_grads, layer_sides)],
+        [],
         10,
     )
+    inner_vectors, *layer_pairs = attend_made
     text_grad = jnp.where(taken_own > 0.5, 0.0, d_mixed)
 
-    image_out_grad = dot32(mixed_placed.T, d_rows).astype(low)
-    d_mixed_rows = dot32(d_rows, image_out_own.T).astype(low)
-    d_image_mixed = dot32(owner.T, d_mixed_rows.reshape(block_count, LAT * own_width)).astype(low)
-    d_image_mixed = d_image_mixed.reshape(image_total, LAT, own_heads, HEAD)
-    d_image_probs = jnp.einsum("iqhd,iphd->ihqp", d_image_mixed, image_values, preferred_element_type=f32)
-    d_image_scores = image_probs * (
-        d_image_probs - jnp.sum(image_probs * d_image_probs, -1, keepdims=True)
-    )
-    d_image_scores = d_image_scores.astype(low)
-    d_probe = jnp.einsum("ihqp,iphd->qhd", d_image_scores, image_keys, preferred_element_type=f32) * score_scale
-    d_image_keys = (
-        jnp.einsum("ihqp,qhd->iphd", d_image_scores, probe, preferred_element_type=f32) * score_scale
-    ).astype(low)
-    d_image_values = jnp.einsum(
-        "ihqp,iqhd->iphd", image_probs.astype(low), d_image_mixed, preferred_element_type=f32
-    ).astype(low)
-    picture_rows = image_total * PATCH
-    image_grad = dot32(
-        pictures.T,
-        jnp.concatenate(
-            [d_image_keys.reshape(picture_rows, own_width), d_image_values.reshape(picture_rows, own_width)], 1
-        ),
-    ).astype(low)
+    image_key_grad, image_value_grad, image_out_grad, d_probe = image_backward(
+        d_rows, pictures, image_keys, probe, mixed_placed, image_out_own, image_slot[0], live_mark
+    )
 
     own_vectors = jnp.concatenate(
-        [inner_gain_grad, inner_shift_grad, up_bias_grad, hidden_gain_grad, hidden_shift_grad]
+        [inner_vectors[0], inner_vectors[1], hidden_vectors[2], hidden_vectors[0], hidden_vectors[1]]
     )
     row_vectors = jnp.concatenate(
         [input_gain_grad[0], input_shift_grad[0], middle_gain_grad[0], middle_shift_grad[0]]
     )
     packed = jnp.concatenate([row_vectors, own_vectors]).reshape(-1, LANES)
     spare = -packed.shape[0] % 8
-    packed = jnp.concatenate([d_probe.reshape(LAT, own_width), jnp.pad(packed, ((0, spare), (0, 0)))], 0)
-    image_grads = (blocks_in(image_grad[:, :own_width]), blocks_in(image_grad[:, own_width:]), image_out_grad)
+    packed = jnp.concatenate([d_probe, jnp.pad(packed, ((0, spare), (0, 0)))], 0)
+    image_grads = (blocks_in(image_key_grad), blocks_in(image_value_grad), image_out_grad)
     owned, (spread, resample_query_grad, latent_grad) = finale(
-        list(zip(hidden_grads + layer_grads, hidden_theirs + layer_theirs)),
+        list(zip(hidden_pairs[:2] + layer_pairs[:4], hidden_pairs[2:] + layer_pairs[4:])),
         image_grads,
-        (INWARD, OUTWARD) + layer_sides,
+        (INWARD, OUTWARD, INWARD, INWARD, INWARD, OUTWARD),
         (INWARD, INWARD, OUTWARD),
         packed,
         latents.astype(f32).T,

time: 653 us -> 598 us (0.916); the launches traced: 642 us -> 599 us
  matrix products: 89.4 us -> 0 us
  Pallas kernels: 470 us -> 551 us
  other arithmetic: 37.2 us -> 17.1 us
  local copies, waits for them, and re-layouts: 30.3 us -> 16.4 us
    dot_general x26 -> x0, matrix products: 81.9 us -> none  [the longest x16 65.6 us: dot32(): return jnp.dot(left, right, preferred_element_type=jnp.float32)]
    pallas_call x4, Pallas kernels: 293 us -> 339 us  [exchange(): pl.pallas_call(kernel, out_shape=tuple(out_shapes), in_specs=in_specs, ou...]
    pallas_call x4, Pallas kernels: 43 us -> 78.9 us  [the longest x1 26.2 us: image_backward(): pl.pallas_call(kernel, out_shape=(jax.ShapeDtypeStruct((picture_width, wi...]
    convert_element_type x12 -> x2, other arithmetic: 12.9 us -> 0.53 us  [the longest x1 0.52 us: on_plane(): live_mark = live.astype(jnp.int32)]
    sub x2 -> x0, matrix products: 7.54 us -> none  [the longest x1 6.62 us: on_plane(): probs = jax.nn.softmax(jnp.where(allowed[None], scores, -1e+30), -1)]
    reduce_sum x6 -> x1, other arithmetic: 7.84 us -> 0.58 us  [on_plane(): tables = xpos_tables(jnp.sum(earlier.astype(f32), 1), own_width)]
    broadcast_in_dim x4 -> x8, other arithmetic: 2.4 us -> 9.12 us  [wide(): return vector.astype(f32)[None, :]]
    unnamed x157 -> x44, local copies, waits for them, and re-layouts: 13.2 us -> 8.13 us
  transfers between devices with their start and end apart: 1 -> 1, of which waited for: 0 -> 0; matrix products, arithmetic and copies ran while one was open for 6% -> 2% of each run, Pallas kernels for 13% -> 17%
where the time goes in v2:
time: 598 us; the launch traced here: 599 us
  Pallas kernels  551 us (92%)
  other arithmetic  17.1 us (3%)
  local copies, waits for them, and re-layouts  16.4 us (3%)
  between operations  14.5 us (2%)
    pallas_call x4, Pallas kernels, exchange(): pl.pallas_call(kernel, out_shape=tuple(out_shapes), in_specs=in_specs, ou...  339 us
    pallas_call x1, Pallas kernels, intake(): pl.pallas_call(kernel, out_shape=tuple(outs), in_specs=[ANYWHERE] * (n_ro...  71.5 us
    pallas_call x1, Pallas kernels, finale(): pl.pallas_call(kernel, out_shape=tuple(outs + small_shapes), in_specs=[ON...  56.9 us
    pallas_call x1, Pallas kernels, image_backward(): pl.pallas_call(kernel, out_shape=(jax.ShapeDtypeStruct((picture_width, wi...  26.2 us
    pallas_call x1, Pallas kernels, attend_forward(): pl.pallas_call(kernel, out_shape=(jax.ShapeDtypeStruct((rows_all, width),...  24.7 us
    pallas_call x1, Pallas kernels, image_forward(): pl.pallas_call(kernel, out_shape=(jax.ShapeDtypeStruct((images * PATCH, 2...  18.1 us
  transfers between devices with their start and end apart: 1, of which 0 were waited for; matrix products, arithmetic and copies ran while one was open for 2% of the time, Pallas kernels for 17%

profile of v2, /device:TPU:0, one launch (start us, length us, event | category | flops | bytes accessed | tf_op | source)
XLA Modules:
  0.0 599.2 jit_solution(3096401617806588035)
XLA Ops:
  7.2 0.7 broadcast_in_dim.81
  8.6 0.8 fusion.3
  9.9 1.3 broadcast_in_dim.106
  11.2 1.3 broadcast_in_dim.107
  13.1 71.5 %shard_map.417 = (bf16[4096,1024]{1,0:T(8,128)(2,1)}, bf16[1024,128]{1,0:T(8,128)(2,1)}, bf16[1024,128]{1,0:T(8,128)(2,1)}, bf16[2048,128]{1,0:T(8,128)(2,1)}, b...) custom-call(bf16[512,1024]{1,0:T(8,128)(2,1)} %bitcast.69, ...), custom_call_target="tpu_custom_call" | custom-call | tf_op jit(solution)/shard_map/pallas_call | solution.py:834
  84.6 18.1 %shard_map.418 = (bf16[4096,256]{1,0:T(8,128)(2,1)}, bf16[1024,128]{1,0:T(8,128)(2,1)}, bf16[64,128]{1,0:T(8,128)(2,1)}) custom-call(s32[16]{0:T(128)} %bitcast.100, s32[16]{0:T(128)} %get-tuple-element.192.live_ref, bf16[4096,1024]{1,0:T(8,128)(2,1)} %get-tuple-element.106.pictures_ref, bf16[1024,128]{1,0:T(8,128)(2,1)} %get-tuple-element.107.key_w, ...), custom_call_target="tpu_custom_call" | custom-call | tf_op jit(solution)/shard_map/pallas_call | solution.py:1698
  102.8 71.6 %shard_map.419 = (f32[128,2048]{1,0:T(8,128)}, bf16[1024,2048]{1,0:T(8,128)(2,1)}, bf16[8,128,512]{2,1,0:T(8,128)(2,1)}, bf16[8,512,128]{2,1,0:T(8,128)(2,1)}) custom-call(bf16[1024,128]{1,0:T(8,128)(2,1)} %get-tuple-element.111.refs_0_.placed_ref, bf16[128,2048]{1,0:T(8,128)(2,1)} %get-tuple-element.112.refs_1_.out_w, bf16[128,2048]{1,0:T(8,128)(2,1)} %bitcast.72, ...), custom_call_target="tpu_custom_call" | custom-call | tf_op jit(solution)/shard_map/pallas_call | solution.py:1454
  174.5 0.8 convert_element_type.12.refs_17_
  175.3 0.7 copy.78
  177.3 1.0 copy.71.sin_ref.refs_11_
  178.3 1.0 copy.70.cos_ref.refs_10_
  179.5 1.0 copy.72.grow_ref.refs_12_
  180.5 1.0 copy.73.column_ref.refs_13_
  182.7 24.7 %shard_map.420 = (bf16[1024,128]{1,0:T(8,128)(2,1)}, bf16[1024,128]{1,0:T(8,128)(2,1)}, bf16[1024,128]{1,0:T(8,128)(2,1)}, f32[1024,128]{1,0:T(8,128)}, f32[1024,8]{1,0:T(8,128)}, /*index=5*/f32[2,1024]{1,0:T(2,128)}) custom-call(bf16[1024,2048]{1,0:T(8,128)(2,1)} %get-tuple-element.113.normed_ref.refs_15_, bf16[2048,128]{1,0:T(8,128)(2,1)} %get-tuple-element.114.query_ref, ...), custom_call_target="tpu_custom_call" | custom-call | tf_op jit(solution)/shard_map/pallas_call | solution.py:1902
  207.4 1.4 bitcast_convert_fusion.1.refs_2_.refs_4_
  208.8 1.3 bitcast_convert_fusion.refs_3_
  210.1 80.1 %shard_map.421 = (bf16[1024,128]{1,0:T(8,128)(2,1)}, f32[1024,128]{1,0:T(8,128)}, f32[1024,128]{1,0:T(8,128)}, f32[128,2048]{1,0:T(8,128)}, bf16[1024,2048]{1,0:...) custom-call(f32[1024,128]{1,0:T(8,128)} %get-tuple-element.117.refs_0_.refs_5_, ...), custom_call_target="tpu_custom_call" | custom-call | tf_op jit(solution)/shard_map/pallas_call | solution.py:1454
  290.2 1.3 dynamic-slice_convert_fusion.2
  291.6 1.4 dynamic-slice_convert_fusion
  292.9 1.3 pad_maximum_fusion.refs_17_
  294.3 10.0 %shard_map.422 = (f32[1024,512]{1,0:T(8,128)}, f32[1024,512]{1,0:T(8,128)}, f32[1024,512]{1,0:T(8,128)}, f32[4,1024]{1,0:T(4,128)}) custom-call(bf16[1024,2048]{1,0:T(8,128)(2,1)} %get-tuple-element.123.lifted_ref.refs_6_, bf16[2048,512]{1,0:T(8,128)(2,1)} %bitcast.59, f32[1,512]{1,0:T(1,128)} %bitcast.90, ...), custom_call_target="tpu_custom_call" | custom-call | tf_op jit(solution)/shard_map/pallas_call | solution.py:1954
  304.2 86.8 %shard_map.423 = (bf16[1024,512]{1,0:T(8,128)(2,1)}, bf16[1024,512]{1,0:T(8,128)(2,1)}, f32[8,512]{1,0:T(8,128)}, bf16[8,2,128,512]{3,2,1,0:T(8,128)(2,1)}, bf16...) custom-call(f32[1024,512]{1,0:T(8,128)} %get-tuple-element.127.refs_, ...), custom_call_target="tpu_custom_call" | custom-call | tf_op jit(solution)/shard_map/pallas_call | solution.py:1454
  391.1 100.2 %shard_map.424 = (f32[8,128]{1,0:T(8,128)}, bf16[8,2,128,128]{3,2,1,0:T(8,128)(2,1)}, bf16[8,2,128,128]{3,2,1,0:T(8,128)(2,1)}, bf16[8,2,128,128]{3,2,1,0:T(8,12...) custom-call(bf16[1024,2048]{1,0:T(8,128)(2,1)} %get-tuple-element.13, ...), custom_call_target="tpu_custom_call" | custom-call | tf_op jit(solution)/shard_map/pallas_call | solution.py:1454
  494.0 0.8 fusion.8
  494.9 26.2 %shard_map.425 = (bf16[1024,128]{1,0:T(8,128)(2,1)}, bf16[1024,128]{1,0:T(8,128)(2,1)}, bf16[128,2048]{1,0:T(8,128)(2,1)}, f32[64,128]{1,0:T(8,128)}) custom-call(s32[16]{0:T(128)} %bitcast.101, s32[16]{0:T(128)} %get-tuple-element.192.live_ref, bf16[1024,2048]{1,0:T(8,128)(2,1)} %get-tuple-element.150.d_ref, ...), custom_call_target="tpu_custom_call" | custom-call | tf_op jit(solution)/shard_map/pallas_call | solution.py:1798
  521.0 1.4 select_maximum_fusion.refs_15_
  522.4 56.9 %shard_map.426 = (bf16[128,4096]{1,0:T(8,128)(2,1)}, bf16[4096,128]{1,0:T(8,128)(2,1)}, bf16[128,1024]{1,0:T(8,128)(2,1)}, bf16[128,1024]{1,0:T(8,128)(2,1)}, bf...) custom-call(bf16[8,2,128,512]{3,2,1,0:T(8,128)(2,1)} %get-tuple-elem, ...), custom_call_target="tpu_custom_call" | custom-call | tf_op jit(solution)/shard_map/pallas_call | solution.py:1613
  579.3 1.3 copy.84
  583.7 1.1 select_bitcast_fusion
  584.8 5.1 shard_map.427
  589.9 0.8 copy.96
  591.3 0.8 copy.98
  (66 shorter events, 11.0 us)
Async XLA Ops:
  7.2 287.1 %all-gather.2.cloned.1.call-start = ((), (), s32[]{:S(2)}) async-start(), calls=%async_computation | async-start | bytes 4718592 | tf_op jit(solution)/shard_map/all_gather | solution.py:2092
  102.8 71.7 %copy-start.4 = (bf16[128,1024]{1,0:T(8,128)(2,1)S(1)}, bf16[128,1024]{1,0:T(8,128)(2,1)}, u32[]{:S(2)}) copy-start(bf16[128,1024]{1,0:T(8,128)(2,1)} %refs_3_.1) | copy-start | bytes 786436
  102.8 72.5 %copy-start.7 = (bf16[64,128]{1,0:T(8,128)(2,1)S(1)}, bf16[64,128]{1,0:T(8,128)(2,1)}, u32[]{:S(2)}) copy-start(bf16[64,128]{1,0:T(8,128)(2,1)} %refs_4_.1) | copy-start | bytes 49156
  102.8 73.3 %copy-start.8 = (s32[1,1024]{1,0:T(1,128)S(1)}, s32[1,1024]{1,0:T(1,128)}, u32[]{:S(2)}) copy-start(s32[1,1024]{1,0:T(1,128)} %refs_14_.1) | copy-start | bytes 12292
  177.2 4.3 copy-start.12
  177.2 4.9 copy-start.13
  207.4 85.5 %copy-start = (bf16[2048,128]{1,0:T(8,128)(2,1)S(1)}, bf16[2048,128]{1,0:T(8,128)(2,1)}, u32[]{:S(2)}) copy-start(bf16[2048,128]{1,0:T(8,128)(2,1)} %get-tuple-element.114.query_ref) | copy-start | bytes 1572868
  207.4 85.5 %copy-start.1 = (bf16[2048,128]{1,0:T(8,128)(2,1)S(1)}, bf16[2048,128]{1,0:T(8,128)(2,1)}, u32[]{:S(2)}) copy-start(bf16[2048,128]{1,0:T(8,128)(2,1)} %get-tuple-element.115.key_ref) | copy-start | bytes 1572868
  207.4 85.5 %copy-start.2 = (bf16[2048,128]{1,0:T(8,128)(2,1)S(1)}, bf16[2048,128]{1,0:T(8,128)(2,1)}, u32[]{:S(2)}) copy-start(bf16[2048,128]{1,0:T(8,128)(2,1)} %get-tuple-element.116.value_ref) | copy-start | bytes 1572868
  391.0 101.6 %copy-start.11 = (f32[1,2048]{1,0:T(1,128)S(1)}, f32[1,2048]{1,0:T(1,128)}, u32[]{:S(2)}) copy-start(f32[1,2048]{1,0:T(1,128)} %get-tuple-element.165) | copy-start | bytes 24580
  391.0 101.6 %copy-start.10 = (f32[1,2048]{1,0:T(1,128)S(1)}, f32[1,2048]{1,0:T(1,128)}, u32[]{:S(2)}) copy-start(f32[1,2048]{1,0:T(1,128)} %get-tuple-element.166) | copy-start | bytes 24580
  522.4 61.3 %copy-start.3 = (f32[128,2048]{1,0:T(8,128)S(1)}, f32[128,2048]{1,0:T(8,128)}, u32[]{:S(2)}) copy-start(f32[128,2048]{1,0:T(8,128)} %get-tuple-element.143) | copy-start | bytes 3145732
  580.6 9.4 %copy-start.5 = (bf16[128,2048]{1,0:T(8,128)(2,1)S(1)}, bf16[128,2048]{1,0:T(8,128)(2,1)}, u32[]{:S(2)}) copy-start(bf16[128,2048]{1,0:T(8,128)(2,1)} %get-tuple-element.142) | copy-start | bytes 1572868
  583.7 7.0 %copy-start.9 = (f32[64,128]{1,0:T(8,128)S(1)}, f32[64,128]{1,0:T(8,128)}, u32[]{:S(2)}) copy-start(f32[64,128]{1,0:T(8,128)} %get-tuple-element.250) | copy-start | bytes 98308
  583.7 7.6 %copy-start.6 = (f32[128,1024]{1,0:T(8,128)S(1)}, f32[128,1024]{1,0:T(8,128)}, u32[]{:S(2)}) copy-start(f32[128,1024]{1,0:T(8,128)} %get-tuple-element.251) | copy-start | bytes 1572868
Sparse Core Ops, SparseCore 0:
  174.6 34.4 all-gather.1

commit v3 on v2

--- a/solution.py
+++ b/solution.py
@@ -577,10 +577,12 @@
 MESH_IDS = pl.DeviceIdType.MESH
 ANYWHERE = pl.BlockSpec(memory_space=pl.ANY)
 ON_CHIP = pl.BlockSpec(memory_space=pltpu.VMEM)
+IN_SMEM = pl.BlockSpec(memory_space=pltpu.SMEM)
 LANES = 128
 PLANE = 8
 VMEM_BYTES = 60 * 1024 * 1024
-PIECES = 4
+PIECE_ROWS = (32, 32, 32, 32)
+PIECES = len(PIECE_ROWS)
 FRONT, BACK, ALL, ROWS, INWARD, OUTWARD, SHARED = range(7)
 
 
@@ -627,14 +629,17 @@
     def __init__(self, here, out, block, first, count, send, recv):
         self.here, self.out, self.block = here, out, block
         self.first, self.count, self.send, self.recv = first, count, send, recv
-        self.half = count // 2
+        self.half = out.shape[1] // 2
         self.sent = []
 
+    def cut(self, ref, first, which):
+        rows = pl.ds(first, self.count)
+        if which == ALL:
+            return ref.at[rows]
+        return ref.at[rows, pl.ds(self.half if which == BACK else 0, self.half)]
+
     def part(self, seq, which):
-        first = seq * self.block + self.first
-        if which == ALL:
-            return rows_at(self.out, first, self.count)
-        return rows_at(self.out, first + (self.half if which == BACK else 0), self.half)
+        return self.cut(self.out, pl.multiple_of(seq * self.block + self.first, 16), which)
 
     def copy(self, src, dst, slot, peer):
         return remote(src, dst, self.send.at[slot], self.recv.at[slot], peer)
@@ -648,9 +653,7 @@
         here, seq = self.here, self.here.seq
 
         def own_part(which):
-            if which == ALL:
-                return rows_at(src, src_first, self.count)
-            return rows_at(src, src_first + (self.half if which == BACK else 0), self.half)
+            return self.cut(src, src_first, which)
 
         self.go(own_part(FRONT), self.part(seq, FRONT), 0, here.x)
         self.go(own_part(BACK), self.part(seq, BACK), 1, here.y)
@@ -689,18 +692,22 @@
             made.wait_send()
 
 
-def wavefront(stages, count, waiting=()):
-    waiting = list(waiting)
-    ticks = count + max(lag for lag, _ in stages)
-    share = -(-len(waiting) // max(ticks - 2, 1))
-    for tick in range(ticks):
-        for lag, stage in reversed(stages):
-            piece = tick - lag
-            if 0 <= piece < count:
-                stage(piece)
-        for launch in waiting[:share]:
-            launch()
-        del waiting[:share]
+def ticks_of(stages, count):
+    def tick_of(tick):
+        def run():
+            for lag, stage in reversed(stages):
+                if 0 <= tick - lag < count:
+                    stage(tick - lag)
+
+        return run
+
+    return [tick_of(tick) for tick in range(count + max(lag for lag, _ in stages))]
+
+
+def take_some(waiting, count):
+    for launch in waiting[:count]:
+        launch()
+    del waiting[:count]
 
 
 def weight_blocks(weight, side):
@@ -800,7 +807,7 @@
                 begin(index)
             spreads[piece][0].own(spreads[piece][1], spreads[piece][2])
 
-        wavefront(
+        for tick in ticks_of(
             [
                 (0, own_rows),
                 (2, lambda piece: spreads[piece][0].forward()),
@@ -808,7 +815,8 @@
                 (4, lambda piece: spreads[piece][0].corner()),
             ],
             len(spreads),
-        )
+        ):
+            tick()
         for index, (weight, out, side) in enumerate(zip(weight_refs, weight_outs, sides)):
             shape = weight_blocks(weight, side)
             for step in range(PLANE):
@@ -853,12 +861,39 @@
     return made[:n_rows], made[n_rows:]
 
 
+LAZY_BYTES = 256 * 1024
+
+
+class Lazy:
+    def __init__(self, src, dst, sem):
+        self.copy = pltpu.make_async_copy(src, dst, sem)
+        self.copy.start()
+        self.dst, self.shape, self.pending = dst, dst.shape, True
+
+    def ready(self):
+        if self.pending:
+            self.copy.wait()
+            self.pending = False
+        return self.dst
+
+    @property
+    def at(self):
+        return self.ready().at
+
+    def __getitem__(self, where):
+        return self.ready()[where]
+
+
+def is_lazy(value, spec):
+    return spec is ON_CHIP and value.size * value.dtype.itemsize >= LAZY_BYTES
+
+
 class Rider:
-    inputs, out_shapes, scratch = (), (), ()
+    inputs, out_shapes, scratch, in_specs = (), (), (), ()
 
     def bind(self, here, ins, outs, scratch):
         self.here, self.ins, self.outs, self.held = here, ins, outs, scratch
-        self.sent, self.kept, self.due, self.launches = [], [], [], []
+        self.sent, self.kept, self.due, self.launches, self.later = [], [], [], [], []
 
     def keep(self, src, dst, sem):
         made = pltpu.make_async_copy(src, dst, sem)
@@ -879,66 +914,60 @@
             made.wait()
 
 
-class PlaneWeights(Rider):
-    def __init__(self, weights, sides):
-        self.inputs, self.sides = weights, sides
+class ChainWeights(Rider):
+    def __init__(self, weights, sides, places):
+        self.inputs, self.sides, self.places = weights, sides, places
         self.blocks = [weight_blocks(weight, side) for weight, side in zip(weights, sides)]
-        self.out_shapes = [
-            jax.ShapeDtypeStruct((PLANE,) + block, weight.dtype) for block, weight in zip(self.blocks, weights)
-        ]
-        dma = pltpu.SemaphoreType.DMA
-        self.scratch = [dma((len(weights), PLANE)), dma((len(weights), PLANE))]
+        shapes = {}
+        for (rows, columns), side, (out, first) in zip(self.blocks, sides, places):
+            if side == INWARD:
+                shapes[out] = (2 * PLANE * rows, first + columns)
+            else:
+                shapes[out] = (rows, 2 * PLANE * columns)
+        self.out_shapes = [jax.ShapeDtypeStruct(shapes[out], weights[0].dtype) for out in range(len(shapes))]
+        dma, count = pltpu.SemaphoreType.DMA, len(weights)
+        self.scratch = [dma((count, PLANE))] * 4 + [dma((count,))]
 
     def peers(self, here):
         return [here.at(lax.rem(here.seq + step, PLANE)) for step in range(1, PLANE)]
 
+    def slot(self, index, seq, img):
+        out, first = self.places[index]
+        (rows, columns), number = self.blocks[index], seq * 2 + img
+        if self.sides[index] == INWARD:
+            return self.outs[out].at[pl.ds(pl.multiple_of(number * rows, rows), rows), pl.ds(first, columns)]
+        return self.outs[out].at[:, pl.ds(pl.multiple_of(number * columns, columns), columns)]
+
     def start(self):
-        here, (send, recv) = self.here, self.held
-        for index, (weight, out, side, block) in enumerate(zip(self.ins, self.outs, self.sides, self.blocks)):
+        here, (send, recv, z_send, z_recv, local) = self.here, self.held
+        self.later = []
+        for index, (weight, side, (rows, columns)) in enumerate(zip(self.ins, self.sides, self.blocks)):
             for step in range(PLANE):
                 target = lax.rem(here.seq + step, PLANE)
                 source = lax.rem(here.seq + PLANE - step, PLANE)
                 if side == INWARD:
-                    part = weight.at[:, pl.ds(pl.multiple_of(target * block[1], block[1]), block[1])]
+                    part = weight.at[:, pl.ds(pl.multiple_of(target * columns, columns), columns)]
                 else:
-                    part = weight.at[pl.ds(pl.multiple_of(target * block[0], block[0]), block[0])]
+                    part = weight.at[pl.ds(pl.multiple_of(target * rows, rows), rows)]
+                mine = self.slot(index, here.seq, here.img)
                 if step == 0:
-                    self.keep(part, out.at[here.seq], recv.at[index, 0])
+                    self.keep(part, mine, local.at[index])
+                    cross = remote(part, mine, z_send.at[index, 0], z_recv.at[index, 0], here.img_peer)
+                    self.launches.append(cross.start)
+                    self.sent.append(cross)
                 else:
-                    self.send(part, out.at[here.seq], send.at[index, step], recv.at[index, step], here.at(target))
-                    self.due.append((out.at[source], send.at[index, step], recv.at[index, step]))
-
-
-class CrossWeights(Rider):
-    def __init__(self, blocks, sides):
-        self.inputs, self.sides = blocks, sides
-        self.out_shapes = []
-        for block, side in zip(blocks, sides):
-            count, rows, columns = block.shape
-            shape = (count, 2, rows, columns) if side == INWARD else (rows, count * 2 * columns)
-            self.out_shapes.append(jax.ShapeDtypeStruct(shape, block.dtype))
-        dma = pltpu.SemaphoreType.DMA
-        self.scratch = [dma((len(blocks), PLANE)), dma((len(blocks), PLANE)), dma((len(blocks), PLANE))]
-
-    def peers(self, here):
-        return [here.img_peer]
-
-    def start(self):
-        here, (send, recv, local) = self.here, self.held
-        for index, (block, out, side) in enumerate(zip(self.ins, self.outs, self.sides)):
-            width = block.shape[2]
-            for seq in range(PLANE):
-
-                def place(img, seq=seq, width=width, out=out, side=side):
-                    if side == INWARD:
-                        return out.at[seq, img]
-                    return out.at[:, pl.ds(pl.multiple_of((seq * 2 + img) * width, width), width)]
-
-                self.send(
-                    block.at[seq], place(here.img), send.at[index, seq], recv.at[index, seq], here.img_peer
-                )
-                self.keep(block.at[seq], place(here.img), local.at[index, seq])
-                self.due.append((place(1 - here.img), send.at[index, seq], recv.at[index, seq]))
+                    self.send(part, mine, send.at[index, step], recv.at[index, step], here.at(target))
+                    self.later.append(functools.partial(self.cross, index, step, source))
+                there = self.slot(index, source, 1 - here.img)
+                self.due.append((there, z_send.at[index, step], z_recv.at[index, step]))
+
+    def cross(self, index, step, source):
+        here, (send, recv, z_send, z_recv, _) = self.here, self.held
+        landed = self.slot(index, source, here.img)
+        remote(landed, landed, send.at[index, step], recv.at[index, step], here.core).wait_recv()
+        made = remote(landed, landed, z_send.at[index, step], z_recv.at[index, step], here.img_peer)
+        made.start()
+        self.sent.append(made)
 
 
 class CrossGrads(Rider):
@@ -971,6 +1000,8 @@
 
 
 class Stream:
+    in_specs = ()
+
     def __init__(self, rows_all, left, right, across, row_inputs, row_kinds, row_outs, row_function, gather):
         self.own_left = left is not None
         self.inputs = ([left] if self.own_left else []) + [right] + list(row_inputs)
@@ -978,24 +1009,23 @@
         self.row_function, self.gather = row_function, gather
         width = right.shape[0] if across else right.shape[1]
         self.width, self.block, self.pieces = width, rows_all // PLANE, PIECES
-        self.count = self.block // self.pieces
-        self.half = self.count // 2
+        self.half = width // 2
         low_type = jnp.bfloat16
         self.out_shapes = [shape for shape, _ in row_outs]
         if gather:
             self.out_shapes.append(jax.ShapeDtypeStruct((rows_all, width), low_type))
         dma = pltpu.SemaphoreType.DMA
-        block, pieces, count, half = self.block, self.pieces, self.count, self.half
+        block, pieces, half = self.block, self.pieces, self.half
         self.scratch = [
             pltpu.VMEM((4, block, width), low_type),
             pltpu.VMEM((4, block, width), low_type),
             pltpu.VMEM((4, block, width), jnp.float32),
-            pltpu.VMEM((pieces, half, width), low_type),
-            pltpu.VMEM((pieces, half, width), low_type),
-            pltpu.VMEM((pieces, count, width), low_type),
-            pltpu.VMEM((pieces, count, width), low_type),
-            pltpu.VMEM((pieces, count, width), low_type),
-            pltpu.VMEM((pieces, count, width), low_type),
+            pltpu.VMEM((block, half), low_type),
+            pltpu.VMEM((block, half), low_type),
+            pltpu.VMEM((block, width), low_type),
+            pltpu.VMEM((block, width), low_type),
+            pltpu.VMEM((block, width), low_type),
+            pltpu.VMEM((block, width), low_type),
             pltpu.VMEM((block, width), low_type),
             dma((4,)),
             dma((4,)),
@@ -1067,68 +1097,75 @@
     def landed(self, dst, piece, slot):
         remote(dst, dst, self.send.at[piece, slot], self.recv.at[piece, slot], self.here.core).wait_recv()
 
+    def rows_of(self, piece):
+        return pl.ds(sum(PIECE_ROWS[:piece]), PIECE_ROWS[piece])
+
+    def columns_of(self, which):
+        return pl.ds(self.half if which == BACK else 0, self.half)
+
     def held(self, kind, piece, which=ALL):
-        first, rows = piece * self.count, self.count
-        if which != ALL:
-            first, rows = first + (self.half if which == BACK else 0), self.half
-        return self.core_in.at[kind, pl.ds(first, rows)]
+        if which == ALL:
+            return self.core_in.at[kind, self.rows_of(piece)]
+        return self.core_in.at[kind, self.rows_of(piece), self.columns_of(which)]
+
+    def halved(self, ref, piece, which):
+        return ref.at[self.rows_of(piece), self.columns_of(which)]
 
     def folded(self, kind, piece):
         if piece == 0:
             self.core_copies[kind].wait_recv()
-        near = self.near[kind, pl.ds(piece * self.count, self.count), :]
+        near = self.near[kind, self.rows_of(piece), :]
         return self.held(kind, piece)[...].astype(jnp.float32) + near
 
     def first_sends(self, piece):
-        here, half = self.here, self.half
+        here = self.here
         self.held(3, piece)[...] = self.folded(3, piece).astype(jnp.bfloat16)
-        self.go(self.held(3, piece, FRONT), self.from_xd.at[piece], piece, 0, here.x)
-        self.go(self.held(3, piece, BACK), self.from_yd.at[piece], piece, 1, here.y)
+        self.go(self.held(3, piece, FRONT), self.from_xd.at[self.rows_of(piece)], piece, 0, here.x)
+        self.go(self.held(3, piece, BACK), self.from_yd.at[self.rows_of(piece)], piece, 1, here.y)
         self.held(1, piece)[...] = self.folded(1, piece).astype(jnp.bfloat16)
-        self.go(self.held(1, piece, FRONT), self.from_x.at[piece, pl.ds(0, half)], piece, 2, here.x)
+        self.go(self.held(1, piece, FRONT), self.halved(self.from_x, piece, FRONT), piece, 2, here.x)
         self.held(2, piece)[...] = self.folded(2, piece).astype(jnp.bfloat16)
-        self.go(self.held(2, piece, BACK), self.from_y.at[piece, pl.ds(half, half)], piece, 3, here.y)
+        self.go(self.held(2, piece, BACK), self.halved(self.from_y, piece, BACK), piece, 3, here.y)
 
     def second_sends(self, piece):
-        here, half = self.here, self.half
-        self.landed(self.from_xd.at[piece], piece, 0)
+        here = self.here
+        self.landed(self.from_xd.at[self.rows_of(piece)], piece, 0)
         at = self.held(2, piece, FRONT)
-        at[...] = (at[...].astype(jnp.float32) + self.from_xd[piece].astype(jnp.float32)).astype(jnp.bfloat16)
-        self.go(at, self.from_y.at[piece, pl.ds(0, half)], piece, 4, here.y)
-        self.landed(self.from_yd.at[piece], piece, 1)
+        at[...] = (at[...].astype(jnp.float32) + self.from_xd[self.rows_of(piece), :].astype(jnp.float32)).astype(jnp.bfloat16)
+        self.go(at, self.halved(self.from_y, piece, FRONT), piece, 4, here.y)
+        self.landed(self.from_yd.at[self.rows_of(piece)], piece, 1)
         at = self.held(1, piece, BACK)
-        at[...] = (at[...].astype(jnp.float32) + self.from_yd[piece].astype(jnp.float32)).astype(jnp.bfloat16)
-        self.go(at, self.from_x.at[piece, pl.ds(half, half)], piece, 5, here.x)
+        at[...] = (at[...].astype(jnp.float32) + self.from_yd[self.rows_of(piece), :].astype(jnp.float32)).astype(jnp.bfloat16)
+        self.go(at, self.halved(self.from_x, piece, BACK), piece, 5, here.x)
 
     def plane_sum(self, piece):
-        half = self.half
-        self.landed(self.from_x.at[piece, pl.ds(0, half)], piece, 2)
-        self.landed(self.from_y.at[piece, pl.ds(half, half)], piece, 3)
-        self.landed(self.from_y.at[piece, pl.ds(0, half)], piece, 4)
-        self.landed(self.from_x.at[piece, pl.ds(half, half)], piece, 5)
+        self.landed(self.halved(self.from_x, piece, FRONT), piece, 2)
+        self.landed(self.halved(self.from_y, piece, BACK), piece, 3)
+        self.landed(self.halved(self.from_y, piece, FRONT), piece, 4)
+        self.landed(self.halved(self.from_x, piece, BACK), piece, 5)
         total = self.folded(0, piece)
-        total = total + self.from_x[piece].astype(jnp.float32) + self.from_y[piece].astype(jnp.float32)
-        self.mine[piece] = total.astype(jnp.bfloat16)
-        self.go(self.mine.at[piece], self.theirs.at[piece], piece, 6, self.here.tp_peer)
+        total = total + self.from_x[self.rows_of(piece), :].astype(jnp.float32) + self.from_y[self.rows_of(piece), :].astype(jnp.float32)
+        self.mine[self.rows_of(piece), :] = total.astype(jnp.bfloat16)
+        self.go(self.mine.at[self.rows_of(piece)], self.theirs.at[self.rows_of(piece)], piece, 6, self.here.tp_peer)
 
     def rows_done(self, piece):
         here = self.here
-        self.landed(self.theirs.at[piece], piece, 6)
-        total = self.mine[piece].astype(jnp.float32) + self.theirs[piece].astype(jnp.float32)
-        rows = pl.ds(piece * self.count, self.count)
+        self.landed(self.theirs.at[self.rows_of(piece)], piece, 6)
+        total = self.mine[self.rows_of(piece), :].astype(jnp.float32) + self.theirs[self.rows_of(piece), :].astype(jnp.float32)
+        rows = self.rows_of(piece)
         views = [ref.at[rows] if kind == ROWS else ref for ref, kind in zip(self.ins, self.row_kinds)]
         out_views = [ref.at[rows] if kind == ROWS else ref for ref, (_, kind) in zip(self.outs, self.row_outs)]
         given = self.row_function(total, piece, views, out_views)
         if self.gather:
             out = self.outs[-1]
             self.low[rows, :] = given
-            first = pl.multiple_of(here.seq * self.block + piece * self.count, 16)
-            keep = pltpu.make_async_copy(self.low.at[rows], out.at[pl.ds(first, self.count)], self.l_sem.at[piece])
+            first = pl.multiple_of(here.seq * self.block + rows.start, 16)
+            keep = pltpu.make_async_copy(self.low.at[rows], out.at[pl.ds(first, rows.size)], self.l_sem.at[piece])
             keep.start()
             spread = Spread(
-                here, out, self.block, piece * self.count, self.count, self.g_send.at[piece], self.g_recv.at[piece]
+                here, out, self.block, rows.start, rows.size, self.g_send.at[piece], self.g_recv.at[piece]
             )
-            spread.own(self.low, piece * self.count)
+            spread.own(self.low, rows.start)
             self.spreads.append((spread, keep))
 
     def stages(self):
@@ -1185,108 +1222,186 @@
         return jnp.concatenate([total, jnp.zeros((8 - count, rows), jnp.float32)], 0).T
 
 
-class InnerFront(Front):
-    def __init__(self, attended, sums, gain, shift, full_width):
-        self.inputs = [attended, sums, gain, shift]
+def chosen_rows(target_rows, first, count):
+    row = first + lax.broadcasted_iota(jnp.int32, (count, target_rows.shape[1]), 0)
+    return (row == target_rows[...]).astype(jnp.float32).astype(jnp.bfloat16)
+
+
+class ImageFront(Rider):
+    def __init__(self, pictures, key_part, value_part, latent_all, probe_part, target_rows):
+        self.inputs = [pictures, key_part, value_part, latent_all, probe_part, target_rows]
+        rows, width = pictures.shape[0], key_part.shape[1]
+        images = rows // PATCH
+        low_type = jnp.bfloat16
+        self.out_shapes = [
+            jax.ShapeDtypeStruct((rows, 2 * width), low_type),
+            jax.ShapeDtypeStruct((images * LAT, width), low_type),
+            jax.ShapeDtypeStruct((LAT, width), low_type),
+        ]
+        self.scratch = [
+            pltpu.VMEM((key_part.shape[0], 2 * width), low_type),
+            pltpu.VMEM((images * LAT, width), low_type),
+        ]
+
+    def run(self):
+        pictures, key_w, value_w, latent_all, probe_w, target_rows = self.ins
+        keys, placed, probe = self.outs
+        both_w, mixed_all = self.held
+        width, scale = probe.shape[1], HEAD ** (-0.5)
+        both_w[:, :width] = key_w[...]
+        both_w[:, width:] = value_w[...]
+        probe[...] = jnp.dot(latent_all[...], probe_w[...], preferred_element_type=jnp.float32).astype(jnp.bfloat16)
+        yield
+        for image in range(pictures.shape[0] // PATCH):
+            rows = slice(image * PATCH, (image + 1) * PATCH)
+            if image % IMAGES_A_STEP == 0:
+                more = slice(image * PATCH, (image + IMAGES_A_STEP) * PATCH)
+                keys[more, :] = jnp.dot(
+                    pictures[more, :], both_w[...], preferred_element_type=jnp.float32
+                ).astype(jnp.bfloat16)
+            mixed = []
+            for first in range(0, width, HEAD):
+                probs = image_probs_of(probe[:, first : first + HEAD], keys[rows, first : first + HEAD], scale)
+                values = keys[rows, width + first : width + first + HEAD]
+                mixed.append(jnp.dot(probs.astype(jnp.bfloat16), values, preferred_element_type=jnp.float32))
+            mixed_all[image * LAT : (image + 1) * LAT, :] = jnp.concatenate(mixed, 1).astype(jnp.bfloat16)
+            yield
+        for first in range(0, placed.shape[0], PATCH):
+            chosen = chosen_rows(target_rows, first, PATCH)
+            placed[first : first + PATCH, :] = jnp.dot(
+                chosen, mixed_all[...], preferred_element_type=jnp.float32
+            ).astype(jnp.bfloat16)
+        self.left = placed
+
+
+class AttendFront(Front):
+    def __init__(self, normed, layer_part, tables, segment, gain, shift, full_width):
+        self.inputs = [normed, layer_part, *tables, segment[:, None], segment[None, :], gain, shift]
         self.full_width = full_width
-        rows, width = attended.shape
-        self.out_shapes = [
-            jax.ShapeDtypeStruct((rows, width), jnp.bfloat16),
-            jax.ShapeDtypeStruct((rows, width), jnp.float32),
-            jax.ShapeDtypeStruct((rows, width), jnp.float32),
-        ]
-        self.scratch = self.total_scratch(sums.shape[0], rows)
+        rows, width = normed.shape[0], layer_part.shape[1] // 3
+        low_shape = jax.ShapeDtypeStruct((rows, width), jnp.bfloat16)
+        wide_shape = jax.ShapeDtypeStruct((rows, width), jnp.float32)
+        lse_shape = jax.ShapeDtypeStruct((rows, 8), jnp.float32)
+        self.out_shapes = [low_shape, low_shape, low_shape, wide_shape, lse_shape, low_shape, wide_shape, wide_shape]
+        self.scratch = self.total_scratch(2, rows)
 
     def run(self):
-        attended, sums, gain, shift = self.ins
-        low, hat, factor_out = self.outs
-        self.held[1][...] = sums[...]
-        total = self.small_sum(self.held)
-        average = total[:, 0:1] / self.full_width
-        factor = lax.rsqrt(total[:, 1:2] / self.full_width - average * average + EPSILON)
-        normal = (attended[...] - average) * factor
+        normed, layer_w, cos_ref, sin_ref, grow_ref, column_ref, row_ref, gain, shift = self.ins
+        q_out, k_out, v_out, att_out, lse_out, low, hat, factor_out = self.outs
+        rows_all, width = att_out.shape
+        scale = HEAD ** (-0.5)
+        f32, low_type = jnp.float32, jnp.bfloat16
+        for first in range(0, rows_all, ATTEND_ROWS):
+            at, keys = slice(first, first + ATTEND_ROWS), first + ATTEND_ROWS
+            cosine, sine, growth = cos_ref[at, :], sin_ref[at, :], grow_ref[at, :]
+            linear = jnp.dot(normed[at, :], layer_w[...], preferred_element_type=f32)
+            lin = linear[:, :width]
+            q_out[at, :] = ((lin * cosine + halves_swapped(lin) * sine) * growth).astype(low_type)
+            lin = linear[:, width : 2 * width]
+            k_out[at, :] = ((lin * cosine + halves_swapped(lin) * sine) * (1.0 / growth)).astype(low_type)
+            v_out[at, :] = linear[:, 2 * width :].astype(low_type)
+            allowed = allowed_part(column_ref, row_ref, first, ATTEND_ROWS, keys)
+            for head in range(width // HEAD):
+                lanes = slice(head * HEAD, (head + 1) * HEAD)
+                scores = lax.dot_general(
+                    q_out[at, lanes] * scale,
+                    k_out[:keys, lanes],
+                    (((1,), (1,)), ((), ())),
+                    preferred_element_type=f32,
+                )
+                scores = jnp.where(allowed, scores, -1e30)
+                best = jnp.max(scores, -1, keepdims=True)
+                weights = jnp.exp(scores - best)
+                total = jnp.sum(weights, -1, keepdims=True)
+                probs = (weights * (1.0 / total)).astype(low_type)
+                att_out[at, lanes] = jnp.dot(probs, v_out[:keys, lanes], preferred_element_type=f32)
+                lse_out[at, head : head + 1] = best + jnp.log(total)
+            rows = att_out[at, :]
+            sums = [jnp.sum(rows, 1, keepdims=True), jnp.sum(rows * rows, 1, keepdims=True)]
+            self.held[1][:, at] = as_lanes(sums)[:2]
+            yield
+        total = self.small_sum(self.held) / self.full_width
+        average = total[:, 0:1]
+        factor = lax.rsqrt(total[:, 1:2] - average * average + EPSILON)
+        normal = (att_out[...] - average) * factor
         hat[...] = normal
         factor_out[...] = jnp.broadcast_to(factor, normal.shape)
-        low[...] = (normal * gain[...] + shift[...]).astype(jnp.bfloat16)
-        return low
+        low[...] = (normal * gain[...] + shift[...]).astype(low_type)
+        self.left = low
 
 
 class GradFront(Front):
     def grads(self, products):
-        here = self.here
         for seq in range(PLANE):
             for product in products:
-                self.launches.append(functools.partial(self.part, product, seq))
-
-    def part(self, product, seq):
-        left, right, outs, side, theirs, send, recv = product
-        here = self.here
+                self.launches.append(functools.partial(self.part, *product, seq))
+
+    def part(self, left, right, outs, side, seq):
         span = (left.shape[1] if side == INWARD else right.shape[1]) // PLANE
         at = slice(seq * span, (seq + 1) * span)
         contract = (((0,), (0,)), ((), ()))
-        if side == INWARD:
-            made = lax.dot_general(left[:, at], right[...], contract, preferred_element_type=jnp.float32)
-        else:
-            made = lax.dot_general(left[...], right[:, at], contract, preferred_element_type=jnp.float32)
+        if side == OUTWARD:
+            outs[0][:, at] = lax.dot_general(
+                left[...], right[:, at], contract, preferred_element_type=jnp.float32
+            ).astype(jnp.bfloat16)
+            return
+        made = lax.dot_general(left[:, at], right[...], contract, preferred_element_type=jnp.float32)
         made = made.astype(jnp.bfloat16)
         half = span // 2
         for number, out in enumerate(outs):
-            if side == INWARD:
-                width = out.shape[3]
-                piece = made[:, number * width : (number + 1) * width]
-                out[seq, 0], out[seq, 1] = piece[:half], piece[half:]
-                src = out.at[seq, 1 - here.img]
-            else:
-                out[:, at] = made
-                src = out.at[:, pl.ds(pl.multiple_of((seq * 2 + 1 - here.img) * half, half), half)]
-            copy = remote(
-                src, theirs[number].at[seq], send.at[number, seq], recv.at[number, seq], here.img_peer
-            )
-            copy.start()
-            self.sent.append(copy)
-            self.due.append((theirs[number].at[seq], send.at[number, seq], recv.at[number, seq]))
-
-
-def grad_shapes(model_width, rows, side):
+            width = out.shape[3]
+            piece = made[:, number * width : (number + 1) * width]
+            out[seq, 0], out[seq, 1] = piece[:half], piece[half:]
+
+
+def grad_shape(model_width, rows, side):
     span = model_width // PLANE
-    if side == INWARD:
-        shapes = [(PLANE, 2, span // 2, rows), (PLANE, span // 2, rows)]
-    else:
-        shapes = [(rows, model_width), (PLANE, rows, span // 2)]
-    return [jax.ShapeDtypeStruct(shape, jnp.bfloat16) for shape in shapes]
+    shape = (PLANE, 2, span // 2, rows) if side == INWARD else (rows, model_width)
+    return jax.ShapeDtypeStruct(shape, jnp.bfloat16)
 
 
 class HiddenFront(GradFront):
-    def __init__(self, activated, slope, d_settled, sums, gain, shift, lifted, cotangent_all, full_width):
-        self.inputs = [activated, slope, d_settled, sums, gain, shift, lifted, cotangent_all]
+    def __init__(self, lifted, up_part, bias, cotangent_all, down_part, gain, shift, full_width):
+        self.inputs = [lifted, up_part, bias, cotangent_all, down_part, gain, shift]
         self.full_width = full_width
-        rows, width = activated.shape
-        model_width = lifted.shape[1]
+        rows, width, model_width = lifted.shape[0], up_part.shape[1], lifted.shape[1]
         low_shape = jax.ShapeDtypeStruct((rows, width), jnp.bfloat16)
-        up, up_theirs = grad_shapes(model_width, width, INWARD)
-        down, down_theirs = grad_shapes(model_width, width, OUTWARD)
         self.out_shapes = [
             low_shape,
             low_shape,
             jax.ShapeDtypeStruct((8, width), jnp.float32),
-            up,
-            down,
-            up_theirs,
-            down_theirs,
+            grad_shape(model_width, width, INWARD),
+            grad_shape(model_width, width, OUTWARD),
         ]
-        dma = pltpu.SemaphoreType.DMA
-        self.scratch = self.total_scratch(sums.shape[0], rows) + [dma((1, PLANE))] * 4
+        self.scratch = self.total_scratch(4, rows) + [pltpu.VMEM((rows, width), jnp.float32)] * 3
 
     def run(self):
-        activated, slope, d_settled, sums, gain, shift, lifted, cotangent_all = self.ins
-        settled, d_hidden, vectors, up, down, up_theirs, down_theirs = self.outs
-        self.held[1][...] = sums[...]
+        lifted, up_w, bias, cotangent_all, down_w, gain, shift = self.ins
+        settled, d_hidden, vectors, up, down = self.outs
+        activated, slope, d_settled = self.held[6:]
+        f32 = jnp.float32
+        rows = activated.shape[0]
+        step = rows // 4
+        for first in range(0, rows, step):
+            at = slice(first, first + step)
+            pre = jnp.dot(lifted[at, :], up_w[...], preferred_element_type=f32) + bias[...]
+            below = 0.5 + 0.5 * lax.erf(pre * (0.5**0.5))
+            act = pre * below
+            activated[at, :] = act
+            slope[at, :] = below + pre * jnp.exp(-0.5 * pre * pre) * (1.0 / (2.0 * jnp.pi) ** 0.5)
+            grad = lax.dot_general(
+                cotangent_all[at, :], down_w[...], (((1,), (1,)), ((), ())), preferred_element_type=f32
+            )
+            d_settled[at, :] = grad
+            scaled = grad * gain[...]
+            sums = [jnp.sum(part, 1, keepdims=True) for part in (act, act * act, scaled, scaled * act)]
+            self.held[1][:, at] = as_lanes(sums)[:4]
+            yield
         total = self.small_sum(self.held[:6]) / self.full_width
         average = total[:, 0:1]
         factor = lax.rsqrt(total[:, 1:2] - average * average + EPSILON)
         mean_scaled = total[:, 2:3]
         mean_cross = factor * (total[:, 3:4] - average * mean_scaled)
-        rows = activated.shape[0]
         step = rows // PLANE
         gain_sum = shift_sum = bias_sum = 0.0
         for first in range(0, rows, step):
@@ -1299,32 +1414,24 @@
             d_hidden[at, :] = low
             gain_sum += jnp.sum(grad * normal, 0, keepdims=True)
             shift_sum += jnp.sum(grad, 0, keepdims=True)
-            bias_sum += jnp.sum(low.astype(jnp.float32), 0, keepdims=True)
+            bias_sum += jnp.sum(low.astype(f32), 0, keepdims=True)
         vectors[...] = jnp.zeros_like(vectors)
         vectors[0:1, :], vectors[1:2, :], vectors[2:3, :] = gain_sum, shift_sum, bias_sum
-        up_send, up_recv, down_send, down_recv = self.held[6:]
-        self.grads(
-            [
-                (lifted, d_hidden, [up], INWARD, [up_theirs], up_send, up_recv),
-                (settled, cotangent_all, [down], OUTWARD, [down_theirs], down_send, down_recv),
-            ]
-        )
-        return d_hidden
-
-
-class AttendFront(GradFront):
+        self.grads([(lifted, d_hidden, [up], INWARD), (settled, cotangent_all, [down], OUTWARD)])
+        self.left = d_hidden
+
+
+class AttendBackFront(GradFront):
     def __init__(self, d_branch, out_part, hat, factor, gain, kept, tables, segment, normed, inner_low, full_width):
         self.inputs = [d_branch, out_part, hat, factor, gain, *kept, *tables]
         self.inputs += [segment[:, None], segment[None, :], normed, inner_low]
         self.full_width = full_width
         rows, width = hat.shape
         model_width = normed.shape[1]
-        low_type, f32, dma = jnp.bfloat16, jnp.float32, pltpu.SemaphoreType.DMA
-        inward, inward_theirs = grad_shapes(model_width, width, INWARD)
-        out, out_theirs = grad_shapes(model_width, width, OUTWARD)
+        low_type, f32 = jnp.bfloat16, jnp.float32
         self.out_shapes = [jax.ShapeDtypeStruct((8, width), f32)]
-        self.out_shapes += [inward, inward, inward, out, inward_theirs, inward_theirs, inward_theirs, out_theirs]
-        self.scratch = self.total_scratch(2, rows) + [dma((3, PLANE)), dma((3, PLANE)), dma((1, PLANE)), dma((1, PLANE))]
+        self.out_shapes += [grad_shape(model_width, width, INWARD)] * 3 + [grad_shape(model_width, width, OUTWARD)]
+        self.scratch = self.total_scratch(2, rows)
         self.scratch += [pltpu.VMEM((rows, width), low_type), pltpu.VMEM((rows, 3 * width), low_type)]
         self.scratch += [pltpu.VMEM((rows, width), f32)] * 4
 
@@ -1332,7 +1439,7 @@
         d_branch, out_part, hat, factor, gain, attended, q_ref, k_ref, v_ref, lse = self.ins[:10]
         cos_ref, sin_ref, grow_ref, column_ref, row_ref, normed, inner_low = self.ins[10:]
         vectors, *grads = self.outs
-        grad_send, grad_recv, out_send, out_recv, d_att, lin_out, d_inner, d_query, d_key, d_value = self.held[6:]
+        d_att, lin_out, d_inner, d_query, d_key, d_value = self.held[6:]
         rows_all, width = hat.shape
         f32, low_type = jnp.float32, jnp.bfloat16
         gain_sum = shift_sum = 0.0
@@ -1347,6 +1454,7 @@
             scaled = grad * gain[...]
             sums = [jnp.sum(scaled, 1, keepdims=True), jnp.sum(scaled * hat[at, :], 1, keepdims=True)]
             self.held[1][:, at] = as_lanes(sums)[:2]
+            yield
         vectors[...] = jnp.zeros_like(vectors)
         vectors[0:1, :], vectors[1:2, :] = gain_sum, shift_sum
         total = self.small_sum(self.held[:6]) / self.full_width
@@ -1388,6 +1496,7 @@
                     d_value[:first, lanes] += value_part[:first]
                 d_key[first:keys, lanes] = key_part[first:]
                 d_value[first:keys, lanes] = value_part[first:]
+                yield
         for first in range(0, rows_all, ATTEND_ROWS):
             at = slice(first, first + ATTEND_ROWS)
             cosine, sine, growth = cos_ref[at, :], sin_ref[at, :], grow_ref[at, :]
@@ -1398,70 +1507,121 @@
             lin_out[at, 2 * width :] = d_value[at, :].astype(low_type)
         self.grads(
             [
-                (normed, lin_out, grads[:3], INWARD, grads[4:7], grad_send, grad_recv),
-                (inner_low, d_branch, grads[3:4], OUTWARD, grads[7:], out_send, out_recv),
+                (normed, lin_out, grads[:3], INWARD),
+                (inner_low, d_branch, grads[3:], OUTWARD),
             ]
         )
-        return lin_out
-
-
-def exchange(front, streams, riders, cid):
+        self.left = lin_out
+
+
+def lazy_call(kernel, inputs, in_specs, out_shapes, out_specs, scratch, cid):
+    late = [is_lazy(value, spec) for value, spec in zip(inputs, in_specs)]
+    buffers = [pltpu.VMEM(value.shape, value.dtype) for value, flag in zip(inputs, late) if flag]
+    n_in, n_out, n_scratch, n_late = len(inputs), len(out_shapes), len(scratch), len(buffers)
+
+    def body(*refs):
+        refs = list(refs)
+        ins, outs, held = refs[:n_in], refs[n_in : n_in + n_out], refs[n_in + n_out : n_in + n_out + n_scratch]
+        spare, sems = refs[n_in + n_out + n_scratch : -1], refs[-1]
+        lazies = []
+        for number, flag in enumerate(late):
+            if flag:
+                ins[number] = Lazy(ins[number], spare[len(lazies)], sems.at[len(lazies)])
+                lazies.append(ins[number])
+        kernel(ins, outs, held)
+        for item in lazies:
+            item.ready()
+
+    return pl.pallas_call(
+        body,
+        out_shape=tuple(out_shapes),
+        in_specs=[ANYWHERE if flag else spec for spec, flag in zip(in_specs, late)],
+        out_specs=tuple(out_specs),
+        scratch_shapes=list(scratch) + buffers + [pltpu.SemaphoreType.DMA((max(n_late, 1),))],
+        compiler_params=pltpu.CompilerParams(
+            collective_id=cid, has_side_effects=True, vmem_limit_bytes=VMEM_BYTES
+        ),
+    )(*inputs)
+
+
+def exchange(front, streams, riders, cid, early=None, pace=1, early_pace=3):
     fronts = [front] if front is not None else []
-    parts = fronts + list(streams) + list(riders)
-
-    def kernel(*refs):
+    earlies = [early] if early is not None else []
+    sums = list(streams) + earlies
+    parts = fronts + sums + list(riders)
+
+    def kernel(ins, outs, held):
         here = Places()
-        refs = list(refs)
-
-        def take(count):
+        ins, outs, held = list(ins), list(outs), list(held)
+
+        def take(refs, count):
             taken = refs[:count]
             del refs[:count]
             return taken
 
-        ins = [take(len(part.inputs)) for part in parts]
-        outs = [take(len(part.out_shapes)) for part in parts]
-        for part, part_ins, part_outs in zip(parts, ins, outs):
-            part.bind(here, part_ins, part_outs, take(len(part.scratch)))
-        wide_parts = fronts + [rider for rider in riders if isinstance(rider, PlaneWeights)]
+        for part in parts:
+            part.bind(
+                here, take(ins, len(part.inputs)), take(outs, len(part.out_shapes)), take(held, len(part.scratch))
+            )
+        wide_parts = [part for part in parts if isinstance(part, (Front, ChainWeights))]
         peers = [here.tp_peer]
-        if isinstance(front, GradFront) or any(not isinstance(rider, PlaneWeights) for rider in riders):
+        if riders:
             peers.append(here.img_peer)
         if wide_parts:
             peers += wide_parts[0].peers(here)
         else:
             peers += [here.core, here.x, here.y]
         greet(peers)
-        if front is not None:
-            streams[0].left = front.run()
-        streams[0].begin()
+        waiting, crossing = [], []
         for rider in riders:
             rider.start()
-        for stream in streams[1:]:
+            if rider.later:
+                take_some(rider.launches, len(rider.launches))
+            waiting += rider.launches + rider.later
+        early_ticks = []
+        if early is not None:
+            early.begin()
+            early_ticks = ticks_of(early.stages(), PIECES)
+        if front is not None:
+            for number, _ in enumerate(front.run()):
+                take_some(waiting, pace)
+                if number % early_pace == 0:
+                    take_some(early_ticks, 1)
+            streams[0].left = front.left
+            waiting += front.launches
+        for stream in streams:
             stream.begin()
         stages = []
         for stream in reversed(streams):
             stages += stream.stages()
-        wavefront(stages, PIECES, [launch for part in fronts + list(riders) for launch in part.launches])
+        ticks = ticks_of(stages, PIECES)
+        share = -(-len(waiting) // max(len(ticks) - 2, 1))
+        for tick in ticks:
+            tick()
+            take_some(early_ticks, 1)
+            take_some(waiting, share)
+        take_some(early_ticks, len(early_ticks))
         for part in parts:
             part.finish()
 
-    out_shapes = [shape for part in parts for shape in part.out_shapes]
-    in_specs = [ON_CHIP] * sum(len(part.inputs) for part in fronts + list(streams))
+    in_specs = []
+    for part in fronts + sums:
+        in_specs += part.in_specs or [ON_CHIP] * len(part.inputs)
     in_specs += [ANYWHERE] * sum(len(rider.inputs) for rider in riders)
     out_specs = [ON_CHIP for part in fronts for _ in part.out_shapes]
-    out_specs += [spec for stream in streams for spec in stream.out_specs()]
+    out_specs += [spec for stream in sums for spec in stream.out_specs()]
     out_specs += [ANYWHERE] * sum(len(rider.out_shapes) for rider in riders)
-    made = pl.pallas_call(
-        kernel,
-        out_shape=tuple(out_shapes),
-        in_specs=in_specs,
-        out_specs=tuple(out_specs),
-        scratch_shapes=[item for part in parts for item in part.scratch],
-        compiler_params=pltpu.CompilerParams(
-            collective_id=cid, has_side_effects=True, vmem_limit_bytes=VMEM_BYTES
-        ),
-    )(*[value for part in parts for value in part.inputs])
-    made = list(made)
+    made = list(
+        lazy_call(
+            kernel,
+            [value for part in parts for value in part.inputs],
+            in_specs,
+            [shape for part in parts for shape in part.out_shapes],
+            out_specs,
+            [item for part in parts for item in part.scratch],
+            cid,
+        )
+    )
     split = []
     for part in parts:
         split.append(made[: len(part.out_shapes)])
@@ -1469,41 +1629,48 @@
     return split
 
 
-def finale(pairs, late, sides, late_sides, small, latents_t, query_rows, cid):
-    n, n_late = len(sides), len(late_sides)
-    all_sides = list(sides) + list(late_sides)
-    grads = [grad for grad, _ in pairs] + list(late)
-
-    def block_shape(grad, side):
-        if side == INWARD:
-            return (grad.shape[2], grad.shape[3])
-        return (grad.shape[0], grad.shape[1] // (2 * PLANE))
-
-    blocks = [block_shape(grad, side) for grad, side in zip(grads, all_sides)]
-    total = n + n_late
-
-    def kernel(*refs):
-        refs = list(refs)
+def finale(pairs, sides, raw, raw_sides, image, vectors, latents_t, query_rows, cid):
+    f32, low_type, dma = jnp.float32, jnp.bfloat16, pltpu.SemaphoreType.DMA
+    d_rows, pictures, keys, probe, placed, out_part, target_rows = image
+    width, model_width, picture_width = probe.shape[1], d_rows.shape[1], pictures.shape[1]
+    images = pictures.shape[0] // PATCH
+    image_shapes = [
+        grad_shape(picture_width, width, INWARD),
+        grad_shape(picture_width, width, INWARD),
+        grad_shape(model_width, width, OUTWARD),
+    ]
+    all_sides = list(sides) + list(raw_sides) + [INWARD, INWARD, OUTWARD]
+    n, n_raw, n_image = len(sides), len(raw_sides), len(image_shapes)
+    total = n + n_raw + n_image
+    shapes = [grad.shape for grad, _ in pairs] + [grad.shape for grad in raw] + [item.shape for item in image_shapes]
+    blocks = [
+        shape[2:] if side == INWARD else (shape[0], shape[1] // (2 * PLANE)) for shape, side in zip(shapes, all_sides)
+    ]
+    small_shape = (LAT + vectors.shape[0], LANES)
+
+    def kernel(ins, outs, held):
+        refs = list(ins) + list(outs) + list(held)
 
         def take(count):
             taken = refs[:count]
             del refs[:count]
             return taken
 
-        grad_refs = take(total)
+        target_ref, d_ref, pictures_ref, keys_ref, probe_ref, placed_ref, out_w = take(7)
+        grad_refs = take(n + n_raw)
         theirs = take(n)
-        small_ref, latents_ref, query_ref = take(3)
+        vectors_ref, latents_ref, query_ref = take(3)
         out_refs = take(total)
         sums_out, query_out, latent_out = take(3)
-        late_theirs = take(n_late)
+        grad_refs += take(n_image)
+        theirs += take(n_raw + n_image)
         summed = take(total)
-        small_theirs, small_mine, small_all, lat_mine, lat_theirs = take(5)
+        small_own, small_theirs, small_mine, small_all, lat_mine, lat_theirs, d_mixed, d_both = take(8)
         z_send, z_recv, send, recv, local, s_send, s_recv = take(7)
         here = Places()
         seq, img = here.seq, here.img
         ring = [here.at(lax.rem(seq + step, PLANE)) for step in range(1, PLANE)]
         greet(ring + [here.img_peer, here.tp_peer])
-        theirs = theirs + late_theirs
 
         def part_of(index, to_seq, to_img):
             ref, block = grad_refs[index], blocks[index]
@@ -1518,9 +1685,8 @@
             return ref.at[pl.ds(pl.multiple_of(from_seq * block[0], block[0]), block[0])]
 
         waits, crossings = [], {}
-        small_cross = remote(small_ref, small_theirs, s_send.at[0], s_recv.at[0], here.img_peer)
-        small_cross.start()
-        for index in range(n, total):
+
+        def cross(index):
             for step in range(PLANE):
                 target = lax.rem(seq + step, PLANE)
                 made = remote(
@@ -1533,223 +1699,48 @@
                 made.start()
                 crossings[index, step] = made
 
-        def deliver(index):
-            for step in range(PLANE):
-                target = lax.rem(seq + step, PLANE)
-                if index >= n:
-                    crossings[index, step].wait_recv()
-                mine = part_of(index, target, img)[...].astype(jnp.float32)
-                summed[index][target] = (mine + theirs[index][target].astype(jnp.float32)).astype(jnp.bfloat16)
-                if step == 0:
-                    made = pltpu.make_async_copy(summed[index].at[target], slot_of(index, seq), local.at[index])
-                    made.start()
-                    waits.append(made.wait)
-                    continue
-                made = remote(
-                    summed[index].at[target],
-                    slot_of(index, seq),
-                    send.at[index, step],
-                    recv.at[index, step],
-                    here.at(target),
-                )
+        def deliver(index, step):
+            target = lax.rem(seq + step, PLANE)
+            if index >= n:
+                crossings[index, step].wait_recv()
+            mine = part_of(index, target, img)[...].astype(f32)
+            summed[index][target] = (mine + theirs[index][target].astype(f32)).astype(low_type)
+            if step == 0:
+                made = pltpu.make_async_copy(summed[index].at[target], slot_of(index, seq), local.at[index])
                 made.start()
-                waits.append(made.wait_send)
-
-        deliver(0)
-        small_cross.wait()
-        small_mine[...] = small_ref[...] + small_theirs[...]
-        small_all[seq] = small_mine[...]
-        small_copies = []
-        for step, peer in enumerate(ring, 1):
-            made = remote(small_mine, small_all.at[seq], s_send.at[step], s_recv.at[step], peer)
+                waits.append(made.wait)
+                return
+            made = remote(
+                summed[index].at[target], slot_of(index, seq), send.at[index, step], recv.at[index, step], here.at(target)
+            )
             made.start()
-            small_copies.append(made)
-        for index in range(1, total):
-            deliver(index)
-        for made in small_copies:
-            made.wait()
-        sums_out[...] = small_all[...]
-        rows = latents_ref.shape[1]
-        latent_part = jnp.zeros(lat_mine.shape, jnp.float32)
-        columns = small_all.shape[2]
-        for source in range(PLANE):
-            probe = small_all[source, :rows, :]
-            at = slice(source * columns, (source + 1) * columns)
-            query_out[:, at] = jnp.dot(
-                latents_ref[...], probe, precision=HIGHEST_PRECISION, preferred_element_type=jnp.float32
-            )
-            latent_part += lax.dot_general(
-                probe,
-                query_ref[:, at],
-                (((1,), (1,)), ((), ())),
-                precision=HIGHEST_PRECISION,
-                preferred_element_type=jnp.float32,
-            )
-        lat_mine[...] = latent_part
-        last = remote(lat_mine, lat_theirs, s_send.at[PLANE], s_recv.at[PLANE], here.tp_peer)
-        last.start()
-        last.wait()
-        latent_out[...] = lat_mine[...] + lat_theirs[...]
-        for index in range(total):
-            for step in range(1, PLANE):
-                source = lax.rem(seq + PLANE - step, PLANE)
-                at = slot_of(index, source)
-                remote(at, at, send.at[index, step], recv.at[index, step], here.core).wait_recv()
-        for wait in waits:
-            wait()
-        for made in crossings.values():
-            made.wait_send()
-
-    dma, low_type, f32 = pltpu.SemaphoreType.DMA, jnp.bfloat16, jnp.float32
-    outs = []
-    for block, side in zip(blocks, all_sides):
-        shape = (block[0], PLANE * block[1]) if side == INWARD else (PLANE * block[0], block[1])
-        outs.append(jax.ShapeDtypeStruct(shape, low_type))
-    small_shapes = [
-        jax.ShapeDtypeStruct((PLANE,) + small.shape, f32),
-        jax.ShapeDtypeStruct(query_rows.shape, f32),
-        jax.ShapeDtypeStruct((latents_t.shape[1], latents_t.shape[0]), f32),
-    ]
-    made = pl.pallas_call(
-        kernel,
-        out_shape=tuple(outs + small_shapes),
-        in_specs=[ON_CHIP] * (total + n + 3),
-        out_specs=tuple([ANYWHERE] * total + [ON_CHIP] * 3),
-        scratch_shapes=[pltpu.VMEM((PLANE,) + block, low_type) for block in blocks[n:]]
-        + [pltpu.VMEM((PLANE,) + block, low_type) for block in blocks]
-        + [
-            pltpu.VMEM(small.shape, f32),
-            pltpu.VMEM(small.shape, f32),
-            pltpu.VMEM((PLANE,) + small.shape, f32),
-            pltpu.VMEM((latents_t.shape[1], latents_t.shape[0]), f32),
-            pltpu.VMEM((latents_t.shape[1], latents_t.shape[0]), f32),
-            dma((n_late, PLANE)),
-            dma((n_late, PLANE)),
-            dma((total, PLANE)),
-            dma((total, PLANE)),
-            dma((total,)),
-            dma((PLANE + 1,)),
-            dma((PLANE + 1,)),
-        ],
-        compiler_params=pltpu.CompilerParams(
-            collective_id=cid, has_side_effects=True, vmem_limit_bytes=VMEM_BYTES
-        ),
-    )(*grads, *[given for _, given in pairs], small, latents_t, query_rows)
-    return made[:total], made[total:]
-
-
-def widened(arrays):
-    def kernel(*refs):
-        for src, dst in zip(refs[: len(arrays)], refs[len(arrays) :]):
-            dst[...] = src[...].astype(jnp.float32)
-
-    return pl.pallas_call(
-        kernel,
-        out_shape=tuple(jax.ShapeDtypeStruct(array.shape, jnp.float32) for array in arrays),
-        in_specs=[ON_CHIP] * len(arrays),
-        out_specs=tuple([ON_CHIP] * len(arrays)),
-        compiler_params=pltpu.CompilerParams(vmem_limit_bytes=VMEM_BYTES),
-    )(*arrays)
-
-
-IMAGES_A_STEP = 4
-
-
-def image_probs_of(probe, keys, scale):
-    scores = lax.dot_general(
-        probe * scale, keys, (((1,), (1,)), ((), ())), preferred_element_type=jnp.float32
-    )
-    weights = jnp.exp(scores - jnp.max(scores, -1, keepdims=True))
-    return weights * (1.0 / jnp.sum(weights, -1, keepdims=True))
-
-
-def image_forward(pictures, key_part, value_part, latent_all, probe_part, slots, live):
-    images, width = slots.shape[0], key_part.shape[1]
-    scale = HEAD ** (-0.5)
-    step = IMAGES_A_STEP * PATCH
-
-    def kernel(slots_ref, live_ref, pictures_ref, key_w, value_w, latent_ref, probe_w, keys, placed, probe, both_w):
-        number = pl.program_id(0)
-
-        @pl.when(number == 0)
-        def _():
-            probe[...] = jnp.dot(latent_ref[...], probe_w[...], preferred_element_type=jnp.float32).astype(
-                jnp.bfloat16
-            )
-            both_w[:, :width] = key_w[...]
-            both_w[:, width:] = value_w[...]
-
-        keys[...] = jnp.dot(pictures_ref[...], both_w[...], preferred_element_type=jnp.float32).astype(jnp.bfloat16)
-        for image in range(IMAGES_A_STEP):
-            slot = number * IMAGES_A_STEP + image
-            alive = (live_ref[slot] > 0).astype(jnp.float32)
-            rows = slice(image * PATCH, (image + 1) * PATCH)
-            mixed = []
-            for first in range(0, width, HEAD):
-                probs = image_probs_of(probe[:, first : first + HEAD], keys[rows, first : first + HEAD], scale)
-                values = keys[rows, width + first : width + first + HEAD]
-                mixed.append(jnp.dot(probs.astype(jnp.bfloat16), values, preferred_element_type=jnp.float32))
-            at = pl.ds(pl.multiple_of(slots_ref[slot] * LAT, LAT), LAT)
-            placed[at, :] = (jnp.concatenate(mixed, 1) * alive).astype(jnp.bfloat16)
-
-    def whole(shape):
-        return pl.BlockSpec(shape, lambda i, slots, live: (0, 0))
-
-    return pl.pallas_call(
-        kernel,
-        out_shape=(
-            jax.ShapeDtypeStruct((images * PATCH, 2 * width), jnp.bfloat16),
-            jax.ShapeDtypeStruct((images * LAT, width), jnp.bfloat16),
-            jax.ShapeDtypeStruct((LAT, width), jnp.bfloat16),
-        ),
-        grid_spec=pltpu.PrefetchScalarGridSpec(
-            num_scalar_prefetch=2,
-            grid=(images // IMAGES_A_STEP,),
-            in_specs=[
-                pl.BlockSpec((step, pictures.shape[1]), lambda i, slots, live: (i, 0)),
-                whole(key_part.shape),
-                whole(value_part.shape),
-                whole(latent_all.shape),
-                whole(probe_part.shape),
-            ],
-            out_specs=(
-                pl.BlockSpec((step, 2 * width), lambda i, slots, live: (i, 0)),
-                whole((images * LAT, width)),
-                whole((LAT, width)),
-            ),
-            scratch_shapes=[pltpu.VMEM((key_part.shape[0], 2 * width), jnp.bfloat16)],
-        ),
-        compiler_params=pltpu.CompilerParams(vmem_limit_bytes=VMEM_BYTES),
-    )(slots, live, pictures, key_part, value_part, latent_all, probe_part)
-
-
-def image_backward(d_rows, pictures, keys, probe, placed, out_part, slots, live):
-    images, width = slots.shape[0], probe.shape[1]
-    model_width, picture_width = d_rows.shape[1], pictures.shape[1]
-    scale = HEAD ** (-0.5)
-    f32, low_type = jnp.float32, jnp.bfloat16
-    step = IMAGES_A_STEP * PATCH
-    steps = images // IMAGES_A_STEP
-
-    def kernel(slots_ref, live_ref, d_ref, pictures_ref, keys_ref, probe_ref, placed_ref, out_w, *rest):
-        key_out, value_out, out_out, probe_out, both_sum, d_mixed, d_both = rest
-        number = pl.program_id(0)
-
-        @pl.when(number == 0)
-        def _():
-            probe_out[...] = jnp.zeros_like(probe_out)
-            d_mixed[...] = lax.dot_general(
-                d_ref[...], out_w[...], (((1,), (1,)), ((), ())), preferred_element_type=f32
+            waits.append(made.wait_send)
+
+        for index in range(n, n + n_raw):
+            cross(index)
+        waiting = [functools.partial(deliver, index, step) for index in range(n + n_raw) for step in range(PLANE)]
+
+        scale = HEAD ** (-0.5)
+        d_slots = jnp.zeros(d_mixed.shape, f32)
+        for first in range(0, d_ref.shape[0], PATCH):
+            d_part = lax.dot_general(
+                d_ref[first : first + PATCH, :], out_w[...], (((1,), (1,)), ((), ())), preferred_element_type=f32
             ).astype(low_type)
-            out_out[...] = lax.dot_general(
-                placed_ref[...], d_ref[...], (((0,), (0,)), ((), ())), preferred_element_type=f32
+            chosen = chosen_rows(target_ref, first, PATCH)
+            d_slots += lax.dot_general(chosen, d_part, (((0,), (0,)), ((), ())), preferred_element_type=f32)
+        d_mixed[...] = d_slots.astype(low_type)
+        take_some(waiting, 1)
+        for first in range(0, model_width, 512):
+            at = slice(first, first + 512)
+            grad_refs[total - 1][:, at] = lax.dot_general(
+                placed_ref[...], d_ref[:, at], (((0,), (0,)), ((), ())), preferred_element_type=f32
             ).astype(low_type)
-
-        for image in range(IMAGES_A_STEP):
-            slot = number * IMAGES_A_STEP + image
-            alive = (live_ref[slot] > 0).astype(low_type)
-            rows = slice(image * PATCH, (image + 1) * PATCH)
-            d_here = d_mixed[pl.ds(pl.multiple_of(slots_ref[slot] * LAT, LAT), LAT), :] * alive
+            take_some(waiting, 1)
+        cross(total - 1)
+        d_probe_sum = jnp.zeros(probe_ref.shape, f32)
+        for number in range(images):
+            rows = slice(number * PATCH, (number + 1) * PATCH)
+            d_here = d_mixed[number * LAT : (number + 1) * LAT, :]
             d_probe = []
             for first in range(0, width, HEAD):
                 at = slice(first, first + HEAD)
@@ -1771,63 +1762,150 @@
                 d_both[rows, width + first : width + first + HEAD] = lax.dot_general(
                     probs.astype(low_type), d_here[:, at], (((0,), (0,)), ((), ())), preferred_element_type=f32
                 ).astype(low_type)
-            probe_out[...] += jnp.concatenate(d_probe, 1)
-        part = lax.dot_general(
-            pictures_ref[...], d_both[...], (((0,), (0,)), ((), ())), preferred_element_type=f32
-        )
-
-        @pl.when(number == 0)
-        def _():
-            both_sum[...] = part
-
-        @pl.when(number > 0)
-        def _():
-            both_sum[...] += part
-
-        @pl.when(number == steps - 1)
-        def _():
-            key_out[...] = both_sum[:, :width].astype(low_type)
-            value_out[...] = both_sum[:, width:].astype(low_type)
-
-    def whole(shape):
-        return pl.BlockSpec(shape, lambda i, slots, live: (0, 0))
-
-    def stepped(columns):
-        return pl.BlockSpec((step, columns), lambda i, slots, live: (i, 0))
+            d_probe_sum += jnp.concatenate(d_probe, 1)
+            take_some(waiting, 2)
+        small_own[:LAT, :] = d_probe_sum
+        small_own[LAT:, :] = vectors_ref[...]
+        small_cross = remote(small_own, small_theirs, s_send.at[0], s_recv.at[0], here.img_peer)
+        small_cross.start()
+        span = picture_width // PLANE
+        for part in range(PLANE):
+            made = lax.dot_general(
+                pictures_ref[:, part * span : (part + 1) * span],
+                d_both[...],
+                (((0,), (0,)), ((), ())),
+                preferred_element_type=f32,
+            ).astype(low_type)
+            for kind in range(2):
+                piece = made[:, kind * width : (kind + 1) * width]
+                grad_refs[n + n_raw + kind][part, 0] = piece[: span // 2]
+                grad_refs[n + n_raw + kind][part, 1] = piece[span // 2 :]
+            take_some(waiting, 2)
+        for kind in range(2):
+            cross(n + n_raw + kind)
+        small_cross.wait()
+        small_mine[...] = small_own[...] + small_theirs[...]
+        small_all[seq] = small_mine[...]
+        small_copies = []
+        for step, peer in enumerate(ring, 1):
+            made = remote(small_mine, small_all.at[seq], s_send.at[step], s_recv.at[step], peer)
+            made.start()
+            small_copies.append(made)
+        take_some(waiting, len(waiting))
+        for index in (total - 1, total - 3, total - 2):
+            for step in range(PLANE):
+                deliver(index, step)
+        for made in small_copies:
+            made.wait()
+        sums_out[...] = small_all[...]
+        latent_part = jnp.zeros(lat_mine.shape, f32)
+        for source in range(PLANE):
+            given = small_all[source, :LAT, :]
+            at = slice(source * width, (source + 1) * width)
+            query_out[:, at] = jnp.dot(
+                latents_ref[...], given, precision=HIGHEST_PRECISION, preferred_element_type=f32
+            )
+            latent_part += lax.dot_general(
+                given,
+                query_ref[:, at],
+                (((1,), (1,)), ((), ())),
+                precision=HIGHEST_PRECISION,
+                preferred_element_type=f32,
+            )
+        lat_mine[...] = latent_part
+        last = remote(lat_mine, lat_theirs, s_send.at[PLANE], s_recv.at[PLANE], here.tp_peer)
+        last.start()
+        last.wait()
+        latent_out[...] = lat_mine[...] + lat_theirs[...]
+        for index in range(total):
+            for step in range(1, PLANE):
+                source = lax.rem(seq + PLANE - step, PLANE)
+                at = slot_of(index, source)
+                remote(at, at, send.at[index, step], recv.at[index, step], here.core).wait_recv()
+        for wait in waits:
+            wait()
+        for made in crossings.values():
+            made.wait_send()
+
+    outs = []
+    for block, side in zip(blocks, all_sides):
+        shape = (block[0], PLANE * block[1]) if side == INWARD else (PLANE * block[0], block[1])
+        outs.append(jax.ShapeDtypeStruct(shape, low_type))
+    lat_shape = (latents_t.shape[1], latents_t.shape[0])
+    small_shapes = [
+        jax.ShapeDtypeStruct((PLANE,) + small_shape, f32),
+        jax.ShapeDtypeStruct(query_rows.shape, f32),
+        jax.ShapeDtypeStruct(lat_shape, f32),
+    ]
+    n_cross = n_raw + n_image
+    made = lazy_call(
+        kernel,
+        [
+            target_rows,
+            d_rows,
+            pictures,
+            keys,
+            probe,
+            placed,
+            out_part,
+            *[grad for grad, _ in pairs],
+            *raw,
+            *[given for _, given in pairs],
+            vectors,
+            latents_t,
+            query_rows,
+        ],
+        [ON_CHIP] * (7 + n + n_raw + n + 3),
+        outs + small_shapes,
+        [ANYWHERE] * total + [ON_CHIP] * 3,
+        [pltpu.VMEM(item.shape, low_type) for item in image_shapes]
+        + [pltpu.VMEM((PLANE,) + tuple(block), low_type) for block in blocks[n:]]
+        + [pltpu.VMEM((PLANE,) + tuple(block), low_type) for block in blocks]
+        + [
+            pltpu.VMEM(small_shape, f32),
+            pltpu.VMEM(small_shape, f32),
+            pltpu.VMEM(small_shape, f32),
+            pltpu.VMEM((PLANE,) + small_shape, f32),
+            pltpu.VMEM(lat_shape, f32),
+            pltpu.VMEM(lat_shape, f32),
+            pltpu.VMEM((d_rows.shape[0], width), low_type),
+            pltpu.VMEM((images * PATCH, 2 * width), low_type),
+            dma((n_cross, PLANE)),
+            dma((n_cross, PLANE)),
+            dma((total, PLANE)),
+            dma((total, PLANE)),
+            dma((total,)),
+            dma((PLANE + 1,)),
+            dma((PLANE + 1,)),
+        ],
+        cid,
+    )
+    return made[:total], made[total:]
+
+
+def widened(arrays):
+    def kernel(*refs):
+        for src, dst in zip(refs[: len(arrays)], refs[len(arrays) :]):
+            dst[...] = src[...].astype(jnp.float32)
 
     return pl.pallas_call(
         kernel,
-        out_shape=(
-            jax.ShapeDtypeStruct((picture_width, width), low_type),
-            jax.ShapeDtypeStruct((picture_width, width), low_type),
-            jax.ShapeDtypeStruct((width, model_width), low_type),
-            jax.ShapeDtypeStruct((LAT, width), f32),
-        ),
-        grid_spec=pltpu.PrefetchScalarGridSpec(
-            num_scalar_prefetch=2,
-            grid=(steps,),
-            in_specs=[
-                whole(d_rows.shape),
-                stepped(picture_width),
-                stepped(2 * width),
-                whole(probe.shape),
-                whole(placed.shape),
-                whole(out_part.shape),
-            ],
-            out_specs=(
-                whole((picture_width, width)),
-                whole((picture_width, width)),
-                whole((width, model_width)),
-                whole((LAT, width)),
-            ),
-            scratch_shapes=[
-                pltpu.VMEM((picture_width, 2 * width), f32),
-                pltpu.VMEM((d_rows.shape[0], width), low_type),
-                pltpu.VMEM((step, 2 * width), low_type),
-            ],
-        ),
+        out_shape=tuple(jax.ShapeDtypeStruct(array.shape, jnp.float32) for array in arrays),
+        in_specs=[ON_CHIP] * len(arrays),
+        out_specs=tuple([ON_CHIP] * len(arrays)),
         compiler_params=pltpu.CompilerParams(vmem_limit_bytes=VMEM_BYTES),
-    )(slots, live, d_rows, pictures, keys, probe, placed, out_part)
+    )(*arrays)
+
+
+IMAGES_A_STEP = 4
+
+
+def image_probs_of(probe, keys, scale):
+    scores = lax.dot_general(
+        probe * scale, keys, (((1,), (1,)), ((), ())), preferred_element_type=jnp.float32
+    )
+    weights = jnp.exp(scores - jnp.max(scores, -1, keepdims=True))
+    return weights * (1.0 / jnp.sum(weights, -1, keepdims=True))
 
 
 def xpos_tables(position, width):
@@ -1858,63 +1936,6 @@
 ATTEND_ROWS = 256
 
 
-def attend_forward(normed, query_w, key_w, value_w, tables, segment):
-    rows_all, width = normed.shape[0], query_w.shape[1]
-    heads = width // HEAD
-    scale = HEAD ** (-0.5)
-    f32, low_type = jnp.float32, jnp.bfloat16
-
-    def kernel(normed_ref, query_ref, key_ref, value_ref, cos_ref, sin_ref, grow_ref, column_ref, row_ref, *outs):
-        q_out, k_out, v_out, att_out, lse_out, stat_out = outs
-        for first in range(0, rows_all, ATTEND_ROWS):
-            at = slice(first, first + ATTEND_ROWS)
-            rows = normed_ref[at, :]
-            cosine, sine, growth = cos_ref[at, :], sin_ref[at, :], grow_ref[at, :]
-            lin = jnp.dot(rows, query_ref[...], preferred_element_type=f32)
-            q_out[at, :] = ((lin * cosine + halves_swapped(lin) * sine) * growth).astype(low_type)
-            lin = jnp.dot(rows, key_ref[...], preferred_element_type=f32)
-            k_out[at, :] = ((lin * cosine + halves_swapped(lin) * sine) * (1.0 / growth)).astype(low_type)
-            v_out[at, :] = jnp.dot(rows, value_ref[...], preferred_element_type=f32).astype(low_type)
-        for first in range(0, rows_all, ATTEND_ROWS):
-            at, keys = slice(first, first + ATTEND_ROWS), first + ATTEND_ROWS
-            allowed = allowed_part(column_ref, row_ref, first, ATTEND_ROWS, keys)
-            for head in range(heads):
-                lanes = slice(head * HEAD, (head + 1) * HEAD)
-                scores = lax.dot_general(
-                    q_out[at, lanes] * scale,
-                    k_out[:keys, lanes],
-                    (((1,), (1,)), ((), ())),
-                    preferred_element_type=f32,
-                )
-                scores = jnp.where(allowed, scores, -1e30)
-                best = jnp.max(scores, -1, keepdims=True)
-                weights = jnp.exp(scores - best)
-                total = jnp.sum(weights, -1, keepdims=True)
-                probs = (weights * (1.0 / total)).astype(low_type)
-                att_out[at, lanes] = jnp.dot(probs, v_out[:keys, lanes], preferred_element_type=f32)
-                lse_out[at, head : head + 1] = best + jnp.log(total)
-        for first in range(0, rows_all, ATTEND_ROWS):
-            at = slice(first, first + ATTEND_ROWS)
-            rows = att_out[at, :]
-            sums = [jnp.sum(rows, 1, keepdims=True), jnp.sum(rows * rows, 1, keepdims=True)]
-            stat_out[:, at] = as_lanes(sums)[:2]
-
-    return pl.pallas_call(
-        kernel,
-        out_shape=(
-            jax.ShapeDtypeStruct((rows_all, width), low_type),
-            jax.ShapeDtypeStruct((rows_all, width), low_type),
-            jax.ShapeDtypeStruct((rows_all, width), low_type),
-            jax.ShapeDtypeStruct((rows_all, width), f32),
-            jax.ShapeDtypeStruct((rows_all, 8), f32),
-            jax.ShapeDtypeStruct((2, rows_all), f32),
-        ),
-        in_specs=[ON_CHIP] * 9,
-        out_specs=(ON_CHIP,) * 6,
-        compiler_params=pltpu.CompilerParams(vmem_limit_bytes=VMEM_BYTES),
-    )(normed, query_w, key_w, value_w, *tables, segment[:, None], segment[None, :])
-
-
 def as_lanes(columns):
     rows = columns[0].shape[0]
     lane = lax.broadcasted_iota(jnp.int32, (rows, LANES), 1)
@@ -1922,50 +1943,6 @@
     for number, column in enumerate(columns):
         joined = jnp.where(lane == number, column, joined)
     return joined.T[:8, :]
-
-
-def hidden_forward(lifted, up_part, bias, cotangent_all, down_part, gain):
-    rows_all, width = lifted.shape[0], up_part.shape[1]
-    model_width = lifted.shape[1]
-    step = min(256, rows_all)
-    f32 = jnp.float32
-
-    def kernel(lifted_ref, up_ref, bias_ref, cot_ref, down_ref, gain_ref, act_out, slope_out, grad_out, stat_out):
-        pre = jnp.dot(lifted_ref[...], up_ref[...], preferred_element_type=f32) + bias_ref[...]
-        below = 0.5 + 0.5 * lax.erf(pre * (0.5**0.5))
-        activated = pre * below
-        act_out[...] = activated
-        slope_out[...] = below + pre * jnp.exp(-0.5 * pre * pre) * (1.0 / (2.0 * jnp.pi) ** 0.5)
-        grad = lax.dot_general(
-            cot_ref[...], down_ref[...], (((1,), (1,)), ((), ())), preferred_element_type=f32
-        )
-        grad_out[...] = grad
-        scaled = grad * gain_ref[...]
-        sums = [activated, activated * activated, scaled, scaled * activated]
-        stat_out[...] = as_lanes([jnp.sum(part, 1, keepdims=True) for part in sums])[:4]
-
-    def whole(shape):
-        return pl.BlockSpec(shape, lambda i: (0, 0))
-
-    def rows(columns):
-        return pl.BlockSpec((step, columns), lambda i: (i, 0))
-
-    wide_shape = jax.ShapeDtypeStruct((rows_all, width), f32)
-    return pl.pallas_call(
-        kernel,
-        out_shape=(wide_shape, wide_shape, wide_shape, jax.ShapeDtypeStruct((4, rows_all), f32)),
-        grid=(rows_all // step,),
-        in_specs=[
-            rows(model_width),
-            whole(up_part.shape),
-            whole(bias.shape),
-            rows(model_width),
-            whole(down_part.shape),
-            whole(gain.shape),
-        ],
-        out_specs=(rows(width), rows(width), rows(width), pl.BlockSpec((4, step), lambda i: (0, i))),
-        compiler_params=pltpu.CompilerParams(vmem_limit_bytes=VMEM_BYTES),
-    )(lifted, up_part, bias, cotangent_all, down_part, gain)
 
 
 def norm_rows(rows, gain, shift):
@@ -2026,29 +2003,21 @@
             resample_query,
             latents,
             resample_out,
-            query_weight,
-            key_weight,
-            value_weight,
-            out_weight,
         ),
-        (INWARD, INWARD, INWARD, SHARED, OUTWARD, INWARD, INWARD, INWARD, OUTWARD),
+        (INWARD, INWARD, INWARD, SHARED, OUTWARD),
         1,
     )
     (pictures,) = rows
-    image_key_own, image_value_own, probe_own, latent_all, image_out_own, *layer_own = own
-    query_own, key_own, value_own, out_own = layer_own
-    qkv_own = jnp.concatenate([query_own, key_own, value_own], 1)
+    image_key_own, image_value_own, probe_own, latent_all, image_out_own = own
 
     slot_range = jnp.arange(image_total, dtype=jnp.int32)
     live = slot_range % IMG_DEV < jnp.repeat(image_count[0], IMG_DEV)
-    live_mark = live.astype(jnp.int32)
     block_count = group_rows // LAT
     owner = (image_slot[0][None, :] == jnp.arange(block_count, dtype=jnp.int32)[:, None]) & live[None, :]
     taken = jnp.repeat(jnp.any(owner, 1).astype(f32), LAT)[:, None]
     taken_own = lax.dynamic_slice_in_dim(taken, seq_rank * row_count, row_count, 0)
-    image_keys, mixed_placed, probe = image_forward(
-        pictures, image_key_own, image_value_own, latent_all, probe_own, image_slot[0], live_mark
-    )
+    first_rows = jnp.where(live, image_slot[0] * LAT, -LAT)
+    target_rows = (first_rows[:, None] + jnp.arange(LAT, dtype=jnp.int32)[None, :]).reshape(1, -1)
 
     def wide(vector):
         return vector.astype(f32)[None, :]
@@ -2065,12 +2034,14 @@
         return norm_rows(mixed, gain[...], shift[...])[0].astype(jnp.bfloat16)
 
     rows_wide = jax.ShapeDtypeStruct((row_count, model_width), f32)
-    (mixed_in, normed), hidden_blocks = exchange(
-        None,
+    (image_keys, mixed_placed, probe), (mixed_in, normed), (qkv_own, out_own) = exchange(
+        ImageFront(
+            pictures, image_key_own, image_value_own, latent_all, probe_own, target_rows
+        ),
         [
             Stream(
                 group_rows,
-                mixed_placed,
+                None,
                 image_out_own,
                 False,
                 (text[0], taken_own, wide(input_gain), wide(input_shift)),
@@ -2080,7 +2051,13 @@
                 True,
             )
         ],
-        [PlaneWeights((up_weight, down_weight), (INWARD, OUTWARD))],
+        [
+            ChainWeights(
+                (query_weight, key_weight, value_weight, out_weight),
+                (INWARD, INWARD, INWARD, OUTWARD),
+                ((0, 0), (0, own_width), (0, 2 * own_width), (1, 0)),
+            )
+        ],
         3,
     )
 
@@ -2090,10 +2067,6 @@
     tables = xpos_tables(jnp.sum(earlier.astype(f32), 1), own_width)
     cot_late, _ = lax.optimization_barrier((cotangent[0], normed))
     cot_all = lax.all_gather(cot_late, SEQ, axis=0, tiled=True)
-    query_rot, keys_rot, values, attended, log_total, inner_sums = attend_forward(
-        normed, query_own, key_own, value_own, tables, segment_all
-    )
-
     inner_gain_own = wide(own_part(inner_gain))
     def middle_step(total, piece, views, outs):
         mixed_view, gain, shift = views
@@ -2101,8 +2074,10 @@
         outs[0][...] = middle
         return norm_rows(middle, gain[...], shift[...])[0].astype(jnp.bfloat16)
 
-    (inner_low, inner_hat, inner_factor), (middle, lifted), hidden_own = exchange(
-        InnerFront(attended, inner_sums, inner_gain_own, wide(own_part(inner_shift)), model_width),
+    attend_made, (middle, lifted), (up_own, down_own) = exchange(
+        AttendFront(
+            normed, qkv_own, tables, segment_all, inner_gain_own, wide(own_part(inner_shift)), model_width
+        ),
         [
             Stream(
                 group_rows,
@@ -2116,19 +2091,14 @@
                 True,
             )
         ],
-        [CrossWeights(hidden_blocks, (INWARD, OUTWARD))],
+        [ChainWeights((up_weight, down_weight), (INWARD, OUTWARD), ((0, 0), (1, 0)))],
         5,
     )
-    up_own, down_own = hidden_own[0].reshape(model_width, -1), hidden_own[1]
+    *attended_kept, inner_low, inner_hat, inner_factor = attend_made
+    query_rot, keys_rot, values, attended, log_total = attended_kept
     own_hidden = up_own.shape[1]
 
     hidden_gain_own = wide(own_part(hidden_gain))
-    activated, slope, d_settled, hidden_sums = hidden_forward(
-        lifted, up_own, wide(own_part(up_bias)), cot_all, down_own, hidden_gain_own
-    )
-    def blocks_in(grad):
-        return grad.reshape(PLANE, 2, -1, grad.shape[1])
-
     def last_step(total, piece, views, outs):
         outs[0][...] = (views[0][...] + total).astype(jnp.bfloat16)
 
@@ -2151,14 +2121,13 @@
 
     hidden_made, (d_middle, middle_gain_grad, middle_shift_grad, d_branch) = exchange(
         HiddenFront(
-            activated,
-            slope,
-            d_settled,
-            hidden_sums,
+            lifted,
+            up_own,
+            wide(own_part(up_bias)),
+            cot_all,
+            down_own,
             hidden_gain_own,
             wide(own_part(hidden_shift)),
-            lifted,
-            cot_all,
             FF,
         ),
         [
@@ -2178,9 +2147,9 @@
         8,
     )
 
-    settled, _, hidden_vectors, *hidden_pairs = hidden_made
-    attend_made, (d_mixed, input_gain_grad, input_shift_grad, d_rows), (result,) = exchange(
-        AttendFront(
+    settled, _, hidden_vectors, *hidden_grads = hidden_made
+    back_made, (d_mixed, input_gain_grad, input_shift_grad, d_rows), (result,), hidden_theirs = exchange(
+        AttendBackFront(
             d_branch,
             out_own,
             inner_hat,
@@ -2205,27 +2174,23 @@
                 norm_back_step,
                 True,
             ),
-            Stream(
-                group_rows,
-                settled,
-                down_own,
-                False,
-                (middle,),
-                (ROWS,),
-                ((jax.ShapeDtypeStruct((row_count, model_width), low), ROWS),),
-                last_step,
-                False,
-            ),
         ],
-        [],
+        [CrossGrads(hidden_grads, (INWARD, OUTWARD))],
         10,
-    )
-    inner_vectors, *layer_pairs = attend_made
+        Stream(
+            group_rows,
+            settled,
+            down_own,
+            False,
+            (middle,),
+            (ROWS,),
+            ((jax.ShapeDtypeStruct((row_count, model_width), low), ROWS),),
+            last_step,
+            False,
+        ),
+    )
+    inner_vectors, *layer_grads = back_made
     text_grad = jnp.where(taken_own > 0.5, 0.0, d_mixed)
-
-    image_key_grad, image_value_grad, image_out_grad, d_probe = image_backward(
-        d_rows, pictures, image_keys, probe, mixed_placed, image_out_own, image_slot[0], live_mark
-    )
 
     own_vectors = jnp.concatenate(
         [inner_vectors[0], inner_vectors[1], hidden_vectors[2], hidden_vectors[0], hidden_vectors[1]]
@@ -2235,13 +2200,14 @@
     )
     packed = jnp.concatenate([row_vectors, own_vectors]).reshape(-1, LANES)
     spare = -packed.shape[0] % 8
-    packed = jnp.concatenate([d_probe, jnp.pad(packed, ((0, spare), (0, 0)))], 0)
-    image_grads = (blocks_in(image_key_grad), blocks_in(image_value_grad), image_out_grad)
+    packed = jnp.pad(packed, ((0, spare), (0, 0)))
+    layer_sides = (INWARD, INWARD, INWARD, OUTWARD)
     owned, (spread, resample_query_grad, latent_grad) = finale(
-        list(zip(hidden_pairs[:2] + layer_pairs[:4], hidden_pairs[2:] + layer_pairs[4:])),
-        image_grads,
-        (INWARD, OUTWARD, INWARD, INWARD, INWARD, OUTWARD),
-        (INWARD, INWARD, OUTWARD),
+        list(zip(hidden_grads, hidden_theirs)),
+        (INWARD, OUTWARD),
+        layer_grads,
+        layer_sides,
+        (d_rows, pictures, image_keys, probe, mixed_placed, image_out_own, target_rows),
         packed,
         latents.astype(f32).T,
         resample_query.astype(f32),

time: 598 us -> 537 us (0.90); the launches traced: 599 us -> 528 us
  Pallas kernels: 551 us -> 481 us
    pallas_call x9 -> x5, Pallas kernels: 475 us -> 421 us  [lazy_call(): pl.pallas_call(body, out_shape=tuple(out_shapes), in_specs=[ANYWHERE if f...]
    pallas_call x1, Pallas kernels: 71.5 us -> 54.1 us  [intake(): pl.pallas_call(kernel, out_shape=tuple(outs), in_specs=[ANYWHERE] * (n_ro...]
  transfers between devices with their start and end apart: 1 -> 1, of which waited for: 0 -> 0; matrix products, arithmetic and copies ran while one was open for 2% -> 3% of each run, Pallas kernels for 17% -> 17%
where the time goes in v3:
time: 537 us; the launch traced here: 528 us
  Pallas kernels  481 us (90%)
  local copies, waits for them, and re-layouts  17.8 us (3%)
  between operations  14.7 us (3%)
  other arithmetic  14.4 us (3%)
    pallas_call x5, Pallas kernels, lazy_call(): pl.pallas_call(body, out_shape=tuple(out_shapes), in_specs=[ANYWHERE if f...  421 us
    pallas_call x1, Pallas kernels, intake(): pl.pallas_call(kernel, out_shape=tuple(outs), in_specs=[ANYWHERE] * (n_ro...  54.1 us
  transfers between devices with their start and end apart: 1, of which 0 were waited for; matrix products, arithmetic and copies ran while one was open for 3% of the time, Pallas kernels for 17%

profile of v3, /device:TPU:0, one launch (start us, length us, event | category | flops | bytes accessed | tf_op | source)
XLA Modules:
  0.0 527.7 jit_solution(16263398489548247641)
XLA Ops:
  7.2 0.7 broadcast_in_dim.87
  8.0 0.7 multiply_select_fusion
  8.7 0.8 fusion.3
  10.1 0.7 add.63.refs_5_.refs_0_
  10.8 1.3 broadcast_in_dim.113
  12.1 1.3 broadcast_in_dim.114
  14.0 54.1 %shard_map.417 = (bf16[4096,1024]{1,0:T(8,128)(2,1)}, bf16[1024,128]{1,0:T(8,128)(2,1)}, bf16[1024,128]{1,0:T(8,128)(2,1)}, bf16[2048,128]{1,0:T(8,128)(2,1)}, b...) custom-call(bf16[512,1024]{1,0:T(8,128)(2,1)} %bitcast.65, bf16[64,1024]{1,0:T(8,128)(2,1)} %refs_1_.1, ...), custom_call_target="tpu_custom_call" | custom-call | tf_op jit(solution)/shard_map/pallas_call | solution.py:842
  68.1 77.4 %shard_map.418 = (bf16[4096,256]{1,0:T(8,128)(2,1)}, bf16[1024,128]{1,0:T(8,128)(2,1)}, bf16[64,128]{1,0:T(8,128)(2,1)}, f32[128,2048]{1,0:T(8,128)}, bf16[1024,...) custom-call(bf16[4096,1024]{1,0:T(8,128)(2,1)} %get-tuple-element.89.refs_0_.refs_2_, ...), custom_call_target="tpu_custom_call" | custom-call | tf_op jit(solution)/shard_map/pallas_call | solution.py:1535
  145.6 0.8 convert_element_type.9.refs_17_
  146.4 0.7 copy.78
  148.4 1.0 copy.71.refs_3_.refs_11_
  149.4 1.0 copy.70.refs_2_.refs_10_
  150.6 1.0 copy.72.refs_4_.refs_12_
  151.6 1.0 copy.73.refs_5_.refs_13_
  153.8 1.3 bitcast_convert_fusion.1.refs_7_.refs_4_
  155.1 1.3 bitcast_convert_fusion.refs_8_
  156.3 91.7 %shard_map.419 = (bf16[1024,128]{1,0:T(8,128)(2,1)}, bf16[1024,128]{1,0:T(8,128)(2,1)}, bf16[1024,128]{1,0:T(8,128)(2,1)}, f32[1024,128]{1,0:T(8,128)}, f32[1024...) custom-call(bf16[1024,2048]{1,0:T(8,128)(2,1)} %get-tuple-element.95, ...), custom_call_target="tpu_custom_call" | custom-call | tf_op jit(solution)/shard_map/pallas_call | solution.py:1535
  248.1 1.3 dynamic-slice_convert_fusion.2
  249.4 1.4 dynamic-slice_convert_fusion
  250.8 81.1 %shard_map.420 = (bf16[1024,512]{1,0:T(8,128)(2,1)}, bf16[1024,512]{1,0:T(8,128)(2,1)}, f32[8,512]{1,0:T(8,128)}, bf16[8,2,128,512]{3,2,1,0:T(8,128)(2,1)}, bf16...) custom-call(bf16[1024,2048]{1,0:T(8,128)(2,1)} %get-tuple-element.99, ...), custom_call_target="tpu_custom_call" | custom-call | tf_op jit(solution)/shard_map/pallas_call | solution.py:1535
  331.9 107.8 %shard_map.421 = (f32[8,128]{1,0:T(8,128)}, bf16[8,2,128,128]{3,2,1,0:T(8,128)(2,1)}, bf16[8,2,128,128]{3,2,1,0:T(8,128)(2,1)}, bf16[8,2,128,128]{3,2,1,0:T(8,12...) custom-call(bf16[1024,2048]{1,0:T(8,128)(2,1)} %get-tuple-element.10, ...), custom_call_target="tpu_custom_call" | custom-call | tf_op jit(solution)/shard_map/pallas_call | solution.py:1535
  439.7 0.7 constant_dynamic-update-slice_fusion.8
  440.4 0.7 constant_dynamic-update-slice_fusion.7
  441.1 0.7 constant_dynamic-update-slice_fusion.4
  441.8 0.7 constant_dynamic-update-slice_fusion.3
  442.5 0.8 fusion.7
  444.0 63.5 %shard_map.422 = (bf16[128,4096]{1,0:T(8,128)(2,1)}, bf16[4096,128]{1,0:T(8,128)(2,1)}, bf16[128,1024]{1,0:T(8,128)(2,1)}, bf16[128,1024]{1,0:T(8,128)(2,1)}, bf...) custom-call(s32[1,1024]{1,0:T(1,128)} %add.63.refs_5_.refs_0_, ...), custom_call_target="tpu_custom_call" | custom-call | tf_op jit(solution)/shard_map/pallas_call | solution.py:1535
  507.5 1.3 copy.84
  512.0 1.1 select_bitcast_fusion
  513.1 5.1 shard_map.423
  518.2 0.8 copy.96
  519.6 0.8 copy.98
  (57 shorter events, 8.4 us)
Async XLA Ops:
  7.2 243.6 %all-gather.2.cloned.1.call-start = ((), (), s32[]{:S(2)}) async-start(), calls=%async_computation | async-start | bytes 4718592 | tf_op jit(solution)/shard_map/all_gather | solution.py:2069
  68.1 77.5 %copy-start = (bf16[128,1024]{1,0:T(8,128)(2,1)S(1)}, bf16[128,1024]{1,0:T(8,128)(2,1)}, u32[]{:S(2)}) copy-start(bf16[128,1024]{1,0:T(8,128)(2,1)} %refs_3_.1) | copy-start | bytes 786436
  68.1 78.3 %copy-start.4 = (bf16[64,128]{1,0:T(8,128)(2,1)S(1)}, bf16[64,128]{1,0:T(8,128)(2,1)}, u32[]{:S(2)}) copy-start(bf16[64,128]{1,0:T(8,128)(2,1)} %refs_4_.1) | copy-start | bytes 49156
  68.1 79.0 %copy-start.5 = (s32[1,1024]{1,0:T(1,128)S(1)}, s32[1,1024]{1,0:T(1,128)}, u32[]{:S(2)}) copy-start(s32[1,1024]{1,0:T(1,128)} %refs_14_.5) | copy-start | bytes 12292
  145.5 7.1 %copy-start.9 = (bf16[2048]{0:T(1024)(128)(2,1)S(1)}, bf16[2048]{0:T(1024)(128)(2,1)}, u32[]{:S(2)}) copy-start(bf16[2048]{0:T(1024)(128)(2,1)} %param.40) | copy-start | bytes 12292
  145.5 7.7 %copy-start.10 = (bf16[2048]{0:T(1024)(128)(2,1)S(1)}, bf16[2048]{0:T(1024)(128)(2,1)}, u32[]{:S(2)}) copy-start(bf16[2048]{0:T(1024)(128)(2,1)} %param.41) | copy-start | bytes 12292
  331.9 109.2 %copy-start.8 = (f32[1,2048]{1,0:T(1,128)S(1)}, f32[1,2048]{1,0:T(1,128)}, u32[]{:S(2)}) copy-start(f32[1,2048]{1,0:T(1,128)} %get-tuple-element.131) | copy-start | bytes 24580
  331.9 109.2 %copy-start.7 = (f32[1,2048]{1,0:T(1,128)S(1)}, f32[1,2048]{1,0:T(1,128)}, u32[]{:S(2)}) copy-start(f32[1,2048]{1,0:T(1,128)} %get-tuple-element.132) | copy-start | bytes 24580
  444.0 68.0 %copy-start.1 = (f32[128,2048]{1,0:T(8,128)S(1)}, f32[128,2048]{1,0:T(8,128)}, u32[]{:S(2)}) copy-start(f32[128,2048]{1,0:T(8,128)} %get-tuple-element.118) | copy-start | bytes 3145732
  507.5 10.7 %copy-start.2 = (bf16[128,2048]{1,0:T(8,128)(2,1)S(1)}, bf16[128,2048]{1,0:T(8,128)(2,1)}, u32[]{:S(2)}) copy-start(bf16[128,2048]{1,0:T(8,128)(2,1)} %get-tuple-element.117) | copy-start | bytes 1572868
  507.5 11.5 %copy-start.6 = (f32[64,128]{1,0:T(8,128)S(1)}, f32[64,128]{1,0:T(8,128)}, u32[]{:S(2)}) copy-start(f32[64,128]{1,0:T(8,128)} %get-tuple-element.216) | copy-start | bytes 98308
  507.5 12.1 %copy-start.3 = (f32[128,1024]{1,0:T(8,128)S(1)}, f32[128,1024]{1,0:T(8,128)}, u32[]{:S(2)}) copy-start(f32[128,1024]{1,0:T(8,128)} %get-tuple-element.217) | copy-start | bytes 1572868
Sparse Core Ops, SparseCore 0:
  145.7 50.9 all-gather.1

commit v4 on v3

--- a/solution.py
+++ b/solution.py
@@ -583,6 +583,7 @@
 VMEM_BYTES = 60 * 1024 * 1024
 PIECE_ROWS = (32, 32, 32, 32)
 PIECES = len(PIECE_ROWS)
+SECOND_LAG = 2
 FRONT, BACK, ALL, ROWS, INWARD, OUTWARD, SHARED = range(7)
 
 
@@ -726,7 +727,8 @@
         row_refs, weight_refs = refs[:n_rows], refs[n_rows : n_rows + n_weights]
         refs = refs[n_rows + n_weights :]
         row_outs, weight_outs = refs[:n_rows], refs[n_rows : n_rows + n_weights]
-        local, send, recv, w_local, w_send, w_recv, z_send, z_recv = refs[n_rows + n_weights :]
+        refs = refs[n_rows + n_weights :]
+        held, (local, send, recv, w_local, w_send, w_recv, z_send, z_recv) = refs[:n_rows], refs[n_rows:]
         here = Places()
         seq, tp, img = here.seq, here.tp, here.img
         others = [lax.rem(seq + step, PLANE) for step in range(1, PLANE)]
@@ -775,13 +777,13 @@
                 made.start()
                 flights.append(made)
 
-        spreads = []
+        spreads, loads, stores = [], [], []
         for number, (rows, out) in enumerate(zip(row_refs, row_outs)):
             block = rows.shape[0]
             count = block // pieces
-            keep = pltpu.make_async_copy(rows, rows_at(out, seq * block, block), local.at[number])
-            keep.start()
-            own_copies.append(keep)
+            loads.append(pltpu.make_async_copy(rows, held[number], local.at[number, 0]))
+            loads[-1].start()
+            stores.append(pltpu.make_async_copy(held[number], rows_at(out, seq * block, block), local.at[number, 1]))
             for piece in range(pieces):
                 at = number * pieces + piece
                 spreads.append(
@@ -803,6 +805,10 @@
                     flights.append(crossing)
 
         def own_rows(piece):
+            if piece == 1:
+                for load, store in zip(loads, stores):
+                    load.wait()
+                    store.start()
             for index in range(piece, n_weights, len(spreads)):
                 begin(index)
             spreads[piece][0].own(spreads[piece][1], spreads[piece][2])
@@ -827,7 +833,7 @@
             spread.finish()
         for made in flights:
             made.wait_send()
-        for made in own_copies:
+        for made in own_copies + stores:
             made.wait()
 
     def whole(weight, side):
@@ -844,8 +850,9 @@
         out_shape=tuple(outs),
         in_specs=[ANYWHERE] * (n_rows + n_weights),
         out_specs=tuple([ANYWHERE] * len(outs)),
-        scratch_shapes=[
-            dma((n_rows,)),
+        scratch_shapes=[pltpu.VMEM(rows.shape, rows.dtype) for rows in gathered]
+        + [
+            dma((n_rows, 2)),
             dma((n_rows * pieces, 10)),
             dma((n_rows * pieces, 10)),
             dma((n_weights,)),
@@ -968,6 +975,30 @@
         made = remote(landed, landed, z_send.at[index, step], z_recv.at[index, step], here.img_peer)
         made.start()
         self.sent.append(made)
+
+
+class GatherRows(Rider):
+    def __init__(self, rows):
+        self.inputs = [rows]
+        self.out_shapes = [jax.ShapeDtypeStruct((PLANE * rows.shape[0], rows.shape[1]), rows.dtype)]
+        dma = pltpu.SemaphoreType.DMA
+        self.scratch = [dma((PIECES, 10)), dma((PIECES, 10)), dma((1,))]
+
+    def start(self):
+        (rows,), (out,), (send, recv, local) = self.ins, self.outs, self.held
+        block = rows.shape[0]
+        self.spreads = []
+        for piece, count in enumerate(PIECE_ROWS):
+            first = sum(PIECE_ROWS[:piece])
+            self.spreads.append(Spread(self.here, out, block, first, count, send.at[piece], recv.at[piece]))
+            self.launches.append(functools.partial(self.spreads[piece].own, rows, first))
+        self.keep(rows, rows_at(out, self.here.seq * block, block), local.at[0])
+        self.later = [spread.forward for spread in self.spreads] + [spread.corner for spread in self.spreads]
+
+    def finish(self):
+        for spread in self.spreads:
+            spread.finish()
+        super().finish()
 
 
 class CrossGrads(Rider):
@@ -1175,6 +1206,16 @@
             stages.append((6, lambda piece: self.spreads[piece][0].corner()))
         return stages
 
+    def phases(self):
+        def phase_of(stage):
+            def run():
+                for piece in range(PIECES):
+                    stage(piece)
+
+            return run
+
+        return [phase_of(stage) for _, stage in self.stages()]
+
     def finish(self):
         for spread, keep in self.spreads:
             spread.finish()
@@ -1183,6 +1224,21 @@
             made.wait_send()
         for made in self.core_copies.values():
             made.wait_send()
+
+
+def full_line(rows):
+    held = rows[...].astype(jnp.float32)
+    return jnp.concatenate([held[number : number + 1, :] for number in range(held.shape[0])], 1)
+
+
+def own_line(here, rows, width):
+    held = rows[...].astype(jnp.float32)
+    count = width // LANES
+    number = lax.broadcasted_iota(jnp.int32, held.shape, 0)
+    parts = [
+        jnp.sum(jnp.where(number == here.seq * count + part, held, 0.0), 0, keepdims=True) for part in range(count)
+    ]
+    return jnp.concatenate(parts, 1)
 
 
 class Front(Rider):
@@ -1228,8 +1284,8 @@
 
 
 class ImageFront(Rider):
-    def __init__(self, pictures, key_part, value_part, latent_all, probe_part, target_rows):
-        self.inputs = [pictures, key_part, value_part, latent_all, probe_part, target_rows]
+    def __init__(self, pictures, key_part, value_part, latent_all, probe_part, target_rows, segment):
+        self.inputs = [pictures, key_part, value_part, latent_all, probe_part, target_rows, segment]
         rows, width = pictures.shape[0], key_part.shape[1]
         images = rows // PATCH
         low_type = jnp.bfloat16
@@ -1238,14 +1294,20 @@
             jax.ShapeDtypeStruct((images * LAT, width), low_type),
             jax.ShapeDtypeStruct((LAT, width), low_type),
         ]
+        self.out_shapes += [jax.ShapeDtypeStruct((segment.shape[1], width), jnp.float32)] * 3
+        self.out_shapes.append(jax.ShapeDtypeStruct((segment.shape[1], 8), jnp.float32))
         self.scratch = [
             pltpu.VMEM((key_part.shape[0], 2 * width), low_type),
             pltpu.VMEM((images * LAT, width), low_type),
         ]
 
     def run(self):
-        pictures, key_w, value_w, latent_all, probe_w, target_rows = self.ins
-        keys, placed, probe = self.outs
+        pictures, key_w, value_w, latent_all, probe_w, target_rows, segment = self.ins
+        keys, placed, probe, *tables, column = self.outs
+        row = segment[...].astype(jnp.float32)
+        column[...] = jnp.broadcast_to(row, (8, row.shape[1])).T
+        for first in range(0, segment.shape[1], ATTEND_ROWS):
+            self.launches.append(functools.partial(xpos_part, segment, column, tables, first))
         both_w, mixed_all = self.held
         width, scale = probe.shape[1], HEAD ** (-0.5)
         both_w[:, :width] = key_w[...]
@@ -1271,12 +1333,12 @@
             placed[first : first + PATCH, :] = jnp.dot(
                 chosen, mixed_all[...], preferred_element_type=jnp.float32
             ).astype(jnp.bfloat16)
-        self.left = placed
+        self.lefts = [placed]
 
 
 class AttendFront(Front):
-    def __init__(self, normed, layer_part, tables, segment, gain, shift, full_width):
-        self.inputs = [normed, layer_part, *tables, segment[:, None], segment[None, :], gain, shift]
+    def __init__(self, normed, layer_part, tables, segment, column, gain, shift, full_width):
+        self.inputs = [normed, layer_part, *tables, segment, column, gain, shift]
         self.full_width = full_width
         rows, width = normed.shape[0], layer_part.shape[1] // 3
         low_shape = jax.ShapeDtypeStruct((rows, width), jnp.bfloat16)
@@ -1286,7 +1348,7 @@
         self.scratch = self.total_scratch(2, rows)
 
     def run(self):
-        normed, layer_w, cos_ref, sin_ref, grow_ref, column_ref, row_ref, gain, shift = self.ins
+        normed, layer_w, cos_ref, sin_ref, grow_ref, segment, column, gain, shift = self.ins
         q_out, k_out, v_out, att_out, lse_out, low, hat, factor_out = self.outs
         rows_all, width = att_out.shape
         scale = HEAD ** (-0.5)
@@ -1300,7 +1362,7 @@
             lin = linear[:, width : 2 * width]
             k_out[at, :] = ((lin * cosine + halves_swapped(lin) * sine) * (1.0 / growth)).astype(low_type)
             v_out[at, :] = linear[:, 2 * width :].astype(low_type)
-            allowed = allowed_part(column_ref, row_ref, first, ATTEND_ROWS, keys)
+            allowed = allowed_part(column, segment, first, ATTEND_ROWS, keys)
             for head in range(width // HEAD):
                 lanes = slice(head * HEAD, (head + 1) * HEAD)
                 scores = lax.dot_general(
@@ -1326,8 +1388,9 @@
         normal = (att_out[...] - average) * factor
         hat[...] = normal
         factor_out[...] = jnp.broadcast_to(factor, normal.shape)
-        low[...] = (normal * gain[...] + shift[...]).astype(low_type)
-        self.left = low
+        gain, shift = (own_line(self.here, line, low.shape[1]) for line in (gain, shift))
+        low[...] = (normal * gain + shift).astype(low_type)
+        self.lefts = [low]
 
 
 class GradFront(Front):
@@ -1380,11 +1443,12 @@
         settled, d_hidden, vectors, up, down = self.outs
         activated, slope, d_settled = self.held[6:]
         f32 = jnp.float32
+        bias, gain, shift = (own_line(self.here, line, settled.shape[1]) for line in (bias, gain, shift))
         rows = activated.shape[0]
         step = rows // 4
         for first in range(0, rows, step):
             at = slice(first, first + step)
-            pre = jnp.dot(lifted[at, :], up_w[...], preferred_element_type=f32) + bias[...]
+            pre = jnp.dot(lifted[at, :], up_w[...], preferred_element_type=f32) + bias
             below = 0.5 + 0.5 * lax.erf(pre * (0.5**0.5))
             act = pre * below
             activated[at, :] = act
@@ -1393,7 +1457,7 @@
                 cotangent_all[at, :], down_w[...], (((1,), (1,)), ((), ())), preferred_element_type=f32
             )
             d_settled[at, :] = grad
-            scaled = grad * gain[...]
+            scaled = grad * gain
             sums = [jnp.sum(part, 1, keepdims=True) for part in (act, act * act, scaled, scaled * act)]
             self.held[1][:, at] = as_lanes(sums)[:4]
             yield
@@ -1407,9 +1471,9 @@
         for first in range(0, rows, step):
             at = slice(first, first + step)
             normal = (activated[at, :] - average[at]) * factor[at]
-            settled[at, :] = (normal * gain[...] + shift[...]).astype(jnp.bfloat16)
+            settled[at, :] = (normal * gain + shift).astype(jnp.bfloat16)
             grad = d_settled[at, :]
-            inner = factor[at] * (grad * gain[...] - mean_scaled[at] - normal * mean_cross[at])
+            inner = factor[at] * (grad * gain - mean_scaled[at] - normal * mean_cross[at])
             low = (slope[at, :] * inner).astype(jnp.bfloat16)
             d_hidden[at, :] = low
             gain_sum += jnp.sum(grad * normal, 0, keepdims=True)
@@ -1418,13 +1482,13 @@
         vectors[...] = jnp.zeros_like(vectors)
         vectors[0:1, :], vectors[1:2, :], vectors[2:3, :] = gain_sum, shift_sum, bias_sum
         self.grads([(lifted, d_hidden, [up], INWARD), (settled, cotangent_all, [down], OUTWARD)])
-        self.left = d_hidden
+        self.lefts = [d_hidden, settled]
 
 
 class AttendBackFront(GradFront):
-    def __init__(self, d_branch, out_part, hat, factor, gain, kept, tables, segment, normed, inner_low, full_width):
+    def __init__(self, d_branch, out_part, hat, factor, gain, kept, tables, segment, column, normed, inner_low, full_width):
         self.inputs = [d_branch, out_part, hat, factor, gain, *kept, *tables]
-        self.inputs += [segment[:, None], segment[None, :], normed, inner_low]
+        self.inputs += [segment, column, normed, inner_low]
         self.full_width = full_width
         rows, width = hat.shape
         model_width = normed.shape[1]
@@ -1437,7 +1501,8 @@
 
     def run(self):
         d_branch, out_part, hat, factor, gain, attended, q_ref, k_ref, v_ref, lse = self.ins[:10]
-        cos_ref, sin_ref, grow_ref, column_ref, row_ref, normed, inner_low = self.ins[10:]
+        cos_ref, sin_ref, grow_ref, segment, column, normed, inner_low = self.ins[10:]
+        gain = own_line(self.here, gain, hat.shape[1])
         vectors, *grads = self.outs
         d_att, lin_out, d_inner, d_query, d_key, d_value = self.held[6:]
         rows_all, width = hat.shape
@@ -1451,7 +1516,7 @@
             d_inner[at, :] = grad
             gain_sum += jnp.sum(grad * hat[at, :], 0, keepdims=True)
             shift_sum += jnp.sum(grad, 0, keepdims=True)
-            scaled = grad * gain[...]
+            scaled = grad * gain
             sums = [jnp.sum(scaled, 1, keepdims=True), jnp.sum(scaled * hat[at, :], 1, keepdims=True)]
             self.held[1][:, at] = as_lanes(sums)[:2]
             yield
@@ -1459,12 +1524,12 @@
         vectors[0:1, :], vectors[1:2, :] = gain_sum, shift_sum
         total = self.small_sum(self.held[:6]) / self.full_width
         d_att[...] = (
-            factor[...] * (d_inner[...] * gain[...] - total[:, 0:1] - hat[...] * total[:, 1:2])
+            factor[...] * (d_inner[...] * gain - total[:, 0:1] - hat[...] * total[:, 1:2])
         ).astype(low_type)
         heads, scale = width // HEAD, HEAD ** (-0.5)
         for first in range(0, rows_all, ATTEND_ROWS):
             at, keys = slice(first, first + ATTEND_ROWS), first + ATTEND_ROWS
-            allowed = allowed_part(column_ref, row_ref, first, ATTEND_ROWS, keys)
+            allowed = allowed_part(column, segment, first, ATTEND_ROWS, keys)
             for head in range(heads):
                 lanes = slice(head * HEAD, (head + 1) * HEAD)
                 scores = lax.dot_general(
@@ -1511,7 +1576,7 @@
                 (inner_low, d_branch, grads[3:], OUTWARD),
             ]
         )
-        self.left = lin_out
+        self.lefts = [lin_out]
 
 
 def lazy_call(kernel, inputs, in_specs, out_shapes, out_specs, scratch, cid):
@@ -1544,7 +1609,7 @@
     )(*inputs)
 
 
-def exchange(front, streams, riders, cid, early=None, pace=1, early_pace=3):
+def exchange(front, streams, riders, cid, early=None, pace=1, early_pace=5):
     fronts = [front] if front is not None else []
     earlies = [early] if early is not None else []
     sums = list(streams) + earlies
@@ -1578,29 +1643,32 @@
             if rider.later:
                 take_some(rider.launches, len(rider.launches))
             waiting += rider.launches + rider.later
-        early_ticks = []
+        early_steps = []
         if early is not None:
             early.begin()
-            early_ticks = ticks_of(early.stages(), PIECES)
+            early_steps = early.phases()
+            take_some(early_steps, 1)
         if front is not None:
-            for number, _ in enumerate(front.run()):
+            for number, _ in enumerate(front.run(), 1):
                 take_some(waiting, pace)
-                if number % early_pace == 0:
-                    take_some(early_ticks, 1)
-            streams[0].left = front.left
+                if number % early_pace == 0 and len(early_steps) > 1:
+                    take_some(early_steps, 1)
+            for stream, left in zip(streams, front.lefts):
+                stream.left = left
             waiting += front.launches
         for stream in streams:
             stream.begin()
         stages = []
-        for stream in reversed(streams):
-            stages += stream.stages()
+        for number, stream in reversed(list(enumerate(streams))):
+            stages += [(lag + number * SECOND_LAG, stage) for lag, stage in stream.stages()]
         ticks = ticks_of(stages, PIECES)
         share = -(-len(waiting) // max(len(ticks) - 2, 1))
-        for tick in ticks:
+        for number, tick in enumerate(ticks):
             tick()
-            take_some(early_ticks, 1)
+            if number >= PIECES:
+                take_some(early_steps, 1)
             take_some(waiting, share)
-        take_some(early_ticks, len(early_ticks))
+        take_some(early_steps, len(early_steps))
         for part in parts:
             part.finish()
 
@@ -1629,7 +1697,7 @@
     return split
 
 
-def finale(pairs, sides, raw, raw_sides, image, vectors, latents_t, query_rows, cid):
+def finale(pairs, sides, raw, raw_sides, image, row_vectors, own_vectors, latents, query_rows, result_parts, cid):
     f32, low_type, dma = jnp.float32, jnp.bfloat16, pltpu.SemaphoreType.DMA
     d_rows, pictures, keys, probe, placed, out_part, target_rows = image
     width, model_width, picture_width = probe.shape[1], d_rows.shape[1], pictures.shape[1]
@@ -1646,7 +1714,11 @@
     blocks = [
         shape[2:] if side == INWARD else (shape[0], shape[1] // (2 * PLANE)) for shape, side in zip(shapes, all_sides)
     ]
-    small_shape = (LAT + vectors.shape[0], LANES)
+    vectors = list(row_vectors) + [array for array, _ in own_vectors]
+    picked = [0] * len(row_vectors) + [row for _, row in own_vectors]
+    vector_rows = sum(vector.shape[1] // LANES for vector in vectors)
+    small_shape = (LAT + vector_rows + -vector_rows % 8, LANES)
+    result_shape = result_parts[0].shape
 
     def kernel(ins, outs, held):
         refs = list(ins) + list(outs) + list(held)
@@ -1659,14 +1731,15 @@
         target_ref, d_ref, pictures_ref, keys_ref, probe_ref, placed_ref, out_w = take(7)
         grad_refs = take(n + n_raw)
         theirs = take(n)
-        vectors_ref, latents_ref, query_ref = take(3)
+        vector_refs = take(len(vectors))
+        latents_ref, query_ref, result_ref, result_here, middle_ref = take(5)
         out_refs = take(total)
-        sums_out, query_out, latent_out = take(3)
+        sums_out, query_out, latent_out, result_out = take(4)
         grad_refs += take(n_image)
         theirs += take(n_raw + n_image)
         summed = take(total)
-        small_own, small_theirs, small_mine, small_all, lat_mine, lat_theirs, d_mixed, d_both = take(8)
-        z_send, z_recv, send, recv, local, s_send, s_recv = take(7)
+        small_own, small_theirs, small_mine, small_all, lat_mine, lat_theirs, d_mixed, d_both, result_theirs = take(9)
+        z_send, z_recv, send, recv, local, s_send, s_recv, r_send, r_recv = take(9)
         here = Places()
         seq, img = here.seq, here.img
         ring = [here.at(lax.rem(seq + step, PLANE)) for step in range(1, PLANE)]
@@ -1716,8 +1789,17 @@
             made.start()
             waits.append(made.wait_send)
 
+        result_copy = remote(result_ref, result_theirs, r_send.at[0], r_recv.at[0], here.tp_peer)
+        result_copy.start()
         for index in range(n, n + n_raw):
             cross(index)
+        at_row = LAT
+        for vector, row in zip(vector_refs, picked):
+            for first in range(0, vector.shape[1], LANES):
+                small_own[at_row : at_row + 1, :] = vector[row : row + 1, first : first + LANES]
+                at_row += 1
+        if at_row < small_shape[0]:
+            small_own[at_row:, :] = jnp.zeros((small_shape[0] - at_row, LANES), f32)
         waiting = [functools.partial(deliver, index, step) for index in range(n + n_raw) for step in range(PLANE)]
 
         scale = HEAD ** (-0.5)
@@ -1765,7 +1847,6 @@
             d_probe_sum += jnp.concatenate(d_probe, 1)
             take_some(waiting, 2)
         small_own[:LAT, :] = d_probe_sum
-        small_own[LAT:, :] = vectors_ref[...]
         small_cross = remote(small_own, small_theirs, s_send.at[0], s_recv.at[0], here.img_peer)
         small_cross.start()
         span = picture_width // PLANE
@@ -1802,12 +1883,16 @@
         for source in range(PLANE):
             given = small_all[source, :LAT, :]
             at = slice(source * width, (source + 1) * width)
-            query_out[:, at] = jnp.dot(
-                latents_ref[...], given, precision=HIGHEST_PRECISION, preferred_element_type=f32
+            query_out[:, at] = lax.dot_general(
+                latents_ref[...].astype(f32),
+                given,
+                (((0,), (0,)), ((), ())),
+                precision=HIGHEST_PRECISION,
+                preferred_element_type=f32,
             )
             latent_part += lax.dot_general(
                 given,
-                query_ref[:, at],
+                query_ref[:, at].astype(f32),
                 (((1,), (1,)), ((), ())),
                 precision=HIGHEST_PRECISION,
                 preferred_element_type=f32,
@@ -1817,6 +1902,9 @@
         last.start()
         last.wait()
         latent_out[...] = lat_mine[...] + lat_theirs[...]
+        result_copy.wait()
+        result_sum = result_here[...].astype(f32) + result_theirs[...].astype(f32)
+        result_out[...] = (middle_ref[...] + result_sum).astype(low_type)
         for index in range(total):
             for step in range(1, PLANE):
                 source = lax.rem(seq + PLANE - step, PLANE)
@@ -1831,11 +1919,12 @@
     for block, side in zip(blocks, all_sides):
         shape = (block[0], PLANE * block[1]) if side == INWARD else (PLANE * block[0], block[1])
         outs.append(jax.ShapeDtypeStruct(shape, low_type))
-    lat_shape = (latents_t.shape[1], latents_t.shape[0])
+    lat_shape = latents.shape
     small_shapes = [
         jax.ShapeDtypeStruct((PLANE,) + small_shape, f32),
         jax.ShapeDtypeStruct(query_rows.shape, f32),
         jax.ShapeDtypeStruct(lat_shape, f32),
+        jax.ShapeDtypeStruct(result_shape, low_type),
     ]
     n_cross = n_raw + n_image
     made = lazy_call(
@@ -1851,13 +1940,15 @@
             *[grad for grad, _ in pairs],
             *raw,
             *[given for _, given in pairs],
-            vectors,
-            latents_t,
+            *vectors,
+            latents,
             query_rows,
+            result_parts[0],
+            *result_parts,
         ],
-        [ON_CHIP] * (7 + n + n_raw + n + 3),
+        [ON_CHIP] * (7 + n + n_raw + n + len(vectors)) + [ON_CHIP] * 2 + [ANYWHERE, ON_CHIP, ON_CHIP],
         outs + small_shapes,
-        [ANYWHERE] * total + [ON_CHIP] * 3,
+        [ANYWHERE] * total + [ON_CHIP] * 4,
         [pltpu.VMEM(item.shape, low_type) for item in image_shapes]
         + [pltpu.VMEM((PLANE,) + tuple(block), low_type) for block in blocks[n:]]
         + [pltpu.VMEM((PLANE,) + tuple(block), low_type) for block in blocks]
@@ -1870,6 +1961,7 @@
             pltpu.VMEM(lat_shape, f32),
             pltpu.VMEM((d_rows.shape[0], width), low_type),
             pltpu.VMEM((images * PATCH, 2 * width), low_type),
+            pltpu.VMEM(result_shape, low_type),
             dma((n_cross, PLANE)),
             dma((n_cross, PLANE)),
             dma((total, PLANE)),
@@ -1877,24 +1969,77 @@
             dma((total,)),
             dma((PLANE + 1,)),
             dma((PLANE + 1,)),
+            dma((1,)),
+            dma((1,)),
         ],
         cid,
     )
     return made[:total], made[total:]
 
 
-def widened(arrays):
+def widened(grads, passed, spread, model_width, n_rows, widths):
+    f32, dma = jnp.float32, pltpu.SemaphoreType.DMA
+    n, n_passed = len(grads), len(passed)
+
     def kernel(*refs):
-        for src, dst in zip(refs[: len(arrays)], refs[len(arrays) :]):
-            dst[...] = src[...].astype(jnp.float32)
-
-    return pl.pallas_call(
+        refs = list(refs)
+
+        def take(count):
+            taken = refs[:count]
+            del refs[:count]
+            return taken
+
+        ins, passed_ins, (spread_ref,) = take(n), take(n_passed), take(1)
+        outs, passed_outs, row_outs, own_outs = take(n), take(n_passed), take(n_rows), take(len(widths))
+        narrow, wide, held, (in_sems, out_sems, passed_sems) = take(n), take(n), take(n_passed), take(3)
+        copies_in = [pltpu.make_async_copy(src, dst, in_sems.at[i]) for i, (src, dst) in enumerate(zip(ins, narrow))]
+        copies_out = [pltpu.make_async_copy(src, dst, out_sems.at[i]) for i, (src, dst) in enumerate(zip(wide, outs))]
+        held_in = [pltpu.make_async_copy(src, dst, passed_sems.at[0, i]) for i, (src, dst) in enumerate(zip(passed_ins, held))]
+        held_out = [pltpu.make_async_copy(src, dst, passed_sems.at[1, i]) for i, (src, dst) in enumerate(zip(held, passed_outs))]
+        for copy in copies_in + held_in:
+            copy.start()
+        for i in range(n):
+            copies_in[i].wait()
+            wide[i][...] = narrow[i][...].astype(f32)
+            copies_out[i].start()
+        for arrive, leave in zip(held_in, held_out):
+            arrive.wait()
+            leave.start()
+        first = LAT
+        for out in row_outs:
+            count = model_width // LANES
+            total = jnp.sum(spread_ref[:, first : first + count, :], 0)
+            for part in range(count):
+                out[:, part * LANES : (part + 1) * LANES] = total[part : part + 1, :]
+            first += count
+        for out, width in zip(own_outs, widths):
+            for seq in range(PLANE):
+                for part in range(width // LANES):
+                    at = seq * width + part * LANES
+                    out[:, at : at + LANES] = spread_ref[seq, first + part : first + part + 1, :]
+            first += width // LANES
+        for copy in copies_out + held_out:
+            copy.wait()
+
+    shapes = [jax.ShapeDtypeStruct(array.shape, f32) for array in grads]
+    shapes += [jax.ShapeDtypeStruct(array.shape, array.dtype) for array in passed]
+    shapes += [jax.ShapeDtypeStruct((1, model_width), f32)] * n_rows
+    shapes += [jax.ShapeDtypeStruct((1, PLANE * width), f32) for width in widths]
+    small = n_rows + len(widths)
+    made = pl.pallas_call(
         kernel,
-        out_shape=tuple(jax.ShapeDtypeStruct(array.shape, jnp.float32) for array in arrays),
-        in_specs=[ON_CHIP] * len(arrays),
-        out_specs=tuple([ON_CHIP] * len(arrays)),
+        out_shape=tuple(shapes),
+        in_specs=[ANYWHERE] * (n + n_passed) + [ON_CHIP],
+        out_specs=tuple([ANYWHERE] * (n + n_passed) + [ON_CHIP] * small),
+        scratch_shapes=[pltpu.VMEM(array.shape, array.dtype) for array in grads]
+        + [pltpu.VMEM(array.shape, f32) for array in grads]
+        + [pltpu.VMEM(array.shape, array.dtype) for array in passed]
+        + [dma((n,)), dma((n,)), dma((2, n_passed))],
         compiler_params=pltpu.CompilerParams(vmem_limit_bytes=VMEM_BYTES),
-    )(*arrays)
+    )(*grads, *passed, spread)
+    made = list(made)
+    cut = [made[:n], made[n : n + n_passed], made[n + n_passed : n + n_passed + n_rows]]
+    return (*cut, made[n + n_passed + n_rows :])
 
 
 IMAGES_A_STEP = 4
@@ -1908,14 +2053,23 @@
     return weights * (1.0 / jnp.sum(weights, -1, keepdims=True))
 
 
-def xpos_tables(position, width):
-    cosine, sine, growth = (table[:, 0, :] for table in xpos_factors(position, HEAD // 2))
-    repeats = width // HEAD
-    return (
-        jnp.tile(cosine, (1, 2 * repeats)),
-        jnp.tile(jnp.concatenate([-sine, sine], 1), (1, repeats)),
-        jnp.tile(growth, (1, 2 * repeats)),
-    )
+def xpos_part(segment, column, tables, first):
+    at, half = slice(first, first + ATTEND_ROWS), HEAD // 2
+    f32 = jnp.float32
+    rows = segment.shape[1]
+    here = segment[:, at].astype(f32)
+    earlier = lax.broadcasted_iota(jnp.int32, (rows, ATTEND_ROWS), 0)
+    now = first + lax.broadcasted_iota(jnp.int32, (rows, ATTEND_ROWS), 1)
+    counted = (column[:, 0:1] == here) & (earlier < now)
+    position = jnp.sum(counted.astype(f32), 0, keepdims=True)
+    ladder = lax.broadcasted_iota(jnp.int32, (half, ATTEND_ROWS), 0).astype(f32)
+    angles = position * jnp.exp(ladder * (-2.0 * jnp.log(f32(10000.0)) / (2.0 * half)))
+    growth = jnp.exp(position / 512.0 * jnp.log((ladder / half + 0.4) / 1.4))
+    cosine, sine = jnp.cos(angles), jnp.sin(angles)
+    repeats = tables[0].shape[1] // HEAD
+    tables[0][at, :] = jnp.concatenate([cosine, cosine] * repeats, 0).T
+    tables[1][at, :] = jnp.concatenate([-sine, sine] * repeats, 0).T
+    tables[2][at, :] = jnp.concatenate([growth, growth] * repeats, 0).T
 
 
 def halves_swapped(rows):
@@ -1926,11 +2080,11 @@
     return jnp.where(lane % HEAD < half, ahead, behind)
 
 
-def allowed_part(segment_column, segment_row, first, count, keys):
+def allowed_part(column, segment, first, count, keys):
     row = first + lax.broadcasted_iota(jnp.int32, (count, keys), 0)
-    column = lax.broadcasted_iota(jnp.int32, (count, keys), 1)
-    same = segment_column[pl.ds(first, count), :] == segment_row[:, :keys]
-    return same & (column <= row)
+    later = lax.broadcasted_iota(jnp.int32, (count, keys), 1)
+    same = column[first : first + count, 0:1] == segment[:, :keys].astype(jnp.float32)
+    return same & (later <= row)
 
 
 ATTEND_ROWS = 256
@@ -1987,13 +2141,9 @@
     f32, low = jnp.float32, jnp.bfloat16
     row_count, model_width = text.shape[1], text.shape[2]
     group_rows = segment.shape[1]
-    seq_rank = lax.axis_index(SEQ)
     image_slots = features.shape[1]
-    image_total = image_slot.shape[1]
     half_width = query_weight.shape[1]
     own_width = half_width // PLANE
-    own_heads = own_width // HEAD
-    score_scale = HEAD ** (-0.5)
 
     rows, own = intake(
         (features[0].reshape(image_slots * PATCH, features.shape[3]),),
@@ -2010,33 +2160,31 @@
     (pictures,) = rows
     image_key_own, image_value_own, probe_own, latent_all, image_out_own = own
 
-    slot_range = jnp.arange(image_total, dtype=jnp.int32)
-    live = slot_range % IMG_DEV < jnp.repeat(image_count[0], IMG_DEV)
-    block_count = group_rows // LAT
-    owner = (image_slot[0][None, :] == jnp.arange(block_count, dtype=jnp.int32)[:, None]) & live[None, :]
-    taken = jnp.repeat(jnp.any(owner, 1).astype(f32), LAT)[:, None]
-    taken_own = lax.dynamic_slice_in_dim(taken, seq_rank * row_count, row_count, 0)
-    first_rows = jnp.where(live, image_slot[0] * LAT, -LAT)
-    target_rows = (first_rows[:, None] + jnp.arange(LAT, dtype=jnp.int32)[None, :]).reshape(1, -1)
-
-    def wide(vector):
-        return vector.astype(f32)[None, :]
-
-    def own_part(vector):
-        width = vector.shape[0] // PLANE
-        return lax.dynamic_slice_in_dim(vector, seq_rank * width, width, 0)
+    counts = image_count.reshape(-1, 1)
+    live = jnp.arange(IMG_DEV, dtype=jnp.int32)[None, :] < counts
+    first_rows = jnp.where(live, image_slot.reshape(live.shape) * LAT, -LAT)
+    target_rows = (first_rows[:, :, None] + jnp.arange(LAT, dtype=jnp.int32)).reshape(1, -1)
+
+    def line(vector):
+        return vector.reshape(-1, LANES)
+
+    def taken_in(targets, piece, rows):
+        first = lax.axis_index(SEQ) * row_count + sum(PIECE_ROWS[:piece])
+        row = first + lax.broadcasted_iota(jnp.int32, (rows, targets.shape[1]), 0)
+        return jnp.max((row == targets[...]).astype(jnp.float32), 1, keepdims=True) > 0.5
 
     def begin(total, piece, views, outs):
-        text_view, taken_view, gain, shift = views
+        text_view, targets, gain, shift = views
         embed = total.astype(jnp.bfloat16).astype(jnp.float32)
-        mixed = jnp.where(taken_view[...] > 0.5, embed, text_view[...].astype(jnp.float32))
+        taken = taken_in(targets, piece, total.shape[0])
+        mixed = jnp.where(taken, embed, text_view[...].astype(jnp.float32))
         outs[0][...] = mixed
-        return norm_rows(mixed, gain[...], shift[...])[0].astype(jnp.bfloat16)
+        return norm_rows(mixed, full_line(gain), full_line(shift))[0].astype(jnp.bfloat16)
 
     rows_wide = jax.ShapeDtypeStruct((row_count, model_width), f32)
-    (image_keys, mixed_placed, probe), (mixed_in, normed), (qkv_own, out_own) = exchange(
+    (image_keys, mixed_placed, probe, *tables, column), (mixed_in, normed), (qkv_own, out_own, up_own) = exchange(
         ImageFront(
-            pictures, image_key_own, image_value_own, latent_all, probe_own, target_rows
+            pictures, image_key_own, image_value_own, latent_all, probe_own, target_rows, segment
         ),
         [
             Stream(
@@ -2044,8 +2192,8 @@
                 None,
                 image_out_own,
                 False,
-                (text[0], taken_own, wide(input_gain), wide(input_shift)),
-                (ROWS, ROWS, ALL, ALL),
+                (text[0], target_rows, line(input_gain), line(input_shift)),
+                (ROWS, ALL, ALL, ALL),
                 ((rows_wide, ROWS),),
                 begin,
                 True,
@@ -2053,30 +2201,23 @@
         ],
         [
             ChainWeights(
-                (query_weight, key_weight, value_weight, out_weight),
-                (INWARD, INWARD, INWARD, OUTWARD),
-                ((0, 0), (0, own_width), (0, 2 * own_width), (1, 0)),
+                (query_weight, key_weight, value_weight, out_weight, up_weight),
+                (INWARD, INWARD, INWARD, OUTWARD, INWARD),
+                ((0, 0), (0, own_width), (0, 2 * own_width), (1, 0), (2, 0)),
             )
         ],
         3,
     )
 
-    segment_all = segment[0]
-    row_index = jnp.arange(group_rows, dtype=jnp.int32)
-    earlier = (row_index[None, :] < row_index[:, None]) & (segment_all[None, :] == segment_all[:, None])
-    tables = xpos_tables(jnp.sum(earlier.astype(f32), 1), own_width)
-    cot_late, _ = lax.optimization_barrier((cotangent[0], normed))
-    cot_all = lax.all_gather(cot_late, SEQ, axis=0, tiled=True)
-    inner_gain_own = wide(own_part(inner_gain))
     def middle_step(total, piece, views, outs):
         mixed_view, gain, shift = views
         middle = mixed_view[...] + total
         outs[0][...] = middle
-        return norm_rows(middle, gain[...], shift[...])[0].astype(jnp.bfloat16)
-
-    attend_made, (middle, lifted), (up_own, down_own) = exchange(
+        return norm_rows(middle, full_line(gain), full_line(shift))[0].astype(jnp.bfloat16)
+
+    attend_made, (middle, lifted), (down_own,), (cot_all,) = exchange(
         AttendFront(
-            normed, qkv_own, tables, segment_all, inner_gain_own, wide(own_part(inner_shift)), model_width
+            normed, qkv_own, tables, segment, column, line(inner_gain), line(inner_shift), model_width
         ),
         [
             Stream(
@@ -2084,34 +2225,34 @@
                 None,
                 out_own,
                 False,
-                (mixed_in, wide(middle_gain), wide(middle_shift)),
+                (mixed_in, line(middle_gain), line(middle_shift)),
                 (ROWS, ALL, ALL),
                 ((rows_wide, ROWS),),
                 middle_step,
                 True,
             )
         ],
-        [ChainWeights((up_weight, down_weight), (INWARD, OUTWARD), ((0, 0), (1, 0)))],
+        [ChainWeights((down_weight,), (OUTWARD,), ((0, 0),)), GatherRows(cotangent[0])],
         5,
+        pace=2,
     )
     *attended_kept, inner_low, inner_hat, inner_factor = attend_made
     query_rot, keys_rot, values, attended, log_total = attended_kept
     own_hidden = up_own.shape[1]
 
-    hidden_gain_own = wide(own_part(hidden_gain))
-    def last_step(total, piece, views, outs):
-        outs[0][...] = (views[0][...] + total).astype(jnp.bfloat16)
-
     vector_out = jax.ShapeDtypeStruct((1, model_width), f32)
 
     def norm_back_step(total, piece, views, outs):
-        rows_view, carried_view, gain = views
+        rows_view, carried_view, gain, *targets = views
         rows_in = rows_view[...]
         center = rows_in - jnp.mean(rows_in, -1, keepdims=True)
         factor = lax.rsqrt(jnp.mean(center * center, -1, keepdims=True) + EPSILON)
         normal = center * factor
-        grad = carried_view[...].astype(jnp.float32) + full_back(total, normal, factor, gain[...])
-        outs[0][...] = grad
+        grad = carried_view[...].astype(jnp.float32) + full_back(total, normal, factor, full_line(gain))
+        if targets:
+            outs[0][...] = jnp.where(taken_in(targets[0], piece, total.shape[0]), 0.0, grad)
+        else:
+            outs[0][...] = grad
         if piece == 0:
             outs[1][...] = jnp.zeros_like(outs[1])
             outs[2][...] = jnp.zeros_like(outs[2])
@@ -2123,11 +2264,11 @@
         HiddenFront(
             lifted,
             up_own,
-            wide(own_part(up_bias)),
+            line(up_bias),
             cot_all,
             down_own,
-            hidden_gain_own,
-            wide(own_part(hidden_shift)),
+            line(hidden_gain),
+            line(hidden_shift),
             FF,
         ),
         [
@@ -2136,28 +2277,31 @@
                 None,
                 up_own,
                 True,
-                (middle, cotangent[0], wide(middle_gain)),
+                (middle, cotangent[0], line(middle_gain)),
                 (ROWS, ROWS, ALL),
                 ((rows_wide, ROWS), (vector_out, ALL), (vector_out, ALL)),
                 norm_back_step,
                 True,
-            )
+            ),
         ],
         [],
         8,
     )
 
     settled, _, hidden_vectors, *hidden_grads = hidden_made
-    back_made, (d_mixed, input_gain_grad, input_shift_grad, d_rows), (result,), hidden_theirs = exchange(
+    result_part, d_branch = lax.optimization_barrier((dot32(settled, down_own).astype(low), d_branch))
+    result_rows = lax.psum_scatter(result_part, SEQ, scatter_dimension=0, tiled=True)
+    back_made, (text_grad, input_gain_grad, input_shift_grad, d_rows), hidden_theirs = exchange(
         AttendBackFront(
             d_branch,
             out_own,
             inner_hat,
             inner_factor,
-            inner_gain_own,
+            line(inner_gain),
             (attended, query_rot, keys_rot, values, log_total),
             tables,
-            segment_all,
+            segment,
+            column,
             normed,
             inner_low,
             model_width,
@@ -2168,8 +2312,8 @@
                 None,
                 qkv_own,
                 True,
-                (mixed_in, d_middle, wide(input_gain)),
-                (ROWS, ROWS, ALL),
+                (mixed_in, d_middle, line(input_gain), target_rows),
+                (ROWS, ROWS, ALL, ALL),
                 ((rows_wide, ROWS), (vector_out, ALL), (vector_out, ALL)),
                 norm_back_step,
                 True,
@@ -2177,56 +2321,40 @@
         ],
         [CrossGrads(hidden_grads, (INWARD, OUTWARD))],
         10,
-        Stream(
-            group_rows,
-            settled,
-            down_own,
-            False,
-            (middle,),
-            (ROWS,),
-            ((jax.ShapeDtypeStruct((row_count, model_width), low), ROWS),),
-            last_step,
-            False,
-        ),
     )
     inner_vectors, *layer_grads = back_made
-    text_grad = jnp.where(taken_own > 0.5, 0.0, d_mixed)
-
-    own_vectors = jnp.concatenate(
-        [inner_vectors[0], inner_vectors[1], hidden_vectors[2], hidden_vectors[0], hidden_vectors[1]]
-    )
-    row_vectors = jnp.concatenate(
-        [input_gain_grad[0], input_shift_grad[0], middle_gain_grad[0], middle_shift_grad[0]]
-    )
-    packed = jnp.concatenate([row_vectors, own_vectors]).reshape(-1, LANES)
-    spare = -packed.shape[0] % 8
-    packed = jnp.pad(packed, ((0, spare), (0, 0)))
+    row_vectors = (input_gain_grad, input_shift_grad, middle_gain_grad, middle_shift_grad)
+    own_vectors = (
+        (inner_vectors, 0),
+        (inner_vectors, 1),
+        (hidden_vectors, 2),
+        (hidden_vectors, 0),
+        (hidden_vectors, 1),
+    )
     layer_sides = (INWARD, INWARD, INWARD, OUTWARD)
-    owned, (spread, resample_query_grad, latent_grad) = finale(
+    owned, (spread, resample_query_grad, latent_grad, result) = finale(
         list(zip(hidden_grads, hidden_theirs)),
         (INWARD, OUTWARD),
         layer_grads,
         layer_sides,
         (d_rows, pictures, image_keys, probe, mixed_placed, image_out_own, target_rows),
-        packed,
-        latents.astype(f32).T,
-        resample_query.astype(f32),
+        row_vectors,
+        own_vectors,
+        latents,
+        resample_query,
+        (result_rows, middle),
         12,
     )
-    up_sum, down_sum, query_sum, key_sum, value_sum, out_sum, image_key_sum, image_value_sum, image_out_sum = widened(owned)
-    spread = spread.reshape(PLANE, -1)
-    first = LAT * own_width
-    row_sums = spread[:, first : first + row_vectors.shape[0]].sum(0).reshape(4, model_width)
-    own_sums = spread[:, first + row_vectors.shape[0] :]
-
-    def joined(start, width):
-        return own_sums[:, start : start + width].reshape(-1)
-
-    inner_gain_sum = joined(0, own_width)
-    inner_shift_sum = joined(own_width, own_width)
-    up_bias_sum = joined(2 * own_width, own_hidden)
-    hidden_gain_sum = joined(2 * own_width + own_hidden, own_hidden)
-    hidden_shift_sum = joined(2 * own_width + 2 * own_hidden, own_hidden)
+    widths = (own_width, own_width, own_hidden, own_hidden, own_hidden)
+    grads, passed, row_sums, own_sums = widened(
+        owned, (result, text_grad, resample_query_grad, latent_grad), spread, model_width, len(row_vectors), widths
+    )
+    up_sum, down_sum, query_sum, key_sum, value_sum, out_sum, image_key_sum, image_value_sum, image_out_sum = grads
+    result, text_grad, resample_query_grad, latent_grad = passed
+    row_sums = [vector.reshape(-1) for vector in row_sums]
+    inner_gain_sum, inner_shift_sum, up_bias_sum, hidden_gain_sum, hidden_shift_sum = (
+        vector.reshape(-1) for vector in own_sums
+    )
 
     return (
         result[None],

time: 537 us -> 486 us (0.905)
  Pallas kernels: 481 us -> 455 us
  local copies, waits for them, and re-layouts: 17.8 us -> 0.77 us
  other arithmetic: 14.4 us -> 1.48 us
  matrix products: 0 us -> 5.54 us
    pallas_call x5, Pallas kernels: 421 us -> 394 us  [lazy_call(): pl.pallas_call(body, out_shape=tuple(out_shapes), in_specs=[ANYWHERE if f...]
    broadcast_in_dim x9 -> x0, other arithmetic: 10.1 us -> none  [the longest x8 8.99 us: wide(): return vector.astype(f32)[None, :]]
    unnamed x38 -> x2, local copies, waits for them, and re-layouts: 8.22 us -> 0.01 us
    dot_general x0 -> x1, matrix products: none -> 5.54 us  [dot32(): return jnp.dot(left, right, preferred_element_type=jnp.float32)]
  transfers between devices with their start and end apart: 1 -> 1, of which waited for: 0 -> 0; matrix products, arithmetic and copies ran while one was open for 3% -> 0% of each run, Pallas kernels for 17% -> 18%
where the time goes in v4:
time: 486 us; the launch traced here: 477 us
  Pallas kernels  455 us (94%)
  between operations  14.6 us (3%)
  matrix products  5.54 us (1%)
    pallas_call x5, Pallas kernels, lazy_call(): pl.pallas_call(body, out_shape=tuple(out_shapes), in_specs=[ANYWHERE if f...  394 us
    pallas_call x1, Pallas kernels, intake(): pl.pallas_call(kernel, out_shape=tuple(outs), in_specs=[ANYWHERE] * (n_ro...  54.1 us
  transfers between devices with their start and end apart: 1, of which 0 were waited for; matrix products, arithmetic and copies ran while one was open for 0% of the time, Pallas kernels for 18%

profile of v4, /device:TPU:0, one launch (start us, length us, event | category | flops | bytes accessed | tf_op | source)
XLA Modules:
  0.0 477.0 jit_solution(17185549129155506625)
XLA Ops:
  7.2 0.0 reduce-scatter.2.cloned.1.call-start
  7.2 0.7 multiply_reduce_fusion
  7.9 0.1 mul.11
  8.0 0.7 fusion
  8.7 0.1 iota_add_fusion
  8.8 0.7 add.28.refs_5_.refs_9_.refs_21_.refs_0_
  9.5 54.1 %shard_map.417 = (bf16[4096,1024]{1,0:T(8,128)(2,1)}, bf16[1024,128]{1,0:T(8,128)(2,1)}, bf16[1024,128]{1,0:T(8,128)(2,1)}, bf16[2048,128]{1,0:T(8,128)(2,1)}, b...) custom-call(bf16[512,1024]{1,0:T(8,128)(2,1)} %bitcast.28, bf16[64,1024]{1,0:T(8,128)(2,1)} %refs_1_.1, ...), custom_call_target="tpu_custom_call" | custom-call | tf_op jit(solution)/shard_map/pallas_call | solution.py:848
  63.6 76.6 %shard_map.418 = (bf16[4096,256]{1,0:T(8,128)(2,1)}, bf16[1024,128]{1,0:T(8,128)(2,1)}, bf16[64,128]{1,0:T(8,128)(2,1)}, f32[1024,128]{1,0:T(8,128)}, f32[1024,1...) custom-call(bf16[4096,1024]{1,0:T(8,128)(2,1)} %get-tuple-element.10, ...), custom_call_target="tpu_custom_call" | custom-call | tf_op jit(solution)/shard_map/pallas_call | solution.py:1600
  140.2 86.0 %shard_map.419 = (bf16[1024,128]{1,0:T(8,128)(2,1)}, bf16[1024,128]{1,0:T(8,128)(2,1)}, bf16[1024,128]{1,0:T(8,128)(2,1)}, f32[1024,128]{1,0:T(8,128)}, f32[1024...) custom-call(bf16[1024,2048]{1,0:T(8,128)(2,1)} %get-tuple-element.11, ...), custom_call_target="tpu_custom_call" | custom-call | tf_op jit(solution)/shard_map/pallas_call | solution.py:1600
  226.2 0.0 copy-start
  226.2 75.0 %shard_map.420 = (bf16[1024,512]{1,0:T(8,128)(2,1)}, bf16[1024,512]{1,0:T(8,128)(2,1)}, f32[8,512]{1,0:T(8,128)}, bf16[8,2,128,512]{3,2,1,0:T(8,128)(2,1)}, bf16...) custom-call(bf16[1024,2048]{1,0:T(8,128)(2,1)} %get-tuple-element.12, ...), custom_call_target="tpu_custom_call" | custom-call | tf_op jit(solution)/shard_map/pallas_call | solution.py:1600
  301.2 0.0 copy-done
  301.2 5.5 %convolution_convert_fusion = bf16[1024,2048]{1,0:T(8,128)(2,1)} fusion(bf16[1024,512]{1,0:T(8,128)(2,1)} %get-tuple-element.127, bf16[512,2048]{1,0:T(8,128)(2,1)S(1)} %copy-done), kind=kOutput, calls=%fused_computation | convolution fusion | flops 2149580800 | bytes 7340032 | tf_op jit(solution)/shard_map/dot_general | solution.py:2110
  306.7 0.0 reduce-scatter.2.cloned.1.call-update
  306.7 88.0 %shard_map.421 = (f32[8,128]{1,0:T(8,128)}, bf16[8,2,128,128]{3,2,1,0:T(8,128)(2,1)}, bf16[8,2,128,128]{3,2,1,0:T(8,128)(2,1)}, bf16[8,2,128,128]{3,2,1,0:T(8,12...) custom-call(bf16[1024,2048]{1,0:T(8,128)(2,1)} %get-tuple-element.12, ...), custom_call_target="tpu_custom_call" | custom-call | tf_op jit(solution)/shard_map/pallas_call | solution.py:1600
  394.7 0.0 reduce-scatter.2.cloned.1.call-done.refs_26_.refs_27_
  394.8 68.0 %shard_map.422 = (bf16[128,4096]{1,0:T(8,128)(2,1)}, bf16[4096,128]{1,0:T(8,128)(2,1)}, bf16[128,1024]{1,0:T(8,128)(2,1)}, bf16[128,1024]{1,0:T(8,128)(2,1)}, bf...) custom-call(s32[1,1024]{1,0:T(1,128)} %add.28.refs_5_.refs_9_.refs_2, ...), custom_call_target="tpu_custom_call" | custom-call | tf_op jit(solution)/shard_map/pallas_call | solution.py:1600
  462.8 6.9 %shard_map.423 = (f32[128,4096]{1,0:T(8,128)}, f32[4096,128]{1,0:T(8,128)}, f32[128,1024]{1,0:T(8,128)}, f32[128,1024]{1,0:T(8,128)}, f32[128,1024]{1,0:T(8,128)...) custom-call(bf16[128,4096]{1,0:T(8,128)(2,1)} %get-tuple-element.158, ...), custom_call_target="tpu_custom_call" | custom-call | tf_op jit(solution)/shard_map/pallas_call | solution.py:2029
Async XLA Ops:
  7.2 387.6 %reduce-scatter.2.cloned.1.call-start = ((), (), s32[]{:S(2)}) async-start(), calls=%async_computation.1 | async-start | bytes 4718592 | tf_op jit(solution)/shard_map/reduce_scatter | solution.py:2293
  226.2 75.0 %copy-start = (bf16[512,2048]{1,0:T(8,128)(2,1)S(1)}, bf16[512,2048]{1,0:T(8,128)(2,1)}, u32[]{:S(2)}) copy-start(bf16[512,2048]{1,0:T(8,128)(2,1)} %get-tuple-element.125.refs_4_) | copy-start | bytes 6291460
Sparse Core Ops, SparseCore 0:
  306.9 60.6 reduce-scatter.1

commit v5 on v4

--- a/solution.py
+++ b/solution.py
@@ -584,6 +584,10 @@
 PIECE_ROWS = (32, 32, 32, 32)
 PIECES = len(PIECE_ROWS)
 SECOND_LAG = 2
+PACE_IMAGE = (0, 7, 7, 7, 7)
+PACE_ATTEND = (0, 1, 1, 0)
+WORK_FROM = 0
+PACE_BACK = (1, 0, 0, 0, 2, 2, 2, 2)
 FRONT, BACK, ALL, ROWS, INWARD, OUTWARD, SHARED = range(7)
 
 
@@ -1314,19 +1318,38 @@
         both_w[:, width:] = value_w[...]
         probe[...] = jnp.dot(latent_all[...], probe_w[...], preferred_element_type=jnp.float32).astype(jnp.bfloat16)
         yield
-        for image in range(pictures.shape[0] // PATCH):
-            rows = slice(image * PATCH, (image + 1) * PATCH)
-            if image % IMAGES_A_STEP == 0:
-                more = slice(image * PATCH, (image + IMAGES_A_STEP) * PATCH)
-                keys[more, :] = jnp.dot(
-                    pictures[more, :], both_w[...], preferred_element_type=jnp.float32
+        heads = range(0, width, HEAD)
+        for group in range(0, pictures.shape[0] // PATCH, IMAGES_A_STEP):
+            more = slice(group * PATCH, (group + IMAGES_A_STEP) * PATCH)
+            both = jnp.dot(pictures[more, :], both_w[...], preferred_element_type=jnp.float32).astype(jnp.bfloat16)
+            keys[more, :] = both
+            scores = [
+                lax.dot_general(
+                    probe[:, first : first + HEAD] * scale,
+                    both[:, first : first + HEAD],
+                    (((1,), (1,)), ((), ())),
+                    preferred_element_type=jnp.float32,
+                )
+                for first in heads
+            ]
+            parts = [(image, head) for image in range(IMAGES_A_STEP) for head in range(len(heads))]
+            rows = [slice(image * PATCH, (image + 1) * PATCH) for image in range(IMAGES_A_STEP)]
+            cut = [scores[head][:, rows[image]] for image, head in parts]
+            best = [jnp.max(part, -1, keepdims=True) for part in cut]
+            weights = [jnp.exp(part - top) for part, top in zip(cut, best)]
+            totals = [jnp.sum(part, -1, keepdims=True) for part in weights]
+            probs = [(part * (1.0 / total)).astype(jnp.bfloat16) for part, total in zip(weights, totals)]
+            mixed = [
+                jnp.dot(
+                    part,
+                    both[rows[image], width + head * HEAD : width + (head + 1) * HEAD],
+                    preferred_element_type=jnp.float32,
                 ).astype(jnp.bfloat16)
-            mixed = []
-            for first in range(0, width, HEAD):
-                probs = image_probs_of(probe[:, first : first + HEAD], keys[rows, first : first + HEAD], scale)
-                values = keys[rows, width + first : width + first + HEAD]
-                mixed.append(jnp.dot(probs.astype(jnp.bfloat16), values, preferred_element_type=jnp.float32))
-            mixed_all[image * LAT : (image + 1) * LAT, :] = jnp.concatenate(mixed, 1).astype(jnp.bfloat16)
+                for part, (image, head) in zip(probs, parts)
+            ]
+            for image in range(IMAGES_A_STEP):
+                at = slice((group + image) * LAT, (group + image + 1) * LAT)
+                mixed_all[at, :] = jnp.concatenate(mixed[image * len(heads) : (image + 1) * len(heads)], 1)
             yield
         for first in range(0, placed.shape[0], PATCH):
             chosen = chosen_rows(target_rows, first, PATCH)
@@ -1363,21 +1386,27 @@
             k_out[at, :] = ((lin * cosine + halves_swapped(lin) * sine) * (1.0 / growth)).astype(low_type)
             v_out[at, :] = linear[:, 2 * width :].astype(low_type)
             allowed = allowed_part(column, segment, first, ATTEND_ROWS, keys)
-            for head in range(width // HEAD):
-                lanes = slice(head * HEAD, (head + 1) * HEAD)
-                scores = lax.dot_general(
+            heads = [slice(start, start + HEAD) for start in range(0, width, HEAD)]
+            scores = [
+                lax.dot_general(
                     q_out[at, lanes] * scale,
                     k_out[:keys, lanes],
                     (((1,), (1,)), ((), ())),
                     preferred_element_type=f32,
                 )
-                scores = jnp.where(allowed, scores, -1e30)
-                best = jnp.max(scores, -1, keepdims=True)
-                weights = jnp.exp(scores - best)
-                total = jnp.sum(weights, -1, keepdims=True)
-                probs = (weights * (1.0 / total)).astype(low_type)
-                att_out[at, lanes] = jnp.dot(probs, v_out[:keys, lanes], preferred_element_type=f32)
-                lse_out[at, head : head + 1] = best + jnp.log(total)
+                for lanes in heads
+            ]
+            scores = [jnp.where(allowed, part, -1e30) for part in scores]
+            best = [jnp.max(part, -1, keepdims=True) for part in scores]
+            weights = [jnp.exp(part - top) for part, top in zip(scores, best)]
+            totals = [jnp.sum(part, -1, keepdims=True) for part in weights]
+            probs = [(part * (1.0 / total)).astype(low_type) for part, total in zip(weights, totals)]
+            mixed = [
+                jnp.dot(part, v_out[:keys, lanes], preferred_element_type=f32) for part, lanes in zip(probs, heads)
+            ]
+            for head, lanes in enumerate(heads):
+                att_out[at, lanes] = mixed[head]
+                lse_out[at, head : head + 1] = best[head] + jnp.log(totals[head])
             rows = att_out[at, :]
             sums = [jnp.sum(rows, 1, keepdims=True), jnp.sum(rows * rows, 1, keepdims=True)]
             self.held[1][:, at] = as_lanes(sums)[:2]
@@ -1399,22 +1428,19 @@
             for product in products:
                 self.launches.append(functools.partial(self.part, *product, seq))
 
-    def part(self, left, right, outs, side, seq):
+    def part(self, left, right, out, side, seq):
         span = (left.shape[1] if side == INWARD else right.shape[1]) // PLANE
         at = slice(seq * span, (seq + 1) * span)
         contract = (((0,), (0,)), ((), ()))
+        half = span // 2
         if side == OUTWARD:
-            outs[0][:, at] = lax.dot_general(
+            out[:, at] = lax.dot_general(
                 left[...], right[:, at], contract, preferred_element_type=jnp.float32
             ).astype(jnp.bfloat16)
-            return
-        made = lax.dot_general(left[:, at], right[...], contract, preferred_element_type=jnp.float32)
-        made = made.astype(jnp.bfloat16)
-        half = span // 2
-        for number, out in enumerate(outs):
-            width = out.shape[3]
-            piece = made[:, number * width : (number + 1) * width]
-            out[seq, 0], out[seq, 1] = piece[:half], piece[half:]
+        else:
+            made = lax.dot_general(left[:, at], right[...], contract, preferred_element_type=jnp.float32)
+            made = made.astype(jnp.bfloat16)
+            out[seq, 0], out[seq, 1] = made[:half], made[half:]
 
 
 def grad_shape(model_width, rows, side):
@@ -1435,12 +1461,13 @@
             jax.ShapeDtypeStruct((8, width), jnp.float32),
             grad_shape(model_width, width, INWARD),
             grad_shape(model_width, width, OUTWARD),
+            jax.ShapeDtypeStruct((rows, model_width), jnp.bfloat16),
         ]
         self.scratch = self.total_scratch(4, rows) + [pltpu.VMEM((rows, width), jnp.float32)] * 3
 
     def run(self):
         lifted, up_w, bias, cotangent_all, down_w, gain, shift = self.ins
-        settled, d_hidden, vectors, up, down = self.outs
+        settled, d_hidden, vectors, up, down, result = self.outs
         activated, slope, d_settled = self.held[6:]
         f32 = jnp.float32
         bias, gain, shift = (own_line(self.here, line, settled.shape[1]) for line in (bias, gain, shift))
@@ -1481,7 +1508,13 @@
             bias_sum += jnp.sum(low.astype(f32), 0, keepdims=True)
         vectors[...] = jnp.zeros_like(vectors)
         vectors[0:1, :], vectors[1:2, :], vectors[2:3, :] = gain_sum, shift_sum, bias_sum
-        self.grads([(lifted, d_hidden, [up], INWARD), (settled, cotangent_all, [down], OUTWARD)])
+        def result_part(first):
+            at = slice(first, first + step)
+            result[at, :] = jnp.dot(settled[at, :], down_w[...], preferred_element_type=f32).astype(jnp.bfloat16)
+
+        for first in range(0, rows, step):
+            self.launches.append(functools.partial(result_part, first))
+        self.grads([(lifted, d_hidden, up, INWARD), (settled, cotangent_all, down, OUTWARD)])
         self.lefts = [d_hidden, settled]
 
 
@@ -1494,7 +1527,7 @@
         model_width = normed.shape[1]
         low_type, f32 = jnp.bfloat16, jnp.float32
         self.out_shapes = [jax.ShapeDtypeStruct((8, width), f32)]
-        self.out_shapes += [grad_shape(model_width, width, INWARD)] * 3 + [grad_shape(model_width, width, OUTWARD)]
+        self.out_shapes += [grad_shape(model_width, 3 * width, INWARD), grad_shape(model_width, width, OUTWARD)]
         self.scratch = self.total_scratch(2, rows)
         self.scratch += [pltpu.VMEM((rows, width), low_type), pltpu.VMEM((rows, 3 * width), low_type)]
         self.scratch += [pltpu.VMEM((rows, width), f32)] * 4
@@ -1503,7 +1536,7 @@
         d_branch, out_part, hat, factor, gain, attended, q_ref, k_ref, v_ref, lse = self.ins[:10]
         cos_ref, sin_ref, grow_ref, segment, column, normed, inner_low = self.ins[10:]
         gain = own_line(self.here, gain, hat.shape[1])
-        vectors, *grads = self.outs
+        vectors, lin_grad, out_grad = self.outs
         d_att, lin_out, d_inner, d_query, d_key, d_value = self.held[6:]
         rows_all, width = hat.shape
         f32, low_type = jnp.float32, jnp.bfloat16
@@ -1530,38 +1563,44 @@
         for first in range(0, rows_all, ATTEND_ROWS):
             at, keys = slice(first, first + ATTEND_ROWS), first + ATTEND_ROWS
             allowed = allowed_part(column, segment, first, ATTEND_ROWS, keys)
-            for head in range(heads):
-                lanes = slice(head * HEAD, (head + 1) * HEAD)
-                scores = lax.dot_general(
-                    q_ref[at, lanes] * scale,
-                    k_ref[:keys, lanes],
-                    (((1,), (1,)), ((), ())),
-                    preferred_element_type=f32,
+            contract_last, contract_first = (((1,), (1,)), ((), ())), (((0,), (0,)), ((), ()))
+            lanes_of = [slice(head * HEAD, (head + 1) * HEAD) for head in range(heads)]
+            d_rows = [d_att[at, lanes] for lanes in lanes_of]
+            scores = [
+                lax.dot_general(
+                    q_ref[at, lanes] * scale, k_ref[:keys, lanes], contract_last, preferred_element_type=f32
                 )
-                scores = jnp.where(allowed, scores, -1e30)
-                probs = jnp.exp(scores - lse[at, head : head + 1])
-                d_rows = d_att[at, lanes]
-                d_probs = lax.dot_general(
-                    d_rows, v_ref[:keys, lanes], (((1,), (1,)), ((), ())), preferred_element_type=f32
+                for lanes in lanes_of
+            ]
+            d_probs = [
+                lax.dot_general(d, v_ref[:keys, lanes], contract_last, preferred_element_type=f32)
+                for d, lanes in zip(d_rows, lanes_of)
+            ]
+            deltas = [
+                jnp.sum(d.astype(f32) * attended[at, lanes], -1, keepdims=True) for d, lanes in zip(d_rows, lanes_of)
+            ]
+            probs = [
+                jnp.exp(jnp.where(allowed, part, -1e30) - lse[at, head : head + 1])
+                for head, part in enumerate(scores)
+            ]
+            d_scores = [(p * (d - delta)).astype(low_type) for p, d, delta in zip(probs, d_probs, deltas)]
+            for head, lanes in enumerate(lanes_of):
+                d_query[at, lanes] = (
+                    jnp.dot(d_scores[head], k_ref[:keys, lanes], preferred_element_type=f32) * scale
                 )
-                delta = jnp.sum(d_rows.astype(f32) * attended[at, lanes], -1, keepdims=True)
-                d_scores = (probs * (d_probs - delta)).astype(low_type)
-                d_query[at, lanes] = jnp.dot(d_scores, k_ref[:keys, lanes], preferred_element_type=f32) * scale
                 key_part = (
-                    lax.dot_general(
-                        d_scores, q_ref[at, lanes], (((0,), (0,)), ((), ())), preferred_element_type=f32
-                    )
+                    lax.dot_general(d_scores[head], q_ref[at, lanes], contract_first, preferred_element_type=f32)
                     * scale
                 )
                 value_part = lax.dot_general(
-                    probs.astype(low_type), d_rows, (((0,), (0,)), ((), ())), preferred_element_type=f32
+                    probs[head].astype(low_type), d_rows[head], contract_first, preferred_element_type=f32
                 )
                 if first:
                     d_key[:first, lanes] += key_part[:first]
                     d_value[:first, lanes] += value_part[:first]
                 d_key[first:keys, lanes] = key_part[first:]
                 d_value[first:keys, lanes] = value_part[first:]
-                yield
+            yield
         for first in range(0, rows_all, ATTEND_ROWS):
             at = slice(first, first + ATTEND_ROWS)
             cosine, sine, growth = cos_ref[at, :], sin_ref[at, :], grow_ref[at, :]
@@ -1572,8 +1611,8 @@
             lin_out[at, 2 * width :] = d_value[at, :].astype(low_type)
         self.grads(
             [
-                (normed, lin_out, grads[:3], INWARD),
-                (inner_low, d_branch, grads[3:], OUTWARD),
+                (normed, lin_out, lin_grad, INWARD),
+                (inner_low, d_branch, out_grad, OUTWARD),
             ]
         )
         self.lefts = [lin_out]
@@ -1609,10 +1648,9 @@
     )(*inputs)
 
 
-def exchange(front, streams, riders, cid, early=None, pace=1, early_pace=5):
+def exchange(front, streams, riders, cid, pace=(), between=0, work_from=0):
     fronts = [front] if front is not None else []
-    earlies = [early] if early is not None else []
-    sums = list(streams) + earlies
+    sums = list(streams)
     parts = fronts + sums + list(riders)
 
     def kernel(ins, outs, held):
@@ -1637,38 +1675,36 @@
         else:
             peers += [here.core, here.x, here.y]
         greet(peers)
-        waiting, crossing = [], []
+        waiting, work = [], []
         for rider in riders:
             rider.start()
             if rider.later:
                 take_some(rider.launches, len(rider.launches))
             waiting += rider.launches + rider.later
-        early_steps = []
-        if early is not None:
-            early.begin()
-            early_steps = early.phases()
-            take_some(early_steps, 1)
         if front is not None:
-            for number, _ in enumerate(front.run(), 1):
-                take_some(waiting, pace)
-                if number % early_pace == 0 and len(early_steps) > 1:
-                    take_some(early_steps, 1)
+            allowed = list(pace)
+            for _ in front.run():
+                take_some(waiting, allowed.pop(0) if allowed else 0)
             for stream, left in zip(streams, front.lefts):
                 stream.left = left
-            waiting += front.launches
+            work = front.launches
         for stream in streams:
             stream.begin()
         stages = []
         for number, stream in reversed(list(enumerate(streams))):
             stages += [(lag + number * SECOND_LAG, stage) for lag, stage in stream.stages()]
         ticks = ticks_of(stages, PIECES)
-        share = -(-len(waiting) // max(len(ticks) - 2, 1))
+        share, last = -(-len(work) // max(len(ticks) - 2 - work_from, 1)), PIECES + 1
         for number, tick in enumerate(ticks):
             tick()
-            if number >= PIECES:
-                take_some(early_steps, 1)
-            take_some(waiting, share)
-        take_some(early_steps, len(early_steps))
+            if number >= work_from:
+                take_some(work, share)
+            if number < 2:
+                take_some(waiting, between)
+            if number >= last:
+                take_some(waiting, -(-len(waiting) // max(len(ticks) - 1 - number, 1)))
+        take_some(work, len(work))
+        take_some(waiting, len(waiting))
         for part in parts:
             part.finish()
 
@@ -1820,32 +1856,42 @@
             take_some(waiting, 1)
         cross(total - 1)
         d_probe_sum = jnp.zeros(probe_ref.shape, f32)
-        for number in range(images):
-            rows = slice(number * PATCH, (number + 1) * PATCH)
-            d_here = d_mixed[number * LAT : (number + 1) * LAT, :]
-            d_probe = []
-            for first in range(0, width, HEAD):
-                at = slice(first, first + HEAD)
-                keys_here = keys_ref[rows, at]
-                values = keys_ref[rows, width + first : width + first + HEAD]
-                probs = image_probs_of(probe_ref[:, at], keys_here, scale)
-                d_probs = lax.dot_general(
-                    d_here[:, at], values, (((1,), (1,)), ((), ())), preferred_element_type=f32
-                )
-                d_scores = probs * (d_probs - jnp.sum(probs * d_probs, -1, keepdims=True))
-                d_scores = d_scores.astype(low_type)
-                d_probe.append(jnp.dot(d_scores, keys_here, preferred_element_type=f32) * scale)
-                d_both[rows, at] = (
-                    lax.dot_general(
-                        d_scores, probe_ref[:, at], (((0,), (0,)), ((), ())), preferred_element_type=f32
-                    )
-                    * scale
-                ).astype(low_type)
-                d_both[rows, width + first : width + first + HEAD] = lax.dot_general(
-                    probs.astype(low_type), d_here[:, at], (((0,), (0,)), ((), ())), preferred_element_type=f32
-                ).astype(low_type)
-            d_probe_sum += jnp.concatenate(d_probe, 1)
-            take_some(waiting, 2)
+        heads = range(0, width, HEAD)
+        for group in range(0, images, IMAGES_A_STEP):
+            parts = [(image, first) for image in range(group, group + IMAGES_A_STEP) for first in heads]
+            contract_last, contract_first = (((1,), (1,)), ((), ())), (((0,), (0,)), ((), ()))
+            keys_of = [keys_ref[i * PATCH : (i + 1) * PATCH, f : f + HEAD] for i, f in parts]
+            values_of = [keys_ref[i * PATCH : (i + 1) * PATCH, width + f : width + f + HEAD] for i, f in parts]
+            probe_of = [probe_ref[:, f : f + HEAD] for _, f in parts]
+            d_of = [d_mixed[i * LAT : (i + 1) * LAT, f : f + HEAD] for i, f in parts]
+            scores = [
+                lax.dot_general(p * scale, k, contract_last, preferred_element_type=f32)
+                for p, k in zip(probe_of, keys_of)
+            ]
+            d_probs = [
+                lax.dot_general(d, v, contract_last, preferred_element_type=f32) for d, v in zip(d_of, values_of)
+            ]
+            best = [jnp.max(part, -1, keepdims=True) for part in scores]
+            weights = [jnp.exp(part - top) for part, top in zip(scores, best)]
+            totals = [jnp.sum(part, -1, keepdims=True) for part in weights]
+            probs = [part * (1.0 / whole) for part, whole in zip(weights, totals)]
+            deltas = [jnp.sum(p * d, -1, keepdims=True) for p, d in zip(probs, d_probs)]
+            d_scores = [(p * (d - delta)).astype(low_type) for p, d, delta in zip(probs, d_probs, deltas)]
+            d_probe = [jnp.dot(d, k, preferred_element_type=f32) for d, k in zip(d_scores, keys_of)]
+            d_keys = [
+                lax.dot_general(d, p, contract_first, preferred_element_type=f32) for d, p in zip(d_scores, probe_of)
+            ]
+            d_values = [
+                lax.dot_general(p.astype(low_type), d, contract_first, preferred_element_type=f32)
+                for p, d in zip(probs, d_of)
+            ]
+            for number, (image, first) in enumerate(parts):
+                rows = slice(image * PATCH, (image + 1) * PATCH)
+                d_both[rows, first : first + HEAD] = (d_keys[number] * scale).astype(low_type)
+                d_both[rows, width + first : width + first + HEAD] = d_values[number].astype(low_type)
+            for number in range(0, len(parts), len(heads)):
+                d_probe_sum += jnp.concatenate(d_probe[number : number + len(heads)], 1) * scale
+            take_some(waiting, 8)
         small_own[:LAT, :] = d_probe_sum
         small_cross = remote(small_own, small_theirs, s_send.at[0], s_recv.at[0], here.img_peer)
         small_cross.start()
@@ -1977,9 +2023,12 @@
     return made[:total], made[total:]
 
 
-def widened(grads, passed, spread, model_width, n_rows, widths):
+def widened(grads, splits, passed, spread, model_width, n_rows, widths):
     f32, dma = jnp.float32, pltpu.SemaphoreType.DMA
-    n, n_passed = len(grads), len(passed)
+    n, n_passed, n_wide = len(grads), len(passed), sum(splits)
+    wide_shapes = []
+    for array, split in zip(grads, splits):
+        wide_shapes += [jax.ShapeDtypeStruct((array.shape[0], array.shape[1] // split), f32)] * split
 
     def kernel(*refs):
         refs = list(refs)
@@ -1990,18 +2039,28 @@
             return taken
 
         ins, passed_ins, (spread_ref,) = take(n), take(n_passed), take(1)
-        outs, passed_outs, row_outs, own_outs = take(n), take(n_passed), take(n_rows), take(len(widths))
-        narrow, wide, held, (in_sems, out_sems, passed_sems) = take(n), take(n), take(n_passed), take(3)
+        outs, passed_outs, row_outs, own_outs = take(n_wide), take(n_passed), take(n_rows), take(len(widths))
+        narrow, wide, held, (in_sems, out_sems, passed_sems) = take(n), take(n_wide), take(n_passed), take(3)
         copies_in = [pltpu.make_async_copy(src, dst, in_sems.at[i]) for i, (src, dst) in enumerate(zip(ins, narrow))]
         copies_out = [pltpu.make_async_copy(src, dst, out_sems.at[i]) for i, (src, dst) in enumerate(zip(wide, outs))]
         held_in = [pltpu.make_async_copy(src, dst, passed_sems.at[0, i]) for i, (src, dst) in enumerate(zip(passed_ins, held))]
         held_out = [pltpu.make_async_copy(src, dst, passed_sems.at[1, i]) for i, (src, dst) in enumerate(zip(held, passed_outs))]
         for copy in copies_in + held_in:
             copy.start()
-        for i in range(n):
+        made = 0
+        for i, split in enumerate(splits):
             copies_in[i].wait()
-            wide[i][...] = narrow[i][...].astype(f32)
-            copies_out[i].start()
+            if split == 1:
+                wide[made][...] = narrow[i][...].astype(f32)
+            else:
+                width = narrow[i].shape[1] // (split * PLANE)
+                for seq in range(PLANE):
+                    for part in range(split):
+                        at = (seq * split + part) * width
+                        wide[made + part][:, seq * width : (seq + 1) * width] = narrow[i][:, at : at + width].astype(f32)
+            for part in range(split):
+                copies_out[made + part].start()
+            made += split
         for arrive, leave in zip(held_in, held_out):
             arrive.wait()
             leave.start()
@@ -2021,7 +2080,7 @@
         for copy in copies_out + held_out:
             copy.wait()
 
-    shapes = [jax.ShapeDtypeStruct(array.shape, f32) for array in grads]
+    shapes = list(wide_shapes)
     shapes += [jax.ShapeDtypeStruct(array.shape, array.dtype) for array in passed]
     shapes += [jax.ShapeDtypeStruct((1, model_width), f32)] * n_rows
     shapes += [jax.ShapeDtypeStruct((1, PLANE * width), f32) for width in widths]
@@ -2030,14 +2089,15 @@
         kernel,
         out_shape=tuple(shapes),
         in_specs=[ANYWHERE] * (n + n_passed) + [ON_CHIP],
-        out_specs=tuple([ANYWHERE] * (n + n_passed) + [ON_CHIP] * small),
+        out_specs=tuple([ANYWHERE] * (n_wide + n_passed) + [ON_CHIP] * small),
         scratch_shapes=[pltpu.VMEM(array.shape, array.dtype) for array in grads]
-        + [pltpu.VMEM(array.shape, f32) for array in grads]
+        + [pltpu.VMEM(item.shape, f32) for item in wide_shapes]
         + [pltpu.VMEM(array.shape, array.dtype) for array in passed]
-        + [dma((n,)), dma((n,)), dma((2, n_passed))],
+        + [dma((n,)), dma((n_wide,)), dma((2, n_passed))],
         compiler_params=pltpu.CompilerParams(vmem_limit_bytes=VMEM_BYTES),
     )(*grads, *passed, spread)
     made = list(made)
+    n = n_wide
     cut = [made[:n], made[n : n + n_passed], made[n + n_passed : n + n_passed + n_rows]]
     return (*cut, made[n + n_passed + n_rows :])
 
@@ -2207,6 +2267,7 @@
             )
         ],
         3,
+        PACE_IMAGE,
     )
 
     def middle_step(total, piece, views, outs):
@@ -2234,7 +2295,7 @@
         ],
         [ChainWeights((down_weight,), (OUTWARD,), ((0, 0),)), GatherRows(cotangent[0])],
         5,
-        pace=2,
+        PACE_ATTEND,
     )
     *attended_kept, inner_low, inner_hat, inner_factor = attend_made
     query_rot, keys_rot, values, attended, log_total = attended_kept
@@ -2288,8 +2349,7 @@
         8,
     )
 
-    settled, _, hidden_vectors, *hidden_grads = hidden_made
-    result_part, d_branch = lax.optimization_barrier((dot32(settled, down_own).astype(low), d_branch))
+    _, _, hidden_vectors, *hidden_grads, result_part = hidden_made
     result_rows = lax.psum_scatter(result_part, SEQ, scatter_dimension=0, tiled=True)
     back_made, (text_grad, input_gain_grad, input_shift_grad, d_rows), hidden_theirs = exchange(
         AttendBackFront(
@@ -2321,6 +2381,9 @@
         ],
         [CrossGrads(hidden_grads, (INWARD, OUTWARD))],
         10,
+        PACE_BACK,
+        1,
+        WORK_FROM,
     )
     inner_vectors, *layer_grads = back_made
     row_vectors = (input_gain_grad, input_shift_grad, middle_gain_grad, middle_shift_grad)
@@ -2331,12 +2394,11 @@
         (hidden_vectors, 0),
         (hidden_vectors, 1),
     )
-    layer_sides = (INWARD, INWARD, INWARD, OUTWARD)
     owned, (spread, resample_query_grad, latent_grad, result) = finale(
         list(zip(hidden_grads, hidden_theirs)),
         (INWARD, OUTWARD),
         layer_grads,
-        layer_sides,
+        (INWARD, OUTWARD),
         (d_rows, pictures, image_keys, probe, mixed_placed, image_out_own, target_rows),
         row_vectors,
         own_vectors,
@@ -2347,7 +2409,13 @@
     )
     widths = (own_width, own_width, own_hidden, own_hidden, own_hidden)
     grads, passed, row_sums, own_sums = widened(
-        owned, (result, text_grad, resample_query_grad, latent_grad), spread, model_width, len(row_vectors), widths
+        owned,
+        (1, 1, 3, 1, 1, 1, 1),
+        (result, text_grad, resample_query_grad, latent_grad),
+        spread,
+        model_width,
+        len(row_vectors),
+        widths,
     )
     up_sum, down_sum, query_sum, key_sum, value_sum, out_sum, image_key_sum, image_value_sum, image_out_sum = grads
     result, text_grad, resample_query_grad, latent_grad = passed

time: 486 us -> 476 us (0.979)
  matrix products: 5.54 us -> 0 us
  Pallas kernels: 455 us -> 450 us
    dot_general x1 -> x0, matrix products: 5.54 us -> none  [dot32(): return jnp.dot(left, right, preferred_element_type=jnp.float32)]
where the time goes in v5:
time: 476 us; the launch traced here: 467 us
  Pallas kernels  450 us (95%)
  between operations  14.4 us (3%)
    pallas_call x5, Pallas kernels, lazy_call(): pl.pallas_call(body, out_shape=tuple(out_shapes), in_specs=[ANYWHERE if f...  389 us
    pallas_call x1, Pallas kernels, intake(): pl.pallas_call(kernel, out_shape=tuple(outs), in_specs=[ANYWHERE] * (n_ro...  54.1 us
  transfers between devices with their start and end apart: 1, of which 0 were waited for; matrix products, arithmetic and copies ran while one was open for 0% of the time, Pallas kernels for 18%

profile of v5, /device:TPU:0, one launch (start us, length us, event | category | flops | bytes accessed | tf_op | source)
XLA Modules:
  0.0 466.6 jit_solution(12336913243551285406)
XLA Ops:
  7.2 0.0 reduce-scatter.2.cloned.1.call-start
  7.2 0.7 multiply_reduce_fusion
  7.9 0.1 mul.11
  8.0 0.7 fusion
  8.7 0.1 iota_add_fusion
  8.8 0.7 add.28.refs_5_.refs_9_.refs_21_.refs_0_
  9.5 54.1 %shard_map.417 = (bf16[4096,1024]{1,0:T(8,128)(2,1)}, bf16[1024,128]{1,0:T(8,128)(2,1)}, bf16[1024,128]{1,0:T(8,128)(2,1)}, bf16[2048,128]{1,0:T(8,128)(2,1)}, b...) custom-call(bf16[512,1024]{1,0:T(8,128)(2,1)} %bitcast.26, bf16[64,1024]{1,0:T(8,128)(2,1)} %refs_1_.1, ...), custom_call_target="tpu_custom_call" | custom-call | tf_op jit(solution)/shard_map/pallas_call | solution.py:852
  63.6 77.8 %shard_map.418 = (bf16[4096,256]{1,0:T(8,128)(2,1)}, bf16[1024,128]{1,0:T(8,128)(2,1)}, bf16[64,128]{1,0:T(8,128)(2,1)}, f32[1024,128]{1,0:T(8,128)}, f32[1024,1...) custom-call(bf16[4096,1024]{1,0:T(8,128)(2,1)} %get-tuple-element.10, ...), custom_call_target="tpu_custom_call" | custom-call | tf_op jit(solution)/shard_map/pallas_call | solution.py:1639
  141.4 84.9 %shard_map.419 = (bf16[1024,128]{1,0:T(8,128)(2,1)}, bf16[1024,128]{1,0:T(8,128)(2,1)}, bf16[1024,128]{1,0:T(8,128)(2,1)}, f32[1024,128]{1,0:T(8,128)}, f32[1024...) custom-call(bf16[1024,2048]{1,0:T(8,128)(2,1)} %get-tuple-element.10, ...), custom_call_target="tpu_custom_call" | custom-call | tf_op jit(solution)/shard_map/pallas_call | solution.py:1639
  226.3 73.0 %shard_map.420 = (bf16[1024,512]{1,0:T(8,128)(2,1)}, bf16[1024,512]{1,0:T(8,128)(2,1)}, f32[8,512]{1,0:T(8,128)}, bf16[8,2,128,512]{3,2,1,0:T(8,128)(2,1)}, bf16...) custom-call(bf16[1024,2048]{1,0:T(8,128)(2,1)} %get-tuple-element.11, ...), custom_call_target="tpu_custom_call" | custom-call | tf_op jit(solution)/shard_map/pallas_call | solution.py:1639
  299.4 0.0 reduce-scatter.2.cloned.1.call-update
  299.4 85.2 %shard_map.421 = (f32[8,128]{1,0:T(8,128)}, bf16[8,2,128,384]{3,2,1,0:T(8,128)(2,1)}, bf16[128,2048]{1,0:T(8,128)(2,1)}, f32[128,2048]{1,0:T(8,128)}, f32[1,2048...) custom-call(bf16[1024,2048]{1,0:T(8,128)(2,1)} %get-tuple-element.12, ...), custom_call_target="tpu_custom_call" | custom-call | tf_op jit(solution)/shard_map/pallas_call | solution.py:1639
  384.6 0.0 reduce-scatter.2.cloned.1.call-done.refs_24_.refs_25_
  384.7 67.9 %shard_map.422 = (bf16[128,4096]{1,0:T(8,128)(2,1)}, bf16[4096,128]{1,0:T(8,128)(2,1)}, bf16[128,3072]{1,0:T(8,128)(2,1)}, bf16[1024,128]{1,0:T(8,128)(2,1)}, bf...) custom-call(s32[1,1024]{1,0:T(1,128)} %add.28.refs_5_.refs_9_.refs_2, ...), custom_call_target="tpu_custom_call" | custom-call | tf_op jit(solution)/shard_map/pallas_call | solution.py:1639
  452.6 6.9 %shard_map.423 = (f32[128,4096]{1,0:T(8,128)}, f32[4096,128]{1,0:T(8,128)}, f32[128,1024]{1,0:T(8,128)}, f32[128,1024]{1,0:T(8,128)}, f32[128,1024]{1,0:T(8,128)...) custom-call(bf16[128,4096]{1,0:T(8,128)(2,1)} %get-tuple-element.148, ...), custom_call_target="tpu_custom_call" | custom-call | tf_op jit(solution)/shard_map/pallas_call | solution.py:2088
Async XLA Ops:
  7.2 377.5 %reduce-scatter.2.cloned.1.call-start = ((), (), s32[]{:S(2)}) async-start(), calls=%async_computation.1 | async-start | bytes 4718592 | tf_op jit(solution)/shard_map/reduce_scatter | solution.py:2353
Sparse Core Ops, SparseCore 0:
  299.5 66.2 reduce-scatter.1

commit v6 on v5

--- a/solution.py
+++ b/solution.py
@@ -585,7 +585,7 @@
 PIECES = len(PIECE_ROWS)
 SECOND_LAG = 2
 PACE_IMAGE = (0, 7, 7, 7, 7)
-PACE_ATTEND = (0, 1, 1, 0)
+PACE_ATTEND = (0, 2, 2, 0)
 WORK_FROM = 0
 PACE_BACK = (1, 0, 0, 0, 2, 2, 2, 2)
 FRONT, BACK, ALL, ROWS, INWARD, OUTWARD, SHARED = range(7)
@@ -1694,7 +1694,7 @@
         for number, stream in reversed(list(enumerate(streams))):
             stages += [(lag + number * SECOND_LAG, stage) for lag, stage in stream.stages()]
         ticks = ticks_of(stages, PIECES)
-        share, last = -(-len(work) // max(len(ticks) - 2 - work_from, 1)), PIECES + 1
+        share, last = -(-len(work) // max(len(ticks) - 2 - work_from, 1)), PIECES - 2
         for number, tick in enumerate(ticks):
             tick()
             if number >= work_from:

time: 476 us -> 473 us (level)
  no operation moved by 1% of the time
where the time goes in v6:
time: 473 us; the launch traced here: 465 us
  Pallas kernels  448 us (95%)
  between operations  14.4 us (3%)
    pallas_call x5, Pallas kernels, lazy_call(): pl.pallas_call(body, out_shape=tuple(out_shapes), in_specs=[ANYWHERE if f...  387 us
    pallas_call x1, Pallas kernels, intake(): pl.pallas_call(kernel, out_shape=tuple(outs), in_specs=[ANYWHERE] * (n_ro...  54.1 us
  transfers between devices with their start and end apart: 1, of which 0 were waited for; matrix products, arithmetic and copies ran while one was open for 0% of the time, Pallas kernels for 18%

profile of v6, /device:TPU:0, one launch (start us, length us, event | category | flops | bytes accessed | tf_op | source)
XLA Modules:
  0.0 464.8 jit_solution(10761361625440921421)
XLA Ops:
  7.2 0.0 reduce-scatter.2.cloned.1.call-start
  7.2 0.7 multiply_reduce_fusion
  7.9 0.1 mul.11
  8.0 0.7 fusion
  8.7 0.1 iota_add_fusion
  8.8 0.7 add.28.refs_5_.refs_9_.refs_21_.refs_0_
  9.5 54.1 %shard_map.417 = (bf16[4096,1024]{1,0:T(8,128)(2,1)}, bf16[1024,128]{1,0:T(8,128)(2,1)}, bf16[1024,128]{1,0:T(8,128)(2,1)}, bf16[2048,128]{1,0:T(8,128)(2,1)}, b...) custom-call(bf16[512,1024]{1,0:T(8,128)(2,1)} %bitcast.26, bf16[64,1024]{1,0:T(8,128)(2,1)} %refs_1_.1, ...), custom_call_target="tpu_custom_call" | custom-call | tf_op jit(solution)/shard_map/pallas_call | solution.py:852
  63.6 74.6 %shard_map.418 = (bf16[4096,256]{1,0:T(8,128)(2,1)}, bf16[1024,128]{1,0:T(8,128)(2,1)}, bf16[64,128]{1,0:T(8,128)(2,1)}, f32[1024,128]{1,0:T(8,128)}, f32[1024,1...) custom-call(bf16[4096,1024]{1,0:T(8,128)(2,1)} %get-tuple-element.10, ...), custom_call_target="tpu_custom_call" | custom-call | tf_op jit(solution)/shard_map/pallas_call | solution.py:1639
  138.2 85.8 %shard_map.419 = (bf16[1024,128]{1,0:T(8,128)(2,1)}, bf16[1024,128]{1,0:T(8,128)(2,1)}, bf16[1024,128]{1,0:T(8,128)(2,1)}, f32[1024,128]{1,0:T(8,128)}, f32[1024...) custom-call(bf16[1024,2048]{1,0:T(8,128)(2,1)} %get-tuple-element.10, ...), custom_call_target="tpu_custom_call" | custom-call | tf_op jit(solution)/shard_map/pallas_call | solution.py:1639
  224.1 73.5 %shard_map.420 = (bf16[1024,512]{1,0:T(8,128)(2,1)}, bf16[1024,512]{1,0:T(8,128)(2,1)}, f32[8,512]{1,0:T(8,128)}, bf16[8,2,128,512]{3,2,1,0:T(8,128)(2,1)}, bf16...) custom-call(bf16[1024,2048]{1,0:T(8,128)(2,1)} %get-tuple-element.11, ...), custom_call_target="tpu_custom_call" | custom-call | tf_op jit(solution)/shard_map/pallas_call | solution.py:1639
  297.6 0.0 reduce-scatter.2.cloned.1.call-update
  297.6 84.8 %shard_map.421 = (f32[8,128]{1,0:T(8,128)}, bf16[8,2,128,384]{3,2,1,0:T(8,128)(2,1)}, bf16[128,2048]{1,0:T(8,128)(2,1)}, f32[128,2048]{1,0:T(8,128)}, f32[1,2048...) custom-call(bf16[1024,2048]{1,0:T(8,128)(2,1)} %get-tuple-element.12, ...), custom_call_target="tpu_custom_call" | custom-call | tf_op jit(solution)/shard_map/pallas_call | solution.py:1639
  382.5 0.0 reduce-scatter.2.cloned.1.call-done.refs_24_.refs_25_
  382.5 68.3 %shard_map.422 = (bf16[128,4096]{1,0:T(8,128)(2,1)}, bf16[4096,128]{1,0:T(8,128)(2,1)}, bf16[128,3072]{1,0:T(8,128)(2,1)}, bf16[1024,128]{1,0:T(8,128)(2,1)}, bf...) custom-call(s32[1,1024]{1,0:T(1,128)} %add.28.refs_5_.refs_9_.refs_2, ...), custom_call_target="tpu_custom_call" | custom-call | tf_op jit(solution)/shard_map/pallas_call | solution.py:1639
  450.7 6.9 %shard_map.423 = (f32[128,4096]{1,0:T(8,128)}, f32[4096,128]{1,0:T(8,128)}, f32[128,1024]{1,0:T(8,128)}, f32[128,1024]{1,0:T(8,128)}, f32[128,1024]{1,0:T(8,128)...) custom-call(bf16[128,4096]{1,0:T(8,128)(2,1)} %get-tuple-element.148, ...), custom_call_target="tpu_custom_call" | custom-call | tf_op jit(solution)/shard_map/pallas_call | solution.py:2088
Async XLA Ops:
  7.2 375.3 %reduce-scatter.2.cloned.1.call-start = ((), (), s32[]{:S(2)}) async-start(), calls=%async_computation.1 | async-start | bytes 4718592 | tf_op jit(solution)/shard_map/reduce_scatter | solution.py:2353
Sparse Core Ops, SparseCore 0:
  297.8 66.3 reduce-scatter.1
